TPU v7x, 512 devices: a whole 4x8x8 slice. The times are simulated.
512 devices in a mesh: section: 8 (over x, core), head: 8 (over z), dp: 8 (over y).
Axes of the slice: x: 4, y: 8, z: 8, core: 2. Of those that a mesh axis runs over, the one named last changes fastest.
Arguments:
- teacher_q: bfloat16 [8, 1024, 8192], P('section', 'dp', 'head'), may hold values from -150 to 150
- teacher_k: bfloat16 [8, 1024, 1024], P('section', 'dp', 'head'), may hold values from -150 to 150
- student_q: bfloat16 [8, 2, 1024, 4096], P('section', None, 'dp', 'head'), may hold values from -150 to 150
- student_k: bfloat16 [8, 2, 1024, 1024], P('section', None, 'dp', 'head'), may hold values from -150 to 150
- student_scale: float32 [8, 32], P(None, 'head'), may hold values from 0.5 to 2
- pairing: int32 [8], replicated, may hold values from 0 to 7, as said below
- placement: int32 [8], replicated, may hold values from 0 to 7, as said below
Outputs:
- student_q_grad: bfloat16 [8, 2, 1024, 4096], P('section', None, 'dp', 'head')
- student_k_grad: bfloat16 [8, 2, 1024, 1024], P('section', None, 'dp', 'head')
- layer_kl: float32 [8, 8], P('dp')
- scale_grad: float32 [8, 32], P(None, 'head')
Inputs may be any that keep to these rules, and one draw needn't show every extreme that they name: `pairing`: each teacher layer of the window is paired with exactly one student layer. `placement`: a section holds at most 2 student layers, in increasing order of layer index, and some section holds exactly 2.
All inputs are finite; a program needn't handle non-finite values.
Results may differ from a plain program's by a relative error of at most 0.0048.
Values may be sent and summed in bfloat16 or wider, within the bound.
No kernel may reach another device: no remote copies, remote signals or barrier semaphores. Data moves between devices by JAX's collectives and lax.ppermute only.
A program may use at most 64 MiB of HBM per device.

v0:
```python
import math

import jax
import jax.numpy as jnp
from jax import lax
from jax.sharding import PartitionSpec as P

STUDENT_HEADS = 32
HEAD_WIDTH = 128
REPLICA_TOKENS = 128


def in_one_piece(arrays, axis, split_dim, concat_dim, along):
    both = jnp.concatenate(arrays, axis=along)
    whole, at, finished = (
        lax.all_to_all(both, axis, split_axis=split_dim, concat_axis=concat_dim, tiled=True),
        0,
        [],
    )
    for a in arrays:
        finished.append(lax.slice_in_dim(whole, at, at + a.shape[along], axis=along))
        at += a.shape[along]
    return tuple(finished)


def copy_for_each(x, axis):
    size = lax.axis_size(axis)
    return lax.all_to_all(jnp.broadcast_to(x[None], (size, *x.shape)), axis, 0, 0, tiled=True)


def of_everyone(x, axis):
    return copy_for_each(x, axis).sum(axis=0)


def causal_mask(length):
    row_ids = lax.broadcasted_iota(jnp.int32, (length, length), 0)
    col_ids = lax.broadcasted_iota(jnp.int32, (length, length), 1)
    return col_ids <= row_ids


def head_terms(query_twins, teacher_key, query_head, student_key, scale_value, mask):
    width = teacher_key.shape[-1]
    inverse = 1.0 / math.sqrt(width)
    teacher_scores = (
        jnp.einsum("hid,jd->hij", query_twins, teacher_key, preferred_element_type=jnp.float32)
        * inverse
    )
    teacher_logp = jax.nn.log_softmax(jnp.where(mask, teacher_scores, -1e30), axis=-1)
    target_logp = jnp.logaddexp(teacher_logp[0], teacher_logp[1]) - math.log(2.0)
    raw_scores = jnp.dot(query_head, student_key.T, preferred_element_type=jnp.float32) * inverse
    student_logp = jax.nn.log_softmax(jnp.where(mask, scale_value * raw_scores, -1e30), axis=-1)
    target_prob = jnp.exp(target_logp)
    student_prob = jnp.exp(student_logp)
    divergence = jnp.sum(jnp.where(mask, target_prob * (target_logp - student_logp), 0.0))
    difference = jnp.where(mask, student_prob - target_prob, 0.0)
    scale_term = jnp.sum(difference * raw_scores)
    logit_grad = (difference * (scale_value * inverse)).astype(jnp.bfloat16)
    query_grad = jnp.dot(logit_grad, student_key, preferred_element_type=jnp.float32)
    key_grad = jnp.dot(logit_grad.T, query_head, preferred_element_type=jnp.float32)
    return (query_grad, key_grad, divergence, scale_term)


def group_terms(teacher_query, teacher_key, student_query, student_key, scales, mask):
    length = teacher_key.shape[0]
    width = teacher_key.shape[1]
    heads_here = scales.shape[0]
    teacher_heads = teacher_query.reshape(length, heads_here, 2, width).transpose(1, 2, 0, 3)
    student_heads = student_query.reshape(length, heads_here, width).transpose(1, 0, 2)

    def one_head(items):
        return head_terms(items[0], teacher_key, items[1], student_key, items[2], mask)

    query_grads, key_gradient_list, divergences, scale_terms = lax.map(
        one_head, (teacher_heads, student_heads, scales)
    )
    query_grads = query_grads.transpose(1, 0, 2).reshape(length, heads_here * width)
    return (query_grads, jnp.sum(key_gradient_list, 0), jnp.sum(divergences), scale_terms)


def local_terms(teacher_query, teacher_key, student_query, student_key, scales):
    length = teacher_key.shape[0]
    groups = teacher_key.shape[1] // HEAD_WIDTH
    mask = causal_mask(length)

    def split_groups(array):
        return array.reshape(length, groups, -1).transpose(1, 0, 2)

    def group_call(items):
        return group_terms(items[0], items[1], items[2], items[3], items[4], mask)

    query_grads, key_gradient_list, divergences, scale_terms = lax.map(
        group_call,
        (
            split_groups(teacher_query),
            split_groups(teacher_key),
            split_groups(student_query),
            split_groups(student_key),
            scales.reshape(groups, -1),
        ),
    )
    query_grads = query_grads.transpose(1, 0, 2).reshape(length, -1)
    key_gradient_list = key_gradient_list.transpose(1, 0, 2).reshape(length, -1)
    return (query_grads, key_gradient_list, jnp.sum(divergences), scale_terms.reshape(-1))


def local(teacher_q, teacher_k, student_q, student_k, student_scale, pairing, placement):
    sections = lax.axis_size("section")
    section_index = lax.axis_index("section")
    slot_count = student_q.shape[1]
    layer_count = pairing.shape[0]
    layer_ids = jnp.arange(layer_count, dtype=jnp.int32)
    held_here = placement == section_index
    rank_here = jnp.cumsum(held_here.astype(jnp.int32)) - 1
    slot_ids = jnp.arange(slot_count, dtype=jnp.int32)
    slot_table = held_here[None, :] & (rank_here[None, :] == slot_ids[:, None])
    table_float = slot_table.astype(jnp.float32)
    target_layer = jnp.sum(jnp.where(pairing == section_index, layer_ids, 0))
    source_section = jnp.sum(jnp.where(layer_ids == target_layer, placement, 0))
    section_ids = jnp.arange(sections, dtype=jnp.int32)
    pair_table = (pairing[None, :] == section_ids[:, None]).astype(jnp.float32)
    route = jnp.dot(pair_table, table_float.T, precision=lax.Precision.HIGHEST).astype(jnp.bfloat16)
    outgoing_query = jnp.einsum(
        "dj,jtc->dtc", route, student_q[0], preferred_element_type=jnp.float32
    ).astype(jnp.bfloat16)
    outgoing_key = jnp.einsum(
        "dj,jtc->dtc", route, student_k[0], preferred_element_type=jnp.float32
    ).astype(jnp.bfloat16)
    arrived_query, arrived_key = in_one_piece((outgoing_query, outgoing_key), "section", 0, 0, 2)
    query_layer = lax.dynamic_index_in_dim(arrived_query, source_section, 0, keepdims=False)
    key_layer = lax.dynamic_index_in_dim(arrived_key, source_section, 0, keepdims=False)
    scale_layer = lax.dynamic_index_in_dim(student_scale, target_layer, 0, keepdims=False)
    query_grad, key_grad, divergence, scale_term = local_terms(
        teacher_q[0], teacher_k[0], query_layer, key_layer, scale_layer
    )
    at_source = (section_ids == source_section)[:, None, None]
    zero_value = jnp.zeros((), jnp.bfloat16)
    back_query = jnp.where(at_source, query_grad.astype(jnp.bfloat16)[None], zero_value)
    back_key = jnp.where(at_source, key_grad.astype(jnp.bfloat16)[None], zero_value)
    returned_query, returned_key = in_one_piece((back_query, back_key), "section", 0, 0, 2)
    query_grad_out = jnp.einsum(
        "dj,dtc->jtc", route, returned_query, preferred_element_type=jnp.float32
    ).astype(jnp.bfloat16)[None]
    key_grad_out = jnp.einsum(
        "dj,dtc->jtc", route, returned_key, preferred_element_type=jnp.float32
    ).astype(jnp.bfloat16)[None]
    is_target = layer_ids == target_layer
    layer_divergence = jnp.where(is_target, divergence, 0.0)
    layer_scale_terms = jnp.where(is_target[:, None], scale_term[None, :], 0.0)
    summed_divergence = of_everyone(layer_divergence, ("section", "head"))
    layer_kl_out = (summed_divergence / (STUDENT_HEADS * REPLICA_TOKENS))[None, :]
    scale_grad_out = of_everyone(layer_scale_terms, ("section", "dp"))
    return (query_grad_out, key_grad_out, layer_kl_out, scale_grad_out)


def solution(mesh):
    return jax.shard_map(
        local,
        mesh=mesh,
        in_specs=(
            P("section", "dp", "head"),
            P("section", "dp", "head"),
            P("section", None, "dp", "head"),
            P("section", None, "dp", "head"),
            P(None, "head"),
            P(),
            P(),
        ),
        out_specs=(
            P("section", None, "dp", "head"),
            P("section", None, "dp", "head"),
            P("dp", None),
            P(None, "head"),
        ),
        check_vma=False,
    )
```

profile of v0, /device:TPU:1, one launch (start us, length us, event | category | flops | bytes accessed | tf_op | source)
XLA Modules:
  0.0 116.4 jit_solution(15866077523002025469)
XLA Ops:
  0.7 0.7 convert_bitcast_fusion
  1.6 0.8 fusion.22
  2.3 0.5 convolution_convert_fusion
  2.8 0.3 convolution_convert_fusion.2
  3.2 1.2 %copy.53 = bf16[8,128,640]{2,1,0:T(8,128)(2,1)} copy(bf16[8,128,640]{2,0,1:T(8,128)(2,1)S(1)} %pad_maximum_fusion) | data formatting | bytes 2621440 | tf_op jit(solution)/shard_map/concatenate | solution.py:14
  4.5 10.5 %all-to-all-start = ((bf16[8,128,640]{2,1,0:T(8,128)(2,1)}), bf16[8,128,640]{2,1,0:T(8,128)(2,1)S(1)}, u32[]{:S(2)}, u32[]{:S(2)}) async-start(bf16[8,128,640]{2,1,0:T(8,128)(2,1)} %copy.53), calls=%async_computation | async-start | bytes 2621440 | tf_op jit(solution)/shard_map/all_to_all | solution.py:16
  15.0 0.6 fusion.30
  16.3 1.3 %select_reduce_fusion = s32[]{:T(128)} fusion(s32[8]{0:T(128)S(1)} %copy-done.5, s32[]{:T(128)} %fusion.30), kind=kLoop, calls=%fused_computation.62 | loop fusion | flops 23 | bytes 40 | tf_op jit(solution)/shard_map/reduce_sum | solution.py:118
  21.2 0.7 iota_compare_fusion.4
  21.9 0.7 iota_compare_fusion.3
  22.5 10.4 %all-to-all-done = bf16[8,128,640]{2,1,0:T(8,128)(2,1)S(1)} async-done(((bf16[8,128,640]{2,1,0:T(8,128)(2,1)}), bf16[8,128,640]{2,1,0:T(8,128)(2,1)S(1)}, u32[]{:S(2)}, u32[]{:S(2)}) %all-to-all-start) | async-done | bytes 1310752 | tf_op jit(solution)/shard_map/all_to_all | solution.py:16
  33.2 17.9 %while.33 = (s32[]{:T(128)}, bf16[4,128,128]{1,2,0:T(8,128)(2,1)S(1)}, f32[4,128,128]{2,1,0:T(8,128)S(1)}, f32[4]{0:T(128)S(1)}, f32[4]{0:T(128)S(1)}, /*index=5...) while((s32[]{:T(128)}, ...), condition=%wide.region_10.11_spmd.clone.clone, body=%wide.region_3.10_spmd.clone.clone.sunk | while | flops 21773568 | bytes 1353413 | solution.py:73
  33.5 0.6 dynamic_slice.82
  35.0 0.8 multiply_reduce_fusion.2
  35.9 0.2 fusion.57
  36.2 0.8 dynamic_update_slice.54
  37.0 0.8 dynamic_update_slice.55
  38.0 0.6 dynamic_slice.82
  39.5 0.8 multiply_reduce_fusion.2
  40.4 0.2 fusion.57
  40.6 0.8 dynamic_update_slice.54
  41.4 0.8 dynamic_update_slice.55
  42.5 0.6 dynamic_slice.82
  43.9 0.8 multiply_reduce_fusion.2
  44.8 0.2 fusion.57
  45.1 0.8 dynamic_update_slice.54
  45.9 0.8 dynamic_update_slice.55
  46.9 0.6 dynamic_slice.82
  48.4 0.8 multiply_reduce_fusion.2
  49.6 0.8 dynamic_update_slice.54
  50.4 0.8 dynamic_update_slice.55
  51.5 0.6 reduce_sum.113
  52.1 1.3 %broadcast_select_fusion.3 = f32[8]{0:T(128)S(1)} fusion(f32[]{:T(128)} %reduce_sum.113, s32[]{:T(128)} %fusion.30), kind=kLoop, calls=%fused_computation.67 | loop fusion | flops 16 | bytes 40 | tf_op jit(solution)/shard_map/jit(_where)/select_n | solution.py:147
  53.4 0.6 broadcast_in_dim.188
  54.1 7.8 %all-to-all-start.2 = ((f32[64,1,8]{2,1,0:T(1,128)}), f32[64,1,8]{2,1,0:T(1,128)S(1)}, u32[]{:S(2)}, u32[]{:S(2)}) async-start(f32[64,1,8]{2,1,0:T(1,128)} %broadcast_in_dim.188), calls=%async_computation.2 | async-start | bytes 65536 | tf_op jit(solution)/shard_map/all_to_all | solution.py:28
  61.9 9.1 %all-to-all-done.2 = f32[64,1,8]{2,1,0:T(1,128)S(1)} async-done(((f32[64,1,8]{2,1,0:T(1,128)}), f32[64,1,8]{2,1,0:T(1,128)S(1)}, u32[]{:S(2)}, u32[]{:S(2)}) %all-to-all-start.2) | async-done | bytes 2080 | tf_op jit(solution)/shard_map/all_to_all | solution.py:28
  71.0 0.7 broadcast_in_dim.192
  71.6 9.3 %all-to-all-start.3 = ((f32[64,8,4]{1,2,0:T(4,128)}), f32[64,8,4]{1,2,0:T(4,128)S(1)}, u32[]{:S(2)}, u32[]{:S(2)}) async-start(f32[64,8,4]{1,2,0:T(4,128)} %broadcast_in_dim.192), calls=%async_computation.3 | async-start | bytes 262144 | tf_op jit(solution)/shard_map/all_to_all | solution.py:28
  81.0 1.2 %pad_maximum_fusion.1 = bf16[8,128,640]{2,1,0:T(8,128)(2,1)} fusion(bf16[8,128,128]{2,1,0:T(8,128)(2,1)S(1)} %broadcast_select_fusion.1, bf16[8,128,512]{2,1,0:T(8,128)(2,1)S(1)} %broadcast_select_fusion), kind=kLoop, calls=%fused_computation.35 | loop fusion | flops 2621440 | bytes 2621440 | tf_op jit(solution)/shard_map/concatenate | solution.py:14
  82.2 8.8 %all-to-all-done.3 = f32[64,8,4]{1,2,0:T(4,128)S(1)} async-done(((f32[64,8,4]{1,2,0:T(4,128)}), f32[64,8,4]{1,2,0:T(4,128)S(1)}, u32[]{:S(2)}, u32[]{:S(2)}) %all-to-all-start.3) | async-done | bytes 8224 | tf_op jit(solution)/shard_map/all_to_all | solution.py:28
  90.9 5.0 %all-to-all-start.1 = ((bf16[8,128,640]{2,1,0:T(8,128)(2,1)}), bf16[8,128,640]{2,1,0:T(8,128)(2,1)S(1)}, u32[]{:S(2)}, u32[]{:S(2)}) async-start(bf16[8,128,640]{2,1,0:T(8,128)(2,1)} %pad_maximum_fusion.1), calls=%async_computation.1 | async-start | bytes 2621440 | tf_op jit(solution)/shard_map/all_to_all | solution.py:16
  96.0 0.5 multiply_bitcast_fusion
  96.5 0.7 reduce_sum.115
  97.2 16.7 %all-to-all-done.1 = bf16[8,128,640]{2,1,0:T(8,128)(2,1)S(1)} async-done(((bf16[8,128,640]{2,1,0:T(8,128)(2,1)}), bf16[8,128,640]{2,1,0:T(8,128)(2,1)S(1)}, u32[]{:S(2)}, u32[]{:S(2)}) %all-to-all-start.1) | async-done | bytes 1310752 | tf_op jit(solution)/shard_map/all_to_all | solution.py:16
  114.0 0.7 fusion.20
  114.7 0.7 copy.63
  115.5 0.3 fusion.21
  115.8 0.6 copy.64
  (69 shorter events, 4.3 us)
Async XLA Ops:
  0.6 1.7 %copy-start = (bf16[1,2,128,512]{3,2,1,0:T(8,128)(2,1)S(1)}, bf16[1,2,128,512]{3,2,1,0:T(8,128)(2,1)}, u32[]{:S(2)}) copy-start(bf16[1,2,128,512]{3,2,1,0:T(8,128)(2,1)} %param.11) | copy-start | bytes 786436
  0.6 2.2 %copy-start.3 = (bf16[1,2,128,128]{3,2,1,0:T(8,128)(2,1)S(1)}, bf16[1,2,128,128]{3,2,1,0:T(8,128)(2,1)}, u32[]{:S(2)}) copy-start(bf16[1,2,128,128]{3,2,1,0:T(8,128)(2,1)} %param.12) | copy-start | bytes 196612
  4.5 10.5 %copy-start.6 = (s32[8]{0:T(128)S(1)}, s32[8]{0:T(128)}, u32[]{:S(2)}) copy-start(s32[8]{0:T(128)} %param.14) | copy-start | bytes 100
  4.5 11.8 %copy-start.5 = (s32[8]{0:T(128)S(1)}, s32[8]{0:T(128)}, u32[]{:S(2)}) copy-start(s32[8]{0:T(128)} %param.15) | copy-start | bytes 100
  4.5 15.1 %copy-start.2 = (bf16[1,128,1024]{2,1,0:T(8,128)(2,1)S(1)}, bf16[1,128,1024]{2,1,0:T(8,128)(2,1)}, u32[]{:S(2)}) copy-start(bf16[1,128,1024]{2,1,0:T(8,128)(2,1)} %param.9) | copy-start | bytes 786436
  4.5 16.5 %copy-start.4 = (f32[8,4]{0,1:T(4,128)S(1)}, f32[8,4]{0,1:T(4,128)}, u32[]{:S(2)}) copy-start(f32[8,4]{0,1:T(4,128)} %param.13) | copy-start | bytes 388
  4.5 28.4 %all-to-all-start = ((bf16[8,128,640]{2,1,0:T(8,128)(2,1)}), bf16[8,128,640]{2,1,0:T(8,128)(2,1)S(1)}, u32[]{:S(2)}, u32[]{:S(2)}) async-start(bf16[8,128,640]{2,1,0:T(8,128)(2,1)} %copy.53), calls=%async_computation | async-start | bytes 2621440 | tf_op jit(solution)/shard_map/all_to_all | solution.py:16
  22.5 10.7 %copy-start.1 = (bf16[1,128,128]{2,1,0:T(8,128)(2,1)S(1)}, bf16[1,128,128]{2,1,0:T(8,128)(2,1)}, u32[]{:S(2)}) copy-start(bf16[1,128,128]{2,1,0:T(8,128)(2,1)} %param.10) | copy-start | bytes 98308
  54.1 16.9 %all-to-all-start.2 = ((f32[64,1,8]{2,1,0:T(1,128)}), f32[64,1,8]{2,1,0:T(1,128)S(1)}, u32[]{:S(2)}, u32[]{:S(2)}) async-start(f32[64,1,8]{2,1,0:T(1,128)} %broadcast_in_dim.188), calls=%async_computation.2 | async-start | bytes 65536 | tf_op jit(solution)/shard_map/all_to_all | solution.py:28
  71.6 19.3 %all-to-all-start.3 = ((f32[64,8,4]{1,2,0:T(4,128)}), f32[64,8,4]{1,2,0:T(4,128)S(1)}, u32[]{:S(2)}, u32[]{:S(2)}) async-start(f32[64,8,4]{1,2,0:T(4,128)} %broadcast_in_dim.192), calls=%async_computation.3 | async-start | bytes 262144 | tf_op jit(solution)/shard_map/all_to_all | solution.py:28
  90.9 22.9 %all-to-all-start.1 = ((bf16[8,128,640]{2,1,0:T(8,128)(2,1)}), bf16[8,128,640]{2,1,0:T(8,128)(2,1)S(1)}, u32[]{:S(2)}, u32[]{:S(2)}) async-start(bf16[8,128,640]{2,1,0:T(8,128)(2,1)} %pad_maximum_fusion.1), calls=%async_computation.1 | async-start | bytes 2621440 | tf_op jit(solution)/shard_map/all_to_all | solution.py:16
where the time goes:
time: 117 us; the launch traced here: 116 us
  waiting for transfers between devices  44.8 us (38%)
  starting transfers between devices  32.6 us (28%)
  local copies, waits for them, and re-layouts  13.5 us (12%)
  other arithmetic  12.5 us (11%)
  matrix products  5.43 us (5%)
  between operations  4.8 us (4%)
  loops' own time  2.72 us (2%)
    all_to_all x2, waiting for transfers between devices, in_one_piece(): lax.all_to_all(both, axis, split_axis=split_dim, concat_axis=concat_dim,...  27 us
    all_to_all x2, waiting for transfers between devices, copy_for_each(): lax.all_to_all(jnp.broadcast_to(x[None], (size, *x.shape)), axis, 0, 0, t...  17.8 us
    all_to_all x2, starting transfers between devices, copy_for_each(): lax.all_to_all(jnp.broadcast_to(x[None], (size, *x.shape)), axis, 0, 0, t...  17.1 us
    all_to_all x2, starting transfers between devices, in_one_piece(): lax.all_to_all(both, axis, split_axis=split_dim, concat_axis=concat_dim,...  15.5 us
    dynamic_update_slice x8, local copies, waits for them, and re-layouts, group_terms(): lax.map(one_head, (teacher_heads, student_heads, scales))  6.27 us
    reduce_sum x4, other arithmetic, head_terms(): scale_term = jnp.sum(difference * raw_scores)  3.14 us
    another operation x1, loops' own time, group_terms(): lax.map(one_head, (teacher_heads, student_heads, scales))  2.72 us
    dynamic_slice x4, local copies, waits for them, and re-layouts, group_terms(): lax.map(one_head, (teacher_heads, student_heads, scales))  2.36 us
  transfers between devices with their start and end apart: 4, of which 4 were waited for; matrix products, arithmetic and copies ran while one was open for 5% of the time, Pallas kernels for 0%

commit v1 on v0

v1 whole, which is shorter than its diff:
```python
import functools
import math

import jax
import jax.numpy as jnp
from jax import lax
from jax.experimental import pallas as pl
from jax.experimental.pallas import tpu as pltpu
from jax.sharding import PartitionSpec as P

STUDENT_HEADS = 32
HEAD_WIDTH = 128
TOKENS = 128
LAYERS = 8
SLOTS = 2
HEADS = 4
PACKED = 2 * TOKENS + 8
SCALE_LANE = 32
INVERSE = 1.0 / math.sqrt(HEAD_WIDTH)
HIDDEN = -1e30
AXES = ("section", "head", "dp")


def dot(a, b, over_a, over_b):
    return lax.dot_general(
        a, b, (((over_a,), (over_b,)), ((), ())), preferred_element_type=jnp.float32
    )


def masks():
    row = lax.broadcasted_iota(jnp.int32, (TOKENS, TOKENS), 0)
    col = lax.broadcasted_iota(jnp.int32, (TOKENS, TOKENS), 1)
    return row, col


def log_softmax(scores, visible, axis):
    scores = jnp.where(visible, scores, HIDDEN)
    shifted = scores - jnp.max(scores, axis=axis, keepdims=True)
    return shifted - jnp.log(jnp.sum(jnp.exp(shifted), axis=axis, keepdims=True))


def teacher_kernel(pairing, placement, q_ref, k_ref, out_ref):
    me = lax.axis_index("section")
    home = jnp.int32(0)
    for layer in range(LAYERS):
        home = jnp.where(pairing[layer] == me, placement[layer], home)
    chip = home // 2
    row, col = masks()
    key = k_ref[0]

    def target(head, turned):
        logps = []
        for twin in (2 * head, 2 * head + 1):
            query = q_ref[0, :, twin * HEAD_WIDTH : (twin + 1) * HEAD_WIDTH]
            if turned:
                scores = dot(key, query, 1, 1) * INVERSE
                logps.append(log_softmax(scores, row <= col, 0))
            else:
                scores = dot(query, key, 1, 1) * INVERSE
                logps.append(log_softmax(scores, col <= row, 1))
        one, two = logps
        high = jnp.maximum(one, two)
        return high + jnp.log1p(jnp.exp(-jnp.abs(one - two))) - math.log(2.0)

    for pair in range(HEADS // 2):
        plain = target(2 * pair, False)
        turned = target(2 * pair + 1, True)
        out_ref[chip, pair * TOKENS : (pair + 1) * TOKENS, :] = jnp.where(
            col <= row, plain, turned
        )
        diagonal = jnp.sum(jnp.where(row == col, turned, 0.0), axis=0, keepdims=True)
        at = 2 * TOKENS + pair
        out_ref[chip, at : at + 1, :] = diagonal


def student_kernel(
    pairing, placement, scale_ref, packed_ref, q_ref, k_ref, sums_ref, grad_ref
):
    me = lax.axis_index("section")
    my_chip, my_core = me // 2, lax.rem(me, 2)
    row, col = masks()
    lane = lax.broadcasted_iota(jnp.int32, (1, TOKENS), 1)
    sums_ref[...] = jnp.zeros_like(sums_ref)

    def layer_step(layer, counts):
        home = placement[layer]
        chip, core = home // 2, lax.rem(home, 2)
        here = chip == my_chip
        slot = jnp.where(core == 0, counts[0], counts[1])

        @pl.when(here)
        def _():
            source = pairing[layer]
            source_chip, source_core = source // 2, lax.rem(source, 2)
            key = k_ref[core, slot]
            divergence = jnp.zeros((TOKENS, TOKENS), jnp.float32)
            found = jnp.zeros((1, TOKENS), jnp.float32)
            grads = []
            for head in range(HEADS):
                pair, turned = head // 2, head % 2 == 1
                query = q_ref[core, slot, :, head * HEAD_WIDTH : (head + 1) * HEAD_WIDTH]
                square = packed_ref[
                    source_core, source_chip, pair * TOKENS : (pair + 1) * TOKENS, :
                ]
                scale = scale_ref[layer, head]
                if turned:
                    at = 2 * TOKENS + pair
                    diagonal = packed_ref[source_core, source_chip, at : at + 1, :]
                    visible, axis = row <= col, 0
                    target_logp = jnp.where(
                        row < col, square, jnp.where(row == col, diagonal, HIDDEN)
                    )
                    raw = dot(key, query, 1, 1) * INVERSE
                else:
                    visible, axis = col <= row, 1
                    target_logp = jnp.where(visible, square, HIDDEN)
                    raw = dot(query, key, 1, 1) * INVERSE
                student_logp = log_softmax(scale * raw, visible, axis)
                target = jnp.exp(target_logp)
                divergence += jnp.where(
                    visible, target * (target_logp - student_logp), 0.0
                )
                difference = jnp.where(visible, jnp.exp(student_logp) - target, 0.0)
                found = jnp.where(
                    lane == SCALE_LANE + HEADS * layer + head,
                    jnp.sum(difference * raw),
                    found,
                )
                grads.append((difference * (scale * INVERSE)).astype(jnp.bfloat16))
            found = jnp.where(lane == layer, jnp.sum(divergence), found)
            sums_ref[...] += jnp.broadcast_to(found, sums_ref.shape)

            @pl.when(core == my_core)
            def _():
                for head in range(HEADS):
                    grad_ref[slot, head] = grads[head]

        one = jnp.int32(1)
        return (
            counts[0] + jnp.where(here & (core == 0), one, 0),
            counts[1] + jnp.where(here & (core == 1), one, 0),
        )

    lax.fori_loop(0, LAYERS, layer_step, (jnp.int32(0), jnp.int32(0)))


def gradient_kernel(placement, grad_ref, q_ref, k_ref, q_out, k_out):
    me = lax.axis_index("section")
    held = jnp.int32(0)
    for layer in range(LAYERS):
        held += (placement[layer] == me).astype(jnp.int32)
    for slot in range(SLOTS):

        @pl.when(slot < held)
        def _():
            key = k_ref[0, slot]
            total = jnp.zeros((TOKENS, HEAD_WIDTH), jnp.float32)
            for head in range(HEADS):
                lanes = slice(head * HEAD_WIDTH, (head + 1) * HEAD_WIDTH)
                query = q_ref[0, slot, :, lanes]
                grad = grad_ref[slot, head]
                over = head % 2
                q_out[0, slot, :, lanes] = dot(grad, key, 1 - over, 0).astype(jnp.bfloat16)
                total += dot(grad, query, over, 0)
            k_out[0, slot] = total.astype(jnp.bfloat16)

        @pl.when(slot >= held)
        def _():
            q_out[0, slot] = jnp.zeros(q_out.shape[2:], jnp.bfloat16)
            k_out[0, slot] = jnp.zeros(k_out.shape[2:], jnp.bfloat16)


def final_kernel(rows_ref, kl_ref, scale_ref):
    divergence = jnp.sum(rows_ref[0], axis=0, keepdims=True)
    kl_ref[...] = divergence[:, :LAYERS] / (STUDENT_HEADS * TOKENS)
    terms = jnp.sum(rows_ref[1], axis=0, keepdims=True)
    terms = jnp.broadcast_to(terms, (LAYERS, TOKENS))
    lane = lax.broadcasted_iota(jnp.int32, (LAYERS, TOKENS), 1)
    layer = lax.broadcasted_iota(jnp.int32, (LAYERS, TOKENS), 0)
    at = lane - SCALE_LANE - HEADS * layer
    for head in range(HEADS):
        scale_ref[:, head : head + 1] = jnp.sum(
            jnp.where(at == head, terms, 0.0), axis=1, keepdims=True
        )


VMEM = pl.BlockSpec(memory_space=pltpu.VMEM)
SMEM = pl.BlockSpec(memory_space=pltpu.SMEM)


def cost(flops, moved):
    return pl.CostEstimate(flops=flops, bytes_accessed=moved, transcendentals=0)


def local(chips, groups, teacher_q, teacher_k, student_q, student_k, student_scale, pairing, placement):
    f32, bf16 = jnp.float32, jnp.bfloat16
    over_x = [[2 * x + core for x in range(chips)] for core in range(2)]
    of_chip = [[2 * x, 2 * x + 1] for x in range(chips)]
    members = len(groups[0])

    packed = pl.pallas_call(
        teacher_kernel,
        out_shape=jax.ShapeDtypeStruct((chips, PACKED, TOKENS), f32),
        in_specs=[SMEM, SMEM, VMEM, VMEM],
        out_specs=VMEM,
        cost_estimate=cost(8 * 2 * TOKENS**3, 400_000),
        name="teacher",
    )(pairing, placement, teacher_q, teacher_k)
    arrived = lax.all_to_all(
        packed, "section", 0, 0, tiled=True, axis_index_groups=over_x
    )
    chip_q = lax.all_gather(student_q[0], "section", axis_index_groups=of_chip)
    chip_k = lax.all_gather(student_k[0], "section", axis_index_groups=of_chip)
    chip_packed = lax.all_gather(arrived, "section", axis_index_groups=of_chip)

    sums, grads = pl.pallas_call(
        student_kernel,
        out_shape=(
            jax.ShapeDtypeStruct((members, TOKENS), f32),
            jax.ShapeDtypeStruct((SLOTS, HEADS, TOKENS, TOKENS), bf16),
        ),
        in_specs=[SMEM, SMEM, SMEM, VMEM, VMEM, VMEM],
        out_specs=(VMEM, VMEM),
        cost_estimate=cost(8 * 2 * TOKENS**3, 1_800_000),
        name="student",
    )(pairing, placement, student_scale, chip_packed, chip_q, chip_k)

    rows = lax.all_to_all(
        sums.reshape(members, 1, TOKENS), AXES, 0, 0, tiled=True, axis_index_groups=groups
    )
    q_grad, k_grad = pl.pallas_call(
        gradient_kernel,
        out_shape=(
            jax.ShapeDtypeStruct(student_q.shape, bf16),
            jax.ShapeDtypeStruct(student_k.shape, bf16),
        ),
        in_specs=[SMEM, VMEM, VMEM, VMEM],
        out_specs=(VMEM, VMEM),
        cost_estimate=cost(16 * 2 * TOKENS**3, 900_000),
        name="gradient",
    )(placement, grads, student_q, student_k)

    both = lax.all_gather(
        rows.reshape(members, TOKENS), "section", axis_index_groups=of_chip
    )
    layer_kl, scale_grad = pl.pallas_call(
        final_kernel,
        out_shape=(
            jax.ShapeDtypeStruct((1, LAYERS), f32),
            jax.ShapeDtypeStruct((LAYERS, HEADS), f32),
        ),
        in_specs=[VMEM],
        out_specs=(VMEM, VMEM),
        name="final",
    )(both)
    return (q_grad, k_grad, layer_kl, scale_grad)


def reduction_groups(sections, heads, replicas):
    def flat(section, head, replica):
        return (section * heads + head) * replicas + replica

    chips = range(sections // 2)
    first = [
        [flat(2 * x, h, d) for x in chips for h in range(heads)] for d in range(replicas)
    ]
    second = [
        [flat(2 * x + 1, h, d) for x in chips for d in range(replicas)] for h in range(heads)
    ]
    return first + second


def solution(mesh):
    sections, heads, replicas = (mesh.shape[a] for a in AXES)
    return jax.shard_map(
        functools.partial(local, sections // 2, reduction_groups(sections, heads, replicas)),
        mesh=mesh,
        in_specs=(
            P("section", "dp", "head"),
            P("section", "dp", "head"),
            P("section", None, "dp", "head"),
            P("section", None, "dp", "head"),
            P(None, "head"),
            P(),
            P(),
        ),
        out_specs=(
            P("section", None, "dp", "head"),
            P("section", None, "dp", "head"),
            P("dp", None),
            P(None, "head"),
        ),
        check_vma=False,
    )
```

time: 117 us -> 80.5 us (0.69)
  blocking collectives: 0 us -> 27.2 us
  waiting for transfers between devices: 44.8 us -> 19.5 us
  starting transfers between devices: 32.6 us -> 8.87 us
  other arithmetic: 12.5 us -> 0 us
  local copies, waits for them, and re-layouts: 13.5 us -> 2.01 us
  between operations: 4.8 us -> 14.1 us
  Pallas kernels: 0 us -> 8.47 us
  matrix products: 5.43 us -> 0 us
  loops' own time: 2.72 us -> 0 us
    all_to_all x4 -> x1, waiting for transfers between devices: 44.8 us -> 6.82 us  [local(): lax.all_to_all(sums.reshape(members, 1, TOKENS), AXES, 0, 0, tiled=True,...]
    all_to_all x4 -> x1, starting transfers between devices: 32.6 us -> 8.83 us  [local(): lax.all_to_all(sums.reshape(members, 1, TOKENS), AXES, 0, 0, tiled=True,...]
    all_gather x0 -> x3, blocking collectives: none -> 15.1 us  [the longest x1 8.95 us: local(): chip_k = lax.all_gather(student_k[0], 'section', axis_index_groups=of_chip)]
    all_gather x0 -> x1, waiting for transfers between devices: none -> 12.7 us  [local(): chip_packed = lax.all_gather(arrived, 'section', axis_index_groups=of_chip)]
    all_to_all x0 -> x1, blocking collectives: none -> 12.1 us  [local(): lax.all_to_all(packed, 'section', 0, 0, tiled=True, axis_index_groups=ove...]
    pallas_call x0 -> x4, Pallas kernels: none -> 8.47 us  [the longest x1 2.88 us: local(): pl.pallas_call(student_kernel, out_shape=(jax.ShapeDtypeStruct((members,...]
    reduce_sum x18 -> x0, other arithmetic: 6.77 us -> none  [the longest x4 3.14 us: head_terms(): scale_term = jnp.sum(difference * raw_scores)]
    dynamic_update_slice x8 -> x0, local copies, waits for them, and re-layouts: 6.27 us -> none  [group_terms(): lax.map(one_head, (teacher_heads, student_heads, scales))]
  transfers between devices with their start and end apart: 4 -> 2, of which waited for: 4 -> 2; matrix products, arithmetic and copies ran while one was open for 5% -> 1% of each run, Pallas kernels for 0% -> 2%
where the time goes in v1:
time: 80.5 us; the launch traced here: 80.1 us
  blocking collectives  27.2 us (34%)
  waiting for transfers between devices  19.5 us (24%)
  between operations  14.1 us (18%)
  starting transfers between devices  8.87 us (11%)
  Pallas kernels  8.47 us (11%)
  local copies, waits for them, and re-layouts  2.01 us (2%)
    all_gather x1, waiting for transfers between devices, local(): chip_packed = lax.all_gather(arrived, 'section', axis_index_groups=of_chip)  12.7 us
    all_to_all x1, blocking collectives, local(): lax.all_to_all(packed, 'section', 0, 0, tiled=True, axis_index_groups=ove...  12.1 us
    all_gather x1, blocking collectives, local(): chip_k = lax.all_gather(student_k[0], 'section', axis_index_groups=of_chip)  8.95 us
    all_to_all x1, starting transfers between devices, local(): lax.all_to_all(sums.reshape(members, 1, TOKENS), AXES, 0, 0, tiled=True,...  8.83 us
    all_to_all x1, waiting for transfers between devices, local(): lax.all_to_all(sums.reshape(members, 1, TOKENS), AXES, 0, 0, tiled=True,...  6.82 us
    all_gather x1, blocking collectives, local(): lax.all_gather(rows.reshape(members, TOKENS), 'section', axis_index_group...  3.87 us
    pallas_call x1, Pallas kernels, local(): pl.pallas_call(student_kernel, out_shape=(jax.ShapeDtypeStruct((members,...  2.88 us
    pallas_call x1, Pallas kernels, local(): pl.pallas_call(teacher_kernel, out_shape=jax.ShapeDtypeStruct((chips, PAC...  2.34 us
  transfers between devices with their start and end apart: 2, of which 2 were waited for; matrix products, arithmetic and copies ran while one was open for 1% of the time, Pallas kernels for 2%

profile of v1, /device:TPU:1, one launch (start us, length us, event | category | flops | bytes accessed | tf_op | source)
XLA Modules:
  0.0 80.1 jit_solution(8329888910320328372)
XLA Ops:
  7.2 0.0 copy-start.2
  7.2 0.0 copy-start.1
  7.2 0.0 all-gather.4.cloned.1.call-start
  7.2 2.3 %teacher.1 = f32[4,264,128]{2,1,0:T(8,128)} custom-call(s32[8]{0:T(128)} %pairing.3, s32[8]{0:T(128)} %placement.5, bf16[1,128,1024]{2,1,0:T(8,128)(2,1)} %q_ref.2, bf16[1,128,128]{2,1,0:T(8,128)(2,1)} %k_ref.2), custom_call_target="tpu_custom_call" | custom-call | flops 33554432 | bytes 400000 | tf_op jit(solution)/shard_map/teacher/pallas_call | solution.py:201
  9.6 0.0 copy-start
  9.6 12.1 %all_to_all.10 = f32[4,264,128]{2,1,0:T(8,128)} all-to-all(f32[4,264,128]{2,1,0:T(8,128)} %teacher.1), channel_id=1, replica_groups={{0,128,256,384},{64,192,320,448},{1,129,257,385},{65,193,321,449},{2,13..., dimensions={0} | all-to-all | bytes 1081344 | tf_op jit(solution)/shard_map/all_to_all | solution.py:209
  21.7 0.0 all-gather.4.cloned.1.call-update
  21.7 0.0 copy-done.2
  21.7 0.7 copy.16.scale_ref
  22.4 0.0 copy-done.1
  22.4 8.9 %all_gather.18.k_ref = bf16[2,2,128,128]{3,2,1,0:T(8,128)(2,1)} all-gather(bf16[1,2,128,128]{3,2,1,0:T(8,128)(2,1)S(1)} %copy-done.1), channel_id=1, replica_groups={{0,64},{128,192},{256,320},{384,448},{1,65},{129,193},{257,321},{385,44..., dimensions={0}, use_global_device_ids=true | all-gather | bytes 196608 | tf_op jit(solution)/shard_map/all_gather | solution.py:213
  31.3 0.0 copy-done
  31.3 2.3 %all_gather.17.q_ref = bf16[2,2,128,512]{3,2,1,0:T(8,128)(2,1)} all-gather(bf16[1,2,128,512]{3,2,1,0:T(8,128)(2,1)S(1)} %copy-done), channel_id=1, replica_groups={{0,64},{128,192},{256,320},{384,448},{1,65},{129,193},{257,321},{385,44..., dimensions={0}, use_global_device_ids=true | all-gather | bytes 786432 | tf_op jit(solution)/shard_map/all_gather | solution.py:212
  33.6 12.7 %all-gather.4.cloned.1.call-done = f32[8,264,128]{2,1,0:T(8,128)} async-done(((f32[4,264,128]{2,1,0:T(8,128)}), f32[8,264,128]{2,1,0:T(8,128)}) %all-gather.4.cloned.1.call-update) | async-done | bytes 1081360 | tf_op jit(solution)/shard_map/all_gather | solution.py:214
  46.3 2.9 %student.1 = (f32[32,128]{1,0:T(8,128)}, bf16[2,4,128,128]{3,2,1,0:T(8,128)(2,1)}) custom-call(s32[8]{0:T(128)} %pairing.3, s32[8]{0:T(128)} %placement.5, f32[8,4]{1,0:T(8,128)} %copy.16.scale_ref, f32[2,4,264,128]{3,2,1,0:T(8,128)} %bitcast.5, bf16[2,2,128,512]{3,2,1,0:T(8,128)(2,1)} %all_gather.17.q_ref, bf16[2,2,128,128]{3,2,1,0:T(8,128)(2,1)} %all_gather.18.k_ref), custom_call_target="tpu_custom_call" | custom-call | flops 33554432 | bytes 1800000 | tf_op jit(solution)/shard_map/student/pallas_call | solution.py:216
  49.2 8.8 %all-to-all-start.1 = ((f32[32,1,128]{2,1,0:T(1,128)}), f32[32,1,128]{2,1,0:T(1,128)S(1)}, u32[]{:S(2)}, u32[]{:S(2)}) async-start(f32[32,1,128]{2,1,0:T(1,128)} %bitcast.7), calls=%async_computation.1 | async-start | bytes 32768 | tf_op jit(solution)/shard_map/all_to_all | solution.py:228
  58.0 1.8 %gradient.1 = (bf16[1,2,128,512]{3,2,1,0:T(8,128)(2,1)}, bf16[1,2,128,128]{3,2,1,0:T(8,128)(2,1)}) custom-call(s32[8]{0:T(128)} %placement.5, bf16[2,4,128,128]{3,2,1,0:T(8,128)(2,1)} %get-tuple-element.10.grad_ref, bf16[1,2,128,512]{3,2,1,0:T(8,128)(2,1)} %q_ref.3, bf16[1,2,128,128]{3,2,1,0:T(8,128)(2,1)} %k_ref.3), custom_call_target="tpu_custom_call" | custom-call | flops 67108864 | bytes 900000 | tf_op jit(solution)/shard_map/gradient/pallas_call | solution.py:231
  59.9 6.8 %all-to-all-done.1 = f32[32,1,128]{2,1,0:T(1,128)S(1)} async-done(((f32[32,1,128]{2,1,0:T(1,128)}), f32[32,1,128]{2,1,0:T(1,128)S(1)}, u32[]{:S(2)}, u32[]{:S(2)}) %all-to-all-start.1) | async-done | bytes 16416 | tf_op jit(solution)/shard_map/all_to_all | solution.py:228
  66.7 3.9 %all-gather.1 = f32[64,1,128]{2,1,0:T(1,128)} all-gather(f32[32,1,128]{2,1,0:T(1,128)S(1)} %all-to-all-done.1), channel_id=3, replica_groups={{0,64},{128,192},{256,320},{384,448},{1,65},{129,193},{257,321},{385,44..., dimensions={0}, use_global_device_ids=true | all-gather | bytes 49152 | tf_op jit(solution)/shard_map/all_gather | solution.py:243
  70.5 1.4 %final.1 = (f32[1,8]{1,0:T(1,128)}, f32[8,4]{1,0:T(8,128)}) custom-call(f32[2,32,128]{2,1,0:T(8,128)} %bitcast.6), custom_call_target="tpu_custom_call" | custom-call | tf_op jit(solution)/shard_map/final/pallas_call | solution.py:246
  72.0 1.3 %copy.18 = f32[8,4]{0,1:T(4,128)} copy(f32[8,4]{1,0:T(8,128)} %get-tuple-element.27) | data formatting | bytes 256
Async XLA Ops:
  7.2 14.5 %copy-start.2 = (f32[8,4]{0,1:T(4,128)S(1)}, f32[8,4]{0,1:T(4,128)}, u32[]{:S(2)}) copy-start(f32[8,4]{0,1:T(4,128)} %param.11) | copy-start | bytes 388
  7.2 15.2 %copy-start.1 = (bf16[1,2,128,128]{3,2,1,0:T(8,128)(2,1)S(1)}, bf16[1,2,128,128]{3,2,1,0:T(8,128)(2,1)}, u32[]{:S(2)}) copy-start(bf16[1,2,128,128]{3,2,1,0:T(8,128)(2,1)} %k_ref.3) | copy-start | bytes 196612
  7.2 39.1 %all-gather.4.cloned.1.call-start = ((), (), s32[]{:S(2)}) async-start(), calls=%async_computation.2 | async-start | bytes 1622016 | tf_op jit(solution)/shard_map/all_gather | solution.py:214
  9.6 21.8 %copy-start = (bf16[1,2,128,512]{3,2,1,0:T(8,128)(2,1)S(1)}, bf16[1,2,128,512]{3,2,1,0:T(8,128)(2,1)}, u32[]{:S(2)}) copy-start(bf16[1,2,128,512]{3,2,1,0:T(8,128)(2,1)} %q_ref.3) | copy-start | bytes 786436
  49.2 17.5 %all-to-all-start.1 = ((f32[32,1,128]{2,1,0:T(1,128)}), f32[32,1,128]{2,1,0:T(1,128)S(1)}, u32[]{:S(2)}, u32[]{:S(2)}) async-start(f32[32,1,128]{2,1,0:T(1,128)} %bitcast.7), calls=%async_computation.1 | async-start | bytes 32768 | tf_op jit(solution)/shard_map/all_to_all | solution.py:228
Sparse Core Ops, SparseCore 0:
  21.8 24.4 all-gather.3

commit v2 on v1

--- a/solution.py
+++ b/solution.py
@@ -73,82 +73,89 @@
         out_ref[chip, at : at + 1, :] = diagonal
 
 
+def slots_of(placement, me):
+    held, layers = jnp.int32(0), [jnp.int32(0)] * SLOTS
+    for layer in range(LAYERS):
+        here = placement[layer] == me
+        layers = [
+            jnp.where(here & (held == slot), layer, had) for slot, had in enumerate(layers)
+        ]
+        held += here.astype(jnp.int32)
+    return layers, held
+
+
+def scores_kernel(placement, scale_ref, q_ref, k_ref, raw_ref, logp_ref):
+    layers, held = slots_of(placement, lax.axis_index("section"))
+    row, col = masks()
+    for slot in range(SLOTS):
+
+        @pl.when(slot < held)
+        def _():
+            key = k_ref[0, slot]
+            for head in range(HEADS):
+                query = q_ref[0, slot, :, head * HEAD_WIDTH : (head + 1) * HEAD_WIDTH]
+                scale = scale_ref[head, layers[slot]]
+                if head % 2:
+                    raw = dot(key, query, 1, 1) * INVERSE
+                    logp_ref[slot, head] = log_softmax(scale * raw, row <= col, 0)
+                else:
+                    raw = dot(query, key, 1, 1) * INVERSE
+                    logp_ref[slot, head] = log_softmax(scale * raw, col <= row, 1)
+                raw_ref[slot, head] = raw
+
+
 def student_kernel(
-    pairing, placement, scale_ref, packed_ref, q_ref, k_ref, sums_ref, grad_ref
+    pairing, placement, scale_ref, arrived_ref, swapped_ref, raw_ref, logp_ref, sums_ref, grad_ref
 ):
     me = lax.axis_index("section")
-    my_chip, my_core = me // 2, lax.rem(me, 2)
+    layers, held = slots_of(placement, me)
     row, col = masks()
     lane = lax.broadcasted_iota(jnp.int32, (1, TOKENS), 1)
     sums_ref[...] = jnp.zeros_like(sums_ref)
-
-    def layer_step(layer, counts):
-        home = placement[layer]
-        chip, core = home // 2, lax.rem(home, 2)
-        here = chip == my_chip
-        slot = jnp.where(core == 0, counts[0], counts[1])
-
-        @pl.when(here)
+    for slot in range(SLOTS):
+
+        @pl.when(slot < held)
         def _():
+            layer = layers[slot]
             source = pairing[layer]
-            source_chip, source_core = source // 2, lax.rem(source, 2)
-            key = k_ref[core, slot]
+            chip, direct = source // 2, lax.rem(source, 2) == lax.rem(me, 2)
+
+            def packed(at, rows):
+                near = arrived_ref[chip, at : at + rows, :]
+                far = swapped_ref[chip, at : at + rows, :]
+                return jnp.where(direct, near, far)
+
             divergence = jnp.zeros((TOKENS, TOKENS), jnp.float32)
             found = jnp.zeros((1, TOKENS), jnp.float32)
-            grads = []
             for head in range(HEADS):
-                pair, turned = head // 2, head % 2 == 1
-                query = q_ref[core, slot, :, head * HEAD_WIDTH : (head + 1) * HEAD_WIDTH]
-                square = packed_ref[
-                    source_core, source_chip, pair * TOKENS : (pair + 1) * TOKENS, :
-                ]
-                scale = scale_ref[layer, head]
-                if turned:
-                    at = 2 * TOKENS + pair
-                    diagonal = packed_ref[source_core, source_chip, at : at + 1, :]
-                    visible, axis = row <= col, 0
-                    target_logp = jnp.where(
-                        row < col, square, jnp.where(row == col, diagonal, HIDDEN)
-                    )
-                    raw = dot(key, query, 1, 1) * INVERSE
+                pair = head // 2
+                scale = scale_ref[head, layer]
+                square = packed(pair * TOKENS, TOKENS)
+                if head % 2:
+                    diagonal = packed(2 * TOKENS + pair, 1)
+                    visible = row <= col
+                    target_logp = jnp.where(row == col, diagonal, square)
                 else:
-                    visible, axis = col <= row, 1
-                    target_logp = jnp.where(visible, square, HIDDEN)
-                    raw = dot(query, key, 1, 1) * INVERSE
-                student_logp = log_softmax(scale * raw, visible, axis)
+                    visible = col <= row
+                    target_logp = square
+                target_logp = jnp.where(visible, target_logp, HIDDEN)
+                student_logp = logp_ref[slot, head]
                 target = jnp.exp(target_logp)
                 divergence += jnp.where(
                     visible, target * (target_logp - student_logp), 0.0
                 )
                 difference = jnp.where(visible, jnp.exp(student_logp) - target, 0.0)
                 found = jnp.where(
-                    lane == SCALE_LANE + HEADS * layer + head,
-                    jnp.sum(difference * raw),
+                    lane == SCALE_LANE + LAYERS * head + layer,
+                    jnp.sum(difference * raw_ref[slot, head]),
                     found,
                 )
-                grads.append((difference * (scale * INVERSE)).astype(jnp.bfloat16))
-            found = jnp.where(lane == layer, jnp.sum(divergence), found)
-            sums_ref[...] += jnp.broadcast_to(found, sums_ref.shape)
-
-            @pl.when(core == my_core)
-            def _():
-                for head in range(HEADS):
-                    grad_ref[slot, head] = grads[head]
-
-        one = jnp.int32(1)
-        return (
-            counts[0] + jnp.where(here & (core == 0), one, 0),
-            counts[1] + jnp.where(here & (core == 1), one, 0),
-        )
-
-    lax.fori_loop(0, LAYERS, layer_step, (jnp.int32(0), jnp.int32(0)))
+                grad_ref[slot, head] = (difference * (scale * INVERSE)).astype(jnp.bfloat16)
+            sums_ref[...] += jnp.where(lane == layer, jnp.sum(divergence), found)
 
 
 def gradient_kernel(placement, grad_ref, q_ref, k_ref, q_out, k_out):
-    me = lax.axis_index("section")
-    held = jnp.int32(0)
-    for layer in range(LAYERS):
-        held += (placement[layer] == me).astype(jnp.int32)
+    _, held = slots_of(placement, lax.axis_index("section"))
     for slot in range(SLOTS):
 
         @pl.when(slot < held)
@@ -174,14 +181,9 @@
     divergence = jnp.sum(rows_ref[0], axis=0, keepdims=True)
     kl_ref[...] = divergence[:, :LAYERS] / (STUDENT_HEADS * TOKENS)
     terms = jnp.sum(rows_ref[1], axis=0, keepdims=True)
-    terms = jnp.broadcast_to(terms, (LAYERS, TOKENS))
-    lane = lax.broadcasted_iota(jnp.int32, (LAYERS, TOKENS), 1)
-    layer = lax.broadcasted_iota(jnp.int32, (LAYERS, TOKENS), 0)
-    at = lane - SCALE_LANE - HEADS * layer
-    for head in range(HEADS):
-        scale_ref[:, head : head + 1] = jnp.sum(
-            jnp.where(at == head, terms, 0.0), axis=1, keepdims=True
-        )
+    scale_ref[...] = jnp.concatenate(
+        [terms[:, SCALE_LANE + LAYERS * h : SCALE_LANE + LAYERS * (h + 1)] for h in range(HEADS)], axis=0
+    )
 
 
 VMEM = pl.BlockSpec(memory_space=pltpu.VMEM)
@@ -209,24 +211,38 @@
     arrived = lax.all_to_all(
         packed, "section", 0, 0, tiled=True, axis_index_groups=over_x
     )
-    chip_q = lax.all_gather(student_q[0], "section", axis_index_groups=of_chip)
-    chip_k = lax.all_gather(student_k[0], "section", axis_index_groups=of_chip)
-    chip_packed = lax.all_gather(arrived, "section", axis_index_groups=of_chip)
+    square = jax.ShapeDtypeStruct((SLOTS, HEADS, TOKENS, TOKENS), f32)
+    raw, logp = pl.pallas_call(
+        scores_kernel,
+        out_shape=(square, square),
+        in_specs=[SMEM, SMEM, VMEM, VMEM],
+        out_specs=(VMEM, VMEM),
+        cost_estimate=cost(8 * 2 * TOKENS**3, 1_400_000),
+        name="scores",
+    )(placement, student_scale.T, student_q, student_k)
+    swap = [(s, s ^ 1) for s in range(2 * chips)]
+    swapped = lax.ppermute(arrived, "section", swap)
 
     sums, grads = pl.pallas_call(
         student_kernel,
         out_shape=(
-            jax.ShapeDtypeStruct((members, TOKENS), f32),
+            jax.ShapeDtypeStruct((1, TOKENS), f32),
             jax.ShapeDtypeStruct((SLOTS, HEADS, TOKENS, TOKENS), bf16),
         ),
-        in_specs=[SMEM, SMEM, SMEM, VMEM, VMEM, VMEM],
+        in_specs=[SMEM, SMEM, SMEM, VMEM, VMEM, VMEM, VMEM],
         out_specs=(VMEM, VMEM),
         cost_estimate=cost(8 * 2 * TOKENS**3, 1_800_000),
         name="student",
-    )(pairing, placement, student_scale, chip_packed, chip_q, chip_k)
-
+    )(pairing, placement, student_scale.T, arrived, swapped, raw, logp)
+
+    sums = lax.all_gather(sums, "section", axis_index_groups=of_chip).sum(axis=0)
     rows = lax.all_to_all(
-        sums.reshape(members, 1, TOKENS), AXES, 0, 0, tiled=True, axis_index_groups=groups
+        jnp.broadcast_to(sums[None], (members, 1, TOKENS)),
+        AXES,
+        0,
+        0,
+        tiled=True,
+        axis_index_groups=groups,
     )
     q_grad, k_grad = pl.pallas_call(
         gradient_kernel,
@@ -247,13 +263,13 @@
         final_kernel,
         out_shape=(
             jax.ShapeDtypeStruct((1, LAYERS), f32),
-            jax.ShapeDtypeStruct((LAYERS, HEADS), f32),
+            jax.ShapeDtypeStruct((HEADS, LAYERS), f32),
         ),
         in_specs=[VMEM],
         out_specs=(VMEM, VMEM),
         name="final",
     )(both)
-    return (q_grad, k_grad, layer_kl, scale_grad)
+    return (q_grad, k_grad, layer_kl, scale_grad.T)
 
 
 def reduction_groups(sections, heads, replicas):

time: 80.5 us -> 54.6 us (0.68)
  between operations: 14.1 us -> 0.66 us
  waiting for transfers between devices: 19.5 us -> 6.6 us
  blocking collectives: 27.2 us -> 20.1 us
  starting transfers between devices: 8.87 us -> 13.9 us
  Pallas kernels: 8.47 us -> 10.8 us
    all_gather x1 -> x0, waiting for transfers between devices: 12.7 us -> none  [local(): chip_packed = lax.all_gather(arrived, 'section', axis_index_groups=of_chip)]
    all_gather x2 -> x1, blocking collectives: 11.3 us -> 1.75 us  [local(): lax.all_gather(sums, 'section', axis_index_groups=of_chip).sum(axis=0)]
    ppermute x0 -> x1, starting transfers between devices: none -> 8.52 us  [local(): swapped = lax.ppermute(arrived, 'section', swap)]
    all_to_all x1, starting transfers between devices: 8.83 us -> 5.4 us  [local(): lax.all_to_all(jnp.broadcast_to(sums[None], (members, 1, TOKENS)), AXES,...]
    all_gather x1, blocking collectives: 3.87 us -> 6.46 us  [local(): lax.all_gather(rows.reshape(members, TOKENS), 'section', axis_index_group...]
    pallas_call x1 -> x2, Pallas kernels: 2.88 us -> 4.97 us  [the longest x1 2.57 us: local(): pl.pallas_call(student_kernel, out_shape=(jax.ShapeDtypeStruct((1, TOKENS...]
    unnamed x8 -> x6, local copies, waits for them, and re-layouts: 2.01 us -> 1.45 us
  transfers between devices with their start and end apart: 2 -> 2, of which waited for: 2 -> 1; matrix products, arithmetic and copies ran while one was open for 1% -> 0% of each run, Pallas kernels for 2% -> 8%
where the time goes in v2:
time: 54.6 us; the launch traced here: 54.2 us
  blocking collectives  20.1 us (37%)
  starting transfers between devices  13.9 us (25%)
  Pallas kernels  10.8 us (20%)
  waiting for transfers between devices  6.6 us (12%)
  local copies, waits for them, and re-layouts  2.06 us (4%)
  between operations  0.66 us (1%)
    all_to_all x1, blocking collectives, local(): lax.all_to_all(packed, 'section', 0, 0, tiled=True, axis_index_groups=ove...  11.9 us
    ppermute x1, starting transfers between devices, local(): swapped = lax.ppermute(arrived, 'section', swap)  8.52 us
    all_to_all x1, waiting for transfers between devices, local(): lax.all_to_all(jnp.broadcast_to(sums[None], (members, 1, TOKENS)), AXES,...  6.59 us
    all_gather x1, blocking collectives, local(): lax.all_gather(rows.reshape(members, TOKENS), 'section', axis_index_group...  6.46 us
    all_to_all x1, starting transfers between devices, local(): lax.all_to_all(jnp.broadcast_to(sums[None], (members, 1, TOKENS)), AXES,...  5.4 us
    pallas_call x1, Pallas kernels, local(): pl.pallas_call(student_kernel, out_shape=(jax.ShapeDtypeStruct((1, TOKENS...  2.57 us
    pallas_call x1, Pallas kernels, local(): pl.pallas_call(scores_kernel, out_shape=(square, square), in_specs=[SMEM,...  2.4 us
    pallas_call x1, Pallas kernels, local(): pl.pallas_call(teacher_kernel, out_shape=jax.ShapeDtypeStruct((chips, PAC...  2.36 us
  transfers between devices with their start and end apart: 2, of which 1 were waited for; matrix products, arithmetic and copies ran while one was open for 0% of the time, Pallas kernels for 8%

profile of v2, /device:TPU:1, one launch (start us, length us, event | category | flops | bytes accessed | tf_op | source)
XLA Modules:
  0.0 54.2 jit_solution(10780316339810215213)
XLA Ops:
  0.6 2.4 %teacher.1 = f32[4,264,128]{2,1,0:T(8,128)} custom-call(s32[8]{0:T(128)} %pairing.3, s32[8]{0:T(128)} %placement.7, bf16[1,128,1024]{2,1,0:T(8,128)(2,1)} %q_ref.3, bf16[1,128,128]{2,1,0:T(8,128)(2,1)} %k_ref.3), custom_call_target="tpu_custom_call" | custom-call | flops 33554432 | bytes 400000 | tf_op jit(solution)/shard_map/teacher/pallas_call | solution.py:203
  3.0 11.9 %all_to_all.10.arrived_ref = f32[4,264,128]{2,1,0:T(8,128)S(1)} all-to-all(f32[4,264,128]{2,1,0:T(8,128)} %teacher.1), channel_id=1, replica_groups={{0,128,256,384},{64,192,320,448},{1,129,257,385},{65,193,321,449},{2,13..., dimensions={0} | all-to-all | bytes 1081344 | tf_op jit(solution)/shard_map/all_to_all | solution.py:211
  14.8 0.0 copy-start
  14.9 8.5 %collective-permute-start = (f32[4,264,128]{2,1,0:T(8,128)S(1)}, f32[4,264,128]{2,1,0:T(8,128)S(1)}, u32[]{:S(2)}, u32[]{:S(2)}) collective-permute-start(f32[4,264,128]{2,1,0:T(8,128)S(1)} %all_to_all.10.arrived_ref), channel_id=1, source_target_pairs={{0,64},{64,0},{128,192},{192,128},{256,320},{320,256},{384,448},{4... | collective-permute-start | bytes 1622024 | tf_op jit(solution)/shard_map/ppermute | solution.py:224
  23.4 2.4 %scores.1 = (f32[2,4,128,128]{3,2,1,0:T(8,128)}, f32[2,4,128,128]{3,2,1,0:T(8,128)}) custom-call(s32[8]{0:T(128)} %placement.7, f32[4,8]{1,0:T(4,128)} %bitcast.5, bf16[1,2,128,512]{3,2,1,0:T(8,128)(2,1)} %q_ref.5, bf16[1,2,128,128]{3,2,1,0:T(8,128)(2,1)} %k_ref.5), custom_call_target="tpu_custom_call" | custom-call | flops 33554432 | bytes 1400000 | tf_op jit(solution)/shard_map/scores/pallas_call | solution.py:215
  25.8 0.0 collective-permute-done.swapped_ref
  25.8 0.0 copy-start.1
  25.8 0.0 copy-done
  25.8 0.8 %copy-done.1 = f32[4,264,128]{2,1,0:T(8,128)} copy-done((f32[4,264,128]{2,1,0:T(8,128)}, f32[4,264,128]{2,1,0:T(8,128)S(1)}, u32[]{:S(2)}) %copy-start.1) | copy-done | bytes 540696
  26.6 2.6 %student.1 = (f32[1,128]{1,0:T(1,128)}, bf16[2,4,128,128]{3,2,1,0:T(8,128)(2,1)}) custom-call(s32[8]{0:T(128)} %pairing.3, s32[8]{0:T(128)} %placement.7, f32[4,8]{1,0:T(4,128)} %bitcast.6, f32[4,264,128]{2,1,0:T(8,128)} %copy-done, f32[4,264,128]{2,1,0:T(8,128)} %copy-done.1, f32[2,4,128,128]{3,2,1,0:T(8,128)} %get-tuple-element.12.raw_ref, ...), custom_call_target="tpu_custom_call" | custom-call | flops 33554432 | bytes 1800000 | tf_op jit(solution)/shard_map/student/pallas_call | solution.py:226
  29.2 0.0 copy-start.2
  29.2 0.7 %copy-done.2 = f32[1,128]{1,0:T(1,128)S(1)} copy-done((f32[1,128]{1,0:T(1,128)S(1)}, f32[1,128]{1,0:T(1,128)}, u32[]{:S(2)}) %copy-start.2) | copy-done | bytes 536
  29.8 1.8 %all-gather.2 = f32[2,1,128]{2,1,0:T(1,128)S(1)} all-gather(f32[1,1,128]{2,1,0:T(1,128)S(1)} %bitcast.8), channel_id=2, replica_groups={{0,64},{128,192},{256,320},{384,448},{1,65},{129,193},{257,321},{385,44..., dimensions={0}, use_global_device_ids=true | all-gather | bytes 1536 | tf_op jit(solution)/shard_map/all_gather | solution.py:238
  31.6 0.6 %broadcast_in_dim.2 = f32[32,1,128]{2,1,0:T(1,128)} broadcast(f32[128]{0:T(128)S(1)} %reduce.1), dimensions={2} | broadcast | bytes 16896 | tf_op jit(solution)/shard_map/broadcast_in_dim | solution.py:240
  32.2 5.4 %all-to-all-start.1 = ((f32[32,1,128]{2,1,0:T(1,128)}), f32[32,1,128]{2,1,0:T(1,128)S(1)}, u32[]{:S(2)}, u32[]{:S(2)}) async-start(f32[32,1,128]{2,1,0:T(1,128)} %broadcast_in_dim.2), calls=%async_computation.1 | async-start | bytes 32768 | tf_op jit(solution)/shard_map/all_to_all | solution.py:239
  37.6 2.0 %gradient.1 = (bf16[1,2,128,512]{3,2,1,0:T(8,128)(2,1)}, bf16[1,2,128,128]{3,2,1,0:T(8,128)(2,1)}) custom-call(s32[8]{0:T(128)} %placement.7, bf16[2,4,128,128]{3,2,1,0:T(8,128)(2,1)} %get-tuple-element.14.grad_ref, bf16[1,2,128,512]{3,2,1,0:T(8,128)(2,1)} %q_ref.5, bf16[1,2,128,128]{3,2,1,0:T(8,128)(2,1)} %k_ref.5), custom_call_target="tpu_custom_call" | custom-call | flops 67108864 | bytes 900000 | tf_op jit(solution)/shard_map/gradient/pallas_call | solution.py:247
  39.6 6.6 %all-to-all-done.1 = f32[32,1,128]{2,1,0:T(1,128)S(1)} async-done(((f32[32,1,128]{2,1,0:T(1,128)}), f32[32,1,128]{2,1,0:T(1,128)S(1)}, u32[]{:S(2)}, u32[]{:S(2)}) %all-to-all-start.1) | async-done | bytes 16416 | tf_op jit(solution)/shard_map/all_to_all | solution.py:239
  46.2 6.5 %all-gather.1 = f32[64,1,128]{2,1,0:T(1,128)} all-gather(f32[32,1,128]{2,1,0:T(1,128)S(1)} %all-to-all-done.1), channel_id=3, replica_groups={{0,64},{128,192},{256,320},{384,448},{1,65},{129,193},{257,321},{385,44..., dimensions={0}, use_global_device_ids=true | all-gather | bytes 49152 | tf_op jit(solution)/shard_map/all_gather | solution.py:259
  52.7 1.5 %final.1 = (f32[1,8]{1,0:T(1,128)}, f32[4,8]{1,0:T(4,128)}) custom-call(f32[2,32,128]{2,1,0:T(8,128)} %bitcast.4), custom_call_target="tpu_custom_call" | custom-call | tf_op jit(solution)/shard_map/final/pallas_call | solution.py:262
  (1 shorter events, 0.0 us)
Async XLA Ops:
  14.8 10.9 %copy-start = (f32[4,264,128]{2,1,0:T(8,128)}, f32[4,264,128]{2,1,0:T(8,128)S(1)}, u32[]{:S(2)}) copy-start(f32[4,264,128]{2,1,0:T(8,128)S(1)} %all_to_all.10.arrived_ref) | copy-start | bytes 1622020
  14.9 10.9 %collective-permute-start = (f32[4,264,128]{2,1,0:T(8,128)S(1)}, f32[4,264,128]{2,1,0:T(8,128)S(1)}, u32[]{:S(2)}, u32[]{:S(2)}) collective-permute-start(f32[4,264,128]{2,1,0:T(8,128)S(1)} %all_to_all.10.arrived_ref), channel_id=1, source_target_pairs={{0,64},{64,0},{128,192},{192,128},{256,320},{320,256},{384,448},{4... | collective-permute-start | bytes 1622024 | tf_op jit(solution)/shard_map/ppermute | solution.py:224
  25.8 0.8 %copy-start.1 = (f32[4,264,128]{2,1,0:T(8,128)}, f32[4,264,128]{2,1,0:T(8,128)S(1)}, u32[]{:S(2)}) copy-start(f32[4,264,128]{2,1,0:T(8,128)S(1)} %collective-permute-done.swapped_ref) | copy-start | bytes 1622020
  29.2 0.7 %copy-start.2 = (f32[1,128]{1,0:T(1,128)S(1)}, f32[1,128]{1,0:T(1,128)}, u32[]{:S(2)}) copy-start(f32[1,128]{1,0:T(1,128)} %get-tuple-element.17) | copy-start | bytes 1540
  32.2 14.0 %all-to-all-start.1 = ((f32[32,1,128]{2,1,0:T(1,128)}), f32[32,1,128]{2,1,0:T(1,128)S(1)}, u32[]{:S(2)}, u32[]{:S(2)}) async-start(f32[32,1,128]{2,1,0:T(1,128)} %broadcast_in_dim.2), calls=%async_computation.1 | async-start | bytes 32768 | tf_op jit(solution)/shard_map/all_to_all | solution.py:239

commit v3 on v2

--- a/solution.py
+++ b/solution.py
@@ -190,6 +190,10 @@
 SMEM = pl.BlockSpec(memory_space=pltpu.SMEM)
 
 
+def kept(array):
+    return pltpu.with_memory_space_constraint(array, pltpu.VMEM)
+
+
 def cost(flops, moved):
     return pl.CostEstimate(flops=flops, bytes_accessed=moved, transcendentals=0)
 
@@ -202,7 +206,7 @@
 
     packed = pl.pallas_call(
         teacher_kernel,
-        out_shape=jax.ShapeDtypeStruct((chips, PACKED, TOKENS), f32),
+        out_shape=pltpu.VMEM((chips, PACKED, TOKENS), f32),
         in_specs=[SMEM, SMEM, VMEM, VMEM],
         out_specs=VMEM,
         cost_estimate=cost(8 * 2 * TOKENS**3, 400_000),
@@ -211,7 +215,7 @@
     arrived = lax.all_to_all(
         packed, "section", 0, 0, tiled=True, axis_index_groups=over_x
     )
-    square = jax.ShapeDtypeStruct((SLOTS, HEADS, TOKENS, TOKENS), f32)
+    square = pltpu.VMEM((SLOTS, HEADS, TOKENS, TOKENS), f32)
     raw, logp = pl.pallas_call(
         scores_kernel,
         out_shape=(square, square),
@@ -226,14 +230,14 @@
     sums, grads = pl.pallas_call(
         student_kernel,
         out_shape=(
-            jax.ShapeDtypeStruct((1, TOKENS), f32),
-            jax.ShapeDtypeStruct((SLOTS, HEADS, TOKENS, TOKENS), bf16),
+            pltpu.VMEM((1, TOKENS), f32),
+            pltpu.VMEM((SLOTS, HEADS, TOKENS, TOKENS), bf16),
         ),
         in_specs=[SMEM, SMEM, SMEM, VMEM, VMEM, VMEM, VMEM],
         out_specs=(VMEM, VMEM),
         cost_estimate=cost(8 * 2 * TOKENS**3, 1_800_000),
         name="student",
-    )(pairing, placement, student_scale.T, arrived, swapped, raw, logp)
+    )(pairing, placement, student_scale.T, *map(kept, (arrived, swapped, raw, logp)))
 
     sums = lax.all_gather(sums, "section", axis_index_groups=of_chip).sum(axis=0)
     rows = lax.all_to_all(
@@ -254,7 +258,7 @@
         out_specs=(VMEM, VMEM),
         cost_estimate=cost(16 * 2 * TOKENS**3, 900_000),
         name="gradient",
-    )(placement, grads, student_q, student_k)
+    )(placement, kept(grads), student_q, student_k)
 
     both = lax.all_gather(
         rows.reshape(members, TOKENS), "section", axis_index_groups=of_chip
@@ -268,7 +272,7 @@
         in_specs=[VMEM],
         out_specs=(VMEM, VMEM),
         name="final",
-    )(both)
+    )(kept(both))
     return (q_grad, k_grad, layer_kl, scale_grad.T)
 
 

time: 54.6 us -> 48.7 us (0.89)
  Pallas kernels: 10.8 us -> 6.65 us
  local copies, waits for them, and re-layouts: 2.06 us -> 0.61 us
    pallas_call x2, Pallas kernels: 4.92 us -> 2.58 us  [the longest x1 1.54 us: local(): pl.pallas_call(teacher_kernel, out_shape=pltpu.VMEM((chips, PACKED, TOKEN...]
    unnamed x6 -> x0, local copies, waits for them, and re-layouts: 1.45 us -> none
    pallas_call x1, Pallas kernels: 2.4 us -> 1.38 us  [local(): pl.pallas_call(scores_kernel, out_shape=(square, square), in_specs=[SMEM,...]
    ppermute x1, starting transfers between devices: 8.52 us -> 7.65 us  [local(): swapped = lax.ppermute(arrived, 'section', swap)]
    pallas_call x1, Pallas kernels: 1.48 us -> 0.73 us  [local(): pl.pallas_call(final_kernel, out_shape=(jax.ShapeDtypeStruct((1, LAYERS),...]
    all_to_all x1, starting transfers between devices: 5.4 us -> 6.1 us  [local(): lax.all_to_all(jnp.broadcast_to(sums[None], (members, 1, TOKENS)), AXES,...]
  transfers between devices with their start and end apart: 2 -> 2, of which waited for: 1 -> 2; matrix products, arithmetic and copies ran while one was open for 0% -> 0% of each run, Pallas kernels for 8% -> 7%
where the time goes in v3:
time: 48.7 us; the launch traced here: 48.4 us
  blocking collectives  19.8 us (41%)
  starting transfers between devices  13.8 us (28%)
  waiting for transfers between devices  6.82 us (14%)
  Pallas kernels  6.65 us (14%)
  between operations  0.67 us (1%)
  local copies, waits for them, and re-layouts  0.61 us (1%)
    all_to_all x1, blocking collectives, local(): lax.all_to_all(packed, 'section', 0, 0, tiled=True, axis_index_groups=ove...  11.7 us
    ppermute x1, starting transfers between devices, local(): swapped = lax.ppermute(arrived, 'section', swap)  7.65 us
    all_to_all x1, waiting for transfers between devices, local(): lax.all_to_all(jnp.broadcast_to(sums[None], (members, 1, TOKENS)), AXES,...  6.67 us
    all_gather x1, blocking collectives, local(): lax.all_gather(rows.reshape(members, TOKENS), 'section', axis_index_group...  6.33 us
    all_to_all x1, starting transfers between devices, local(): lax.all_to_all(jnp.broadcast_to(sums[None], (members, 1, TOKENS)), AXES,...  6.1 us
    pallas_call x1, Pallas kernels, local(): pl.pallas_call(gradient_kernel, out_shape=(jax.ShapeDtypeStruct(student_q...  1.96 us
    all_gather x1, blocking collectives, local(): lax.all_gather(sums, 'section', axis_index_groups=of_chip).sum(axis=0)  1.84 us
    pallas_call x1, Pallas kernels, local(): pl.pallas_call(teacher_kernel, out_shape=pltpu.VMEM((chips, PACKED, TOKEN...  1.54 us
  transfers between devices with their start and end apart: 2, of which 2 were waited for; matrix products, arithmetic and copies ran while one was open for 0% of the time, Pallas kernels for 7%

profile of v3, /device:TPU:1, one launch (start us, length us, event | category | flops | bytes accessed | tf_op | source)
XLA Modules:
  0.0 48.4 jit_solution(5955076107914763002)
XLA Ops:
  0.6 1.5 %teacher.1 = f32[4,264,128]{2,1,0:T(8,128)S(1)} custom-call(s32[8]{0:T(128)} %pairing.3, s32[8]{0:T(128)} %placement.7, bf16[1,128,1024]{2,1,0:T(8,128)(2,1)} %q_ref.3, bf16[1,128,128]{2,1,0:T(8,128)(2,1)} %k_ref.3), custom_call_target="tpu_custom_call" | custom-call | flops 33554432 | bytes 400000 | tf_op jit(solution)/shard_map/teacher/pallas_call | solution.py:207
  2.2 11.7 %all_to_all.10.arrived_ref = f32[4,264,128]{2,1,0:T(8,128)S(1)} all-to-all(f32[4,264,128]{2,1,0:T(8,128)S(1)} %teacher.1), channel_id=1, replica_groups={{0,128,256,384},{64,192,320,448},{1,129,257,385},{65,193,321,449},{2,13..., dimensions={0} | all-to-all | bytes 1081344 | tf_op jit(solution)/shard_map/all_to_all | solution.py:215
  13.8 7.7 %collective-permute-start = (f32[4,264,128]{2,1,0:T(8,128)S(1)}, f32[4,264,128]{2,1,0:T(8,128)S(1)}, u32[]{:S(2)}, u32[]{:S(2)}) collective-permute-start(f32[4,264,128]{2,1,0:T(8,128)S(1)} %all_to_all.10.arrived_ref), channel_id=1, source_target_pairs={{0,64},{64,0},{128,192},{192,128},{256,320},{320,256},{384,448},{4... | collective-permute-start | bytes 1622024 | tf_op jit(solution)/shard_map/ppermute | solution.py:228
  21.5 1.4 %scores.1 = (f32[2,4,128,128]{3,2,1,0:T(8,128)S(1)}, f32[2,4,128,128]{3,2,1,0:T(8,128)S(1)}) custom-call(s32[8]{0:T(128)} %placement.7, f32[4,8]{1,0:T(4,128)} %bitcast.6, bf16[1,2,128,512]{3,2,1,0:T(8,128)(2,1)} %q_ref.5, bf16[1,2,128,128]{3,2,1,0:T(8,128)(2,1)} %k_ref.5), custom_call_target="tpu_custom_call" | custom-call | flops 33554432 | bytes 1400000 | tf_op jit(solution)/shard_map/scores/pallas_call | solution.py:219
  22.9 0.2 collective-permute-done.swapped_ref
  23.0 1.0 %student.1 = (f32[1,128]{1,0:T(1,128)S(1)}, bf16[2,4,128,128]{3,2,1,0:T(8,128)(2,1)S(1)}) custom-call(s32[8]{0:T(128)} %pairing.3, s32[8]{0:T(128)} %placement.7, f32[4,8]{1,0:T(4,128)} %bitcast.7, f32[4,264,128]{2,1,0:T(8,128)S(1)} %all_to_all.10.arrived_ref, f32[4,264,128]{2,1,0:T(8,128)S(1)} %collective-permute-done.swapped_ref, ...), custom_call_target="tpu_custom_call" | custom-call | flops 33554432 | bytes 1800000 | tf_op jit(solution)/shard_map/student/pallas_call | solution.py:230
  24.1 1.8 %all-gather.2 = f32[2,1,128]{2,1,0:T(1,128)S(1)} all-gather(f32[1,1,128]{2,1,0:T(1,128)S(1)} %bitcast.5), channel_id=2, replica_groups={{0,64},{128,192},{256,320},{384,448},{1,65},{129,193},{257,321},{385,44..., dimensions={0}, use_global_device_ids=true | all-gather | bytes 1536 | tf_op jit(solution)/shard_map/all_gather | solution.py:242
  25.9 0.6 %broadcast_in_dim.2 = f32[32,1,128]{2,1,0:T(1,128)} broadcast(f32[128]{0:T(128)S(1)} %reduce.1), dimensions={2} | broadcast | bytes 16896 | tf_op jit(solution)/shard_map/broadcast_in_dim | solution.py:244
  26.6 6.1 %all-to-all-start.1 = ((f32[32,1,128]{2,1,0:T(1,128)}), f32[32,1,128]{2,1,0:T(1,128)S(1)}, u32[]{:S(2)}, u32[]{:S(2)}) async-start(f32[32,1,128]{2,1,0:T(1,128)} %broadcast_in_dim.2), calls=%async_computation.1 | async-start | bytes 32768 | tf_op jit(solution)/shard_map/all_to_all | solution.py:243
  32.7 2.0 %gradient.1 = (bf16[1,2,128,512]{3,2,1,0:T(8,128)(2,1)}, bf16[1,2,128,128]{3,2,1,0:T(8,128)(2,1)}) custom-call(s32[8]{0:T(128)} %placement.7, bf16[2,4,128,128]{3,2,1,0:T(8,128)(2,1)S(1)} %get-tuple-element.14.grad_ref, bf16[1,2,128,512]{3,2,1,0:T(8,128)(2,1)} %q_ref.5, bf16[1,2,128,128]{3,2,1,0:T(8,128)(2,1)} %k_ref.5), custom_call_target="tpu_custom_call" | custom-call | flops 67108864 | bytes 900000 | tf_op jit(solution)/shard_map/gradient/pallas_call | solution.py:251
  34.6 6.7 %all-to-all-done.1 = f32[32,1,128]{2,1,0:T(1,128)S(1)} async-done(((f32[32,1,128]{2,1,0:T(1,128)}), f32[32,1,128]{2,1,0:T(1,128)S(1)}, u32[]{:S(2)}, u32[]{:S(2)}) %all-to-all-start.1) | async-done | bytes 16416 | tf_op jit(solution)/shard_map/all_to_all | solution.py:243
  41.3 6.3 %all-gather.1 = f32[64,1,128]{2,1,0:T(1,128)S(1)} all-gather(f32[32,1,128]{2,1,0:T(1,128)S(1)} %all-to-all-done.1), channel_id=3, replica_groups={{0,64},{128,192},{256,320},{384,448},{1,65},{129,193},{257,321},{385,44..., dimensions={0}, use_global_device_ids=true | all-gather | bytes 49152 | tf_op jit(solution)/shard_map/all_gather | solution.py:263
  47.6 0.7 %final.1 = (f32[1,8]{1,0:T(1,128)}, f32[4,8]{1,0:T(4,128)}) custom-call(f32[2,32,128]{2,1,0:T(8,128)S(1)} %bitcast.4), custom_call_target="tpu_custom_call" | custom-call | tf_op jit(solution)/shard_map/final/pallas_call | solution.py:266
  (1 shorter events, 0.0 us)
Async XLA Ops:
  13.8 9.2 %collective-permute-start = (f32[4,264,128]{2,1,0:T(8,128)S(1)}, f32[4,264,128]{2,1,0:T(8,128)S(1)}, u32[]{:S(2)}, u32[]{:S(2)}) collective-permute-start(f32[4,264,128]{2,1,0:T(8,128)S(1)} %all_to_all.10.arrived_ref), channel_id=1, source_target_pairs={{0,64},{64,0},{128,192},{192,128},{256,320},{320,256},{384,448},{4... | collective-permute-start | bytes 1622024 | tf_op jit(solution)/shard_map/ppermute | solution.py:228
  26.6 14.7 %all-to-all-start.1 = ((f32[32,1,128]{2,1,0:T(1,128)}), f32[32,1,128]{2,1,0:T(1,128)S(1)}, u32[]{:S(2)}, u32[]{:S(2)}) async-start(f32[32,1,128]{2,1,0:T(1,128)} %broadcast_in_dim.2), calls=%async_computation.1 | async-start | bytes 32768 | tf_op jit(solution)/shard_map/all_to_all | solution.py:243

commit v4 on v3

--- a/solution.py
+++ b/solution.py
@@ -73,7 +73,107 @@
         out_ref[chip, at : at + 1, :] = diagonal
 
 
-def slots_of(placement, me):
+def for_my_layers(pairing, placement, work):
+    me = lax.axis_index("section")
+    chip, core = me // 2, lax.rem(me, 2)
+
+    def step(layer, carry):
+        slots, rank = carry[:2], carry[2]
+        home, source = placement[layer], pairing[layer]
+        home_core = lax.rem(home, 2)
+        here = home // 2 == chip
+        mine = here & (lax.rem(source, 2) == core)
+        slot = jnp.where(home_core == 0, slots[0], slots[1])
+
+        @pl.when(mine)
+        def _():
+            work(layer, source // 2, home_core, slot, rank)
+
+        return (
+            slots[0] + (here & (home_core == 0)).astype(jnp.int32),
+            slots[1] + (here & (home_core == 1)).astype(jnp.int32),
+            rank + mine.astype(jnp.int32),
+        )
+
+    lax.fori_loop(0, LAYERS, step, (jnp.int32(0),) * 3)
+
+
+def scores_kernel(pairing, placement, scale_ref, q_ref, k_ref, raw_ref, logp_ref):
+    row, col = masks()
+
+    def work(layer, source_chip, home_core, slot, rank):
+        key = k_ref[home_core, slot]
+        for head in range(HEADS):
+            query = q_ref[home_core, slot, :, head * HEAD_WIDTH : (head + 1) * HEAD_WIDTH]
+            scale = scale_ref[head, layer]
+            if head % 2:
+                raw = dot(key, query, 1, 1) * INVERSE
+                logp_ref[rank, head] = log_softmax(scale * raw, row <= col, 0)
+            else:
+                raw = dot(query, key, 1, 1) * INVERSE
+                logp_ref[rank, head] = log_softmax(scale * raw, col <= row, 1)
+            raw_ref[rank, head] = raw
+
+    for_my_layers(pairing, placement, work)
+
+
+def student_kernel(
+    pairing, placement, scale_ref, arrived_ref, raw_ref, logp_ref, sums_ref, grad_ref, sent_ref
+):
+    core = lax.rem(lax.axis_index("section"), 2)
+    row, col = masks()
+    lane = lax.broadcasted_iota(jnp.int32, (1, TOKENS), 1)
+    sums_ref[...] = jnp.zeros_like(sums_ref)
+
+    def work(layer, source_chip, home_core, slot, rank):
+        divergence = jnp.zeros((TOKENS, TOKENS), jnp.float32)
+        found = jnp.zeros((1, TOKENS), jnp.float32)
+        grads = []
+        for head in range(HEADS):
+            pair = head // 2
+            scale = scale_ref[head, layer]
+            square = arrived_ref[source_chip, pair * TOKENS : (pair + 1) * TOKENS, :]
+            if head % 2:
+                at = 2 * TOKENS + pair
+                diagonal = arrived_ref[source_chip, at : at + 1, :]
+                visible = row <= col
+                target_logp = jnp.where(row == col, diagonal, square)
+            else:
+                visible = col <= row
+                target_logp = square
+            target_logp = jnp.where(visible, target_logp, HIDDEN)
+            student_logp = logp_ref[rank, head]
+            target = jnp.exp(target_logp)
+            divergence += jnp.where(visible, target * (target_logp - student_logp), 0.0)
+            difference = jnp.where(visible, jnp.exp(student_logp) - target, 0.0)
+            found = jnp.where(
+                lane == SCALE_LANE + LAYERS * head + layer,
+                jnp.sum(difference * raw_ref[rank, head]),
+                found,
+            )
+            grads.append((difference * (scale * INVERSE)).astype(jnp.bfloat16))
+        sums_ref[...] += jnp.where(lane == layer, jnp.sum(divergence), found)
+
+        @pl.when(home_core == core)
+        def _():
+            for head in range(HEADS):
+                grad_ref[slot, head] = grads[head]
+
+        @pl.when(home_core != core)
+        def _():
+            for head in range(HEADS):
+                sent_ref[slot, head] = grads[head]
+
+    for_my_layers(pairing, placement, work)
+
+
+def spread_kernel(pair_ref, out_ref):
+    out_ref[...] = jnp.broadcast_to(pair_ref[0] + pair_ref[1], out_ref.shape)
+
+
+def gradient_kernel(pairing, placement, grad_ref, sent_ref, q_ref, k_ref, q_out, k_out):
+    me = lax.axis_index("section")
+    core = lax.rem(me, 2)
     held, layers = jnp.int32(0), [jnp.int32(0)] * SLOTS
     for layer in range(LAYERS):
         here = placement[layer] == me
@@ -81,91 +181,17 @@
             jnp.where(here & (held == slot), layer, had) for slot, had in enumerate(layers)
         ]
         held += here.astype(jnp.int32)
-    return layers, held
-
-
-def scores_kernel(placement, scale_ref, q_ref, k_ref, raw_ref, logp_ref):
-    layers, held = slots_of(placement, lax.axis_index("section"))
-    row, col = masks()
     for slot in range(SLOTS):
 
         @pl.when(slot < held)
         def _():
-            key = k_ref[0, slot]
-            for head in range(HEADS):
-                query = q_ref[0, slot, :, head * HEAD_WIDTH : (head + 1) * HEAD_WIDTH]
-                scale = scale_ref[head, layers[slot]]
-                if head % 2:
-                    raw = dot(key, query, 1, 1) * INVERSE
-                    logp_ref[slot, head] = log_softmax(scale * raw, row <= col, 0)
-                else:
-                    raw = dot(query, key, 1, 1) * INVERSE
-                    logp_ref[slot, head] = log_softmax(scale * raw, col <= row, 1)
-                raw_ref[slot, head] = raw
-
-
-def student_kernel(
-    pairing, placement, scale_ref, arrived_ref, swapped_ref, raw_ref, logp_ref, sums_ref, grad_ref
-):
-    me = lax.axis_index("section")
-    layers, held = slots_of(placement, me)
-    row, col = masks()
-    lane = lax.broadcasted_iota(jnp.int32, (1, TOKENS), 1)
-    sums_ref[...] = jnp.zeros_like(sums_ref)
-    for slot in range(SLOTS):
-
-        @pl.when(slot < held)
-        def _():
-            layer = layers[slot]
-            source = pairing[layer]
-            chip, direct = source // 2, lax.rem(source, 2) == lax.rem(me, 2)
-
-            def packed(at, rows):
-                near = arrived_ref[chip, at : at + rows, :]
-                far = swapped_ref[chip, at : at + rows, :]
-                return jnp.where(direct, near, far)
-
-            divergence = jnp.zeros((TOKENS, TOKENS), jnp.float32)
-            found = jnp.zeros((1, TOKENS), jnp.float32)
-            for head in range(HEADS):
-                pair = head // 2
-                scale = scale_ref[head, layer]
-                square = packed(pair * TOKENS, TOKENS)
-                if head % 2:
-                    diagonal = packed(2 * TOKENS + pair, 1)
-                    visible = row <= col
-                    target_logp = jnp.where(row == col, diagonal, square)
-                else:
-                    visible = col <= row
-                    target_logp = square
-                target_logp = jnp.where(visible, target_logp, HIDDEN)
-                student_logp = logp_ref[slot, head]
-                target = jnp.exp(target_logp)
-                divergence += jnp.where(
-                    visible, target * (target_logp - student_logp), 0.0
-                )
-                difference = jnp.where(visible, jnp.exp(student_logp) - target, 0.0)
-                found = jnp.where(
-                    lane == SCALE_LANE + LAYERS * head + layer,
-                    jnp.sum(difference * raw_ref[slot, head]),
-                    found,
-                )
-                grad_ref[slot, head] = (difference * (scale * INVERSE)).astype(jnp.bfloat16)
-            sums_ref[...] += jnp.where(lane == layer, jnp.sum(divergence), found)
-
-
-def gradient_kernel(placement, grad_ref, q_ref, k_ref, q_out, k_out):
-    _, held = slots_of(placement, lax.axis_index("section"))
-    for slot in range(SLOTS):
-
-        @pl.when(slot < held)
-        def _():
+            direct = lax.rem(pairing[layers[slot]], 2) == core
             key = k_ref[0, slot]
             total = jnp.zeros((TOKENS, HEAD_WIDTH), jnp.float32)
             for head in range(HEADS):
                 lanes = slice(head * HEAD_WIDTH, (head + 1) * HEAD_WIDTH)
                 query = q_ref[0, slot, :, lanes]
-                grad = grad_ref[slot, head]
+                grad = jnp.where(direct, grad_ref[slot, head], sent_ref[1 - core, slot, head])
                 over = head % 2
                 q_out[0, slot, :, lanes] = dot(grad, key, 1 - over, 0).astype(jnp.bfloat16)
                 total += dot(grad, query, over, 0)
@@ -188,6 +214,7 @@
 
 VMEM = pl.BlockSpec(memory_space=pltpu.VMEM)
 SMEM = pl.BlockSpec(memory_space=pltpu.SMEM)
+SMALL = pltpu.CompilerParams(vmem_limit_bytes=16 * 2**20)
 
 
 def kept(array):
@@ -215,38 +242,48 @@
     arrived = lax.all_to_all(
         packed, "section", 0, 0, tiled=True, axis_index_groups=over_x
     )
-    square = pltpu.VMEM((SLOTS, HEADS, TOKENS, TOKENS), f32)
+    def of_both_cores(array):
+        return lax.all_gather(array, "section", axis_index_groups=of_chip)
+
+    at_once = 2 * SLOTS
+    square = pltpu.VMEM((at_once, HEADS, TOKENS, TOKENS), f32)
     raw, logp = pl.pallas_call(
         scores_kernel,
         out_shape=(square, square),
-        in_specs=[SMEM, SMEM, VMEM, VMEM],
+        in_specs=[SMEM, SMEM, SMEM, VMEM, VMEM],
         out_specs=(VMEM, VMEM),
         cost_estimate=cost(8 * 2 * TOKENS**3, 1_400_000),
+        compiler_params=SMALL,
         name="scores",
-    )(placement, student_scale.T, student_q, student_k)
-    swap = [(s, s ^ 1) for s in range(2 * chips)]
-    swapped = lax.ppermute(arrived, "section", swap)
-
-    sums, grads = pl.pallas_call(
+    )(
+        pairing,
+        placement,
+        student_scale.T,
+        kept(of_both_cores(student_q[0])),
+        kept(of_both_cores(student_k[0])),
+    )
+
+    grad_shape = pltpu.VMEM((SLOTS, HEADS, TOKENS, TOKENS), bf16)
+    sums, grads, sent = pl.pallas_call(
         student_kernel,
-        out_shape=(
-            pltpu.VMEM((1, TOKENS), f32),
-            pltpu.VMEM((SLOTS, HEADS, TOKENS, TOKENS), bf16),
-        ),
-        in_specs=[SMEM, SMEM, SMEM, VMEM, VMEM, VMEM, VMEM],
-        out_specs=(VMEM, VMEM),
+        out_shape=(pltpu.VMEM((1, TOKENS), f32), grad_shape, grad_shape),
+        in_specs=[SMEM, SMEM, SMEM, VMEM, VMEM, VMEM],
+        out_specs=(VMEM, VMEM, VMEM),
         cost_estimate=cost(8 * 2 * TOKENS**3, 1_800_000),
+        compiler_params=SMALL,
         name="student",
-    )(pairing, placement, student_scale.T, *map(kept, (arrived, swapped, raw, logp)))
-
-    sums = lax.all_gather(sums, "section", axis_index_groups=of_chip).sum(axis=0)
+    )(pairing, placement, student_scale.T, *map(kept, (arrived, raw, logp)))
+
+    sums = pl.pallas_call(
+        spread_kernel,
+        out_shape=pltpu.VMEM((members, TOKENS), f32),
+        in_specs=[VMEM],
+        out_specs=VMEM,
+        compiler_params=SMALL,
+        name="spread",
+    )(kept(of_both_cores(sums)))
     rows = lax.all_to_all(
-        jnp.broadcast_to(sums[None], (members, 1, TOKENS)),
-        AXES,
-        0,
-        0,
-        tiled=True,
-        axis_index_groups=groups,
+        sums.reshape(members, 1, TOKENS), AXES, 0, 0, tiled=True, axis_index_groups=groups
     )
     q_grad, k_grad = pl.pallas_call(
         gradient_kernel,
@@ -254,15 +291,14 @@
             jax.ShapeDtypeStruct(student_q.shape, bf16),
             jax.ShapeDtypeStruct(student_k.shape, bf16),
         ),
-        in_specs=[SMEM, VMEM, VMEM, VMEM],
+        in_specs=[SMEM, SMEM, VMEM, VMEM, VMEM, VMEM],
         out_specs=(VMEM, VMEM),
         cost_estimate=cost(16 * 2 * TOKENS**3, 900_000),
+        compiler_params=SMALL,
         name="gradient",
-    )(placement, kept(grads), student_q, student_k)
-
-    both = lax.all_gather(
-        rows.reshape(members, TOKENS), "section", axis_index_groups=of_chip
-    )
+    )(pairing, placement, kept(grads), kept(of_both_cores(sent)), student_q, student_k)
+
+    both = of_both_cores(rows.reshape(members, TOKENS))
     layer_kl, scale_grad = pl.pallas_call(
         final_kernel,
         out_shape=(
@@ -271,6 +307,7 @@
         ),
         in_specs=[VMEM],
         out_specs=(VMEM, VMEM),
+        compiler_params=SMALL,
         name="final",
     )(kept(both))
     return (q_grad, k_grad, layer_kl, scale_grad.T)

time: 48.7 us -> 45.6 us (0.936)
  blocking collectives: 19.8 us -> 25 us
  waiting for transfers between devices: 6.82 us -> 1.7 us
  starting transfers between devices: 13.8 us -> 10.1 us
  Pallas kernels: 6.65 us -> 7.24 us
    all_gather x2 -> x5, blocking collectives: 8.16 us -> 25 us  [of_both_cores(): return lax.all_gather(array, 'section', axis_index_groups=of_chip)]
    all_to_all x1 -> x0, blocking collectives: 11.7 us -> none  [local(): lax.all_to_all(packed, 'section', 0, 0, tiled=True, axis_index_groups=ove...]
    ppermute x1 -> x0, starting transfers between devices: 7.65 us -> none  [local(): swapped = lax.ppermute(arrived, 'section', swap)]
    all_to_all x1 -> x2, waiting for transfers between devices: 6.67 us -> 1.7 us  [the longest x1 1.69 us: local(): lax.all_to_all(sums.reshape(members, 1, TOKENS), AXES, 0, 0, tiled=True,...]
    all_to_all x1 -> x2, starting transfers between devices: 6.1 us -> 10.1 us  [the longest x1 5.08 us: local(): lax.all_to_all(sums.reshape(members, 1, TOKENS), AXES, 0, 0, tiled=True,...]
    pallas_call x1, Pallas kernels: 1.54 us -> 2.35 us  [local(): pl.pallas_call(teacher_kernel, out_shape=pltpu.VMEM((chips, PACKED, TOKEN...]
    unnamed x0 -> x10, local copies, waits for them, and re-layouts: none -> 0.68 us
    pallas_call x1 -> x2, Pallas kernels: 1.04 us -> 1.69 us  [the longest x1 1.09 us: local(): pl.pallas_call(student_kernel, out_shape=(pltpu.VMEM((1, TOKENS), f32), g...]
  transfers between devices with their start and end apart: 2 -> 2, of which waited for: 2 -> 1; matrix products, arithmetic and copies ran while one was open for 0% -> 0% of each run, Pallas kernels for 7% -> 5%
where the time goes in v4:
time: 45.6 us; the launch traced here: 45.3 us
  blocking collectives  25 us (55%)
  starting transfers between devices  10.1 us (22%)
  Pallas kernels  7.24 us (16%)
  waiting for transfers between devices  1.7 us (4%)
  local copies, waits for them, and re-layouts  0.68 us (1%)
  between operations  0.67 us (1%)
    all_gather x5, blocking collectives, of_both_cores(): return lax.all_gather(array, 'section', axis_index_groups=of_chip)  25 us
    all_to_all x1, starting transfers between devices, local(): lax.all_to_all(sums.reshape(members, 1, TOKENS), AXES, 0, 0, tiled=True,...  5.08 us
    all_to_all x1, starting transfers between devices, local(): lax.all_to_all(packed, 'section', 0, 0, tiled=True, axis_index_groups=ove...  4.97 us
    pallas_call x1, Pallas kernels, local(): pl.pallas_call(teacher_kernel, out_shape=pltpu.VMEM((chips, PACKED, TOKEN...  2.35 us
    all_to_all x1, waiting for transfers between devices, local(): lax.all_to_all(sums.reshape(members, 1, TOKENS), AXES, 0, 0, tiled=True,...  1.69 us
    pallas_call x1, Pallas kernels, local(): pl.pallas_call(gradient_kernel, out_shape=(jax.ShapeDtypeStruct(student_q...  1.33 us
    pallas_call x1, Pallas kernels, local(): pl.pallas_call(scores_kernel, out_shape=(square, square), in_specs=[SMEM,...  1.15 us
    pallas_call x1, Pallas kernels, local(): pl.pallas_call(student_kernel, out_shape=(pltpu.VMEM((1, TOKENS), f32), g...  1.09 us
  transfers between devices with their start and end apart: 2, of which 1 were waited for; matrix products, arithmetic and copies ran while one was open for 0% of the time, Pallas kernels for 5%

profile of v4, /device:TPU:1, one launch (start us, length us, event | category | flops | bytes accessed | tf_op | source)
XLA Modules:
  0.0 45.3 jit_solution(13986701763422661773)
XLA Ops:
  0.6 2.4 %teacher.1 = f32[4,264,128]{2,1,0:T(8,128)} custom-call(s32[8]{0:T(128)} %pairing.7, s32[8]{0:T(128)} %placement.7, bf16[1,128,1024]{2,1,0:T(8,128)(2,1)} %q_ref.2, bf16[1,128,128]{2,1,0:T(8,128)(2,1)} %k_ref.2), custom_call_target="tpu_custom_call" | custom-call | flops 33554432 | bytes 400000 | tf_op jit(solution)/shard_map/teacher/pallas_call | solution.py:234
  3.0 0.0 copy-start.1
  3.0 0.0 copy-start
  3.0 5.0 %all-to-all-start = ((f32[4,264,128]{2,1,0:T(8,128)}), f32[4,264,128]{2,1,0:T(8,128)S(1)}, u32[]{:S(2)}, u32[]{:S(2)}) async-start(f32[4,264,128]{2,1,0:T(8,128)} %teacher.1), calls=%async_computation | async-start | bytes 1081344 | tf_op jit(solution)/shard_map/all_to_all | solution.py:242
  8.0 0.0 copy-done.1
  8.0 7.1 %all_gather.22.k_ref = bf16[2,2,128,128]{3,2,1,0:T(8,128)(2,1)S(1)} all-gather(bf16[1,2,128,128]{3,2,1,0:T(8,128)(2,1)S(1)} %copy-done.1), channel_id=1, replica_groups={{0,64},{128,192},{256,320},{384,448},{1,65},{129,193},{257,321},{385,44..., dimensions={0}, use_global_device_ids=true | all-gather | bytes 196608 | tf_op jit(solution)/shard_map/all_gather | solution.py:246
  15.0 0.0 copy-done
  15.0 0.0 copy-start.2
  15.0 2.3 %all_gather.21.q_ref = bf16[2,2,128,512]{3,2,1,0:T(8,128)(2,1)S(1)} all-gather(bf16[1,2,128,512]{3,2,1,0:T(8,128)(2,1)S(1)} %copy-done), channel_id=1, replica_groups={{0,64},{128,192},{256,320},{384,448},{1,65},{129,193},{257,321},{385,44..., dimensions={0}, use_global_device_ids=true | all-gather | bytes 786432 | tf_op jit(solution)/shard_map/all_gather | solution.py:246
  17.3 0.0 copy-start.3
  17.3 0.0 copy-start.4
  17.3 0.0 copy-done.2
  17.4 0.6 %copy-done.3 = s32[8]{0:T(128)S(1)} copy-done((s32[8]{0:T(128)S(1)}, s32[8]{0:T(128)}, u32[]{:S(2)}) %copy-start.3) | copy-done | bytes 56
  18.0 0.0 copy-done.4
  18.0 1.1 %scores.1 = (f32[4,4,128,128]{3,2,1,0:T(8,128)S(1)}, f32[4,4,128,128]{3,2,1,0:T(8,128)S(1)}) custom-call(s32[8]{0:T(128)S(1)} %copy-done.3, s32[8]{0:T(128)S(1)} %copy-done.4, f32[4,8]{1,0:T(4,128)S(1)} %bitcast.10, bf16[2,2,128,512]{3,2,1,0:T(8,128)(2,1)S(1)} %all_gather.21.q_ref, bf16[2,2,128,128]{3,2,1,0:T(8,128)(2,1)S(1)} %all_gather.22.k_ref), custom_call_target="tpu_custom_call" | custom-call | flops 33554432 | bytes 1400000 | tf_op jit(solution)/shard_map/scores/pallas_call | solution.py:250
  19.2 0.0 all-to-all-done.arrived_ref
  19.2 1.1 %student.1 = (f32[1,128]{1,0:T(1,128)S(1)}, bf16[2,4,128,128]{3,2,1,0:T(8,128)(2,1)S(1)}, bf16[2,4,128,128]{3,2,1,0:T(8,128)(2,1)S(1)}) custom-call(s32[8]{0:T(128)S(1)} %copy-done.3, s32[8]{0:T(128)S(1)} %copy-done.4, f32[4,8]{1,0:T(4,128)S(1)} %bitcast.11, f32[4,264,128]{2,1,0:T(8,128)S(1)} %all-to-all-done.arrived_ref, ...), custom_call_target="tpu_custom_call" | custom-call | flops 33554432 | bytes 1800000 | tf_op jit(solution)/shard_map/student/pallas_call | solution.py:267
  20.3 3.6 %all-gather.3.pair_ref = f32[2,1,128]{2,1,0:T(1,128)S(1)} all-gather(f32[1,1,128]{2,1,0:T(1,128)S(1)} %bitcast.12), channel_id=3, replica_groups={{0,64},{128,192},{256,320},{384,448},{1,65},{129,193},{257,321},{385,44..., dimensions={0}, use_global_device_ids=true | all-gather | bytes 1536 | tf_op jit(solution)/shard_map/all_gather | solution.py:246
  23.9 0.6 %spread.1 = f32[32,128]{1,0:T(8,128)} custom-call(f32[2,1,128]{2,1,0:T(1,128)S(1)} %all-gather.3.pair_ref), custom_call_target="tpu_custom_call" | custom-call | tf_op jit(solution)/shard_map/spread/pallas_call | solution.py:277
  24.5 5.1 %all-to-all-start.1 = ((f32[32,1,128]{2,1,0:T(1,128)}), f32[32,1,128]{2,1,0:T(1,128)S(1)}, u32[]{:S(2)}, u32[]{:S(2)}) async-start(f32[32,1,128]{2,1,0:T(1,128)} %bitcast.4), calls=%async_computation.1 | async-start | bytes 32768 | tf_op jit(solution)/shard_map/all_to_all | solution.py:285
  29.6 5.6 %all-gather = bf16[4,4,128,128]{3,2,1,0:T(8,128)(2,1)S(1)} all-gather(bf16[2,4,128,128]{3,2,1,0:T(8,128)(2,1)S(1)} %get-tuple-element.16), channel_id=2, replica_groups={{0,64},{128,192},{256,320},{384,448},{1,65},{129,193},{257,321},{385,44..., dimensions={0}, use_global_device_ids=true | all-gather | bytes 786432 | tf_op jit(solution)/shard_map/all_gather | solution.py:246
  35.2 1.3 %gradient.1 = (bf16[1,2,128,512]{3,2,1,0:T(8,128)(2,1)}, bf16[1,2,128,128]{3,2,1,0:T(8,128)(2,1)}) custom-call(s32[8]{0:T(128)S(1)} %copy-done.3, s32[8]{0:T(128)S(1)} %copy-done.4, bf16[2,4,128,128]{3,2,1,0:T(8,128)(2,1)S(1)} %get-tuple-element.15.grad_ref, bf16[2,2,4,128,128]{4,3,2,1,0:T(8,128)(2,1)S(1)} %bitcast.8, bf16[1,2,128,512]{3,2,1,0:T(8,128)(2,1)S(1)} %copy-done, ...), custom_call_target="tpu_custom_call" | custom-call | flops 67108864 | bytes 900000 | tf_op jit(solution)/shard_map/gradient/pallas_call | solution.py:288
  36.5 1.7 %all-to-all-done.1 = f32[32,1,128]{2,1,0:T(1,128)S(1)} async-done(((f32[32,1,128]{2,1,0:T(1,128)}), f32[32,1,128]{2,1,0:T(1,128)S(1)}, u32[]{:S(2)}, u32[]{:S(2)}) %all-to-all-start.1) | async-done | bytes 16416 | tf_op jit(solution)/shard_map/all_to_all | solution.py:285
  38.2 6.4 %all-gather.2 = f32[64,1,128]{2,1,0:T(1,128)S(1)} all-gather(f32[32,1,128]{2,1,0:T(1,128)S(1)} %all-to-all-done.1), channel_id=4, replica_groups={{0,64},{128,192},{256,320},{384,448},{1,65},{129,193},{257,321},{385,44..., dimensions={0}, use_global_device_ids=true | all-gather | bytes 49152 | tf_op jit(solution)/shard_map/all_gather | solution.py:246
  44.6 0.7 %final.1 = (f32[1,8]{1,0:T(1,128)}, f32[4,8]{1,0:T(4,128)}) custom-call(f32[2,32,128]{2,1,0:T(8,128)S(1)} %bitcast.9), custom_call_target="tpu_custom_call" | custom-call | tf_op jit(solution)/shard_map/final/pallas_call | solution.py:302
Async XLA Ops:
  3.0 5.0 %copy-start.1 = (bf16[1,2,128,128]{3,2,1,0:T(8,128)(2,1)S(1)}, bf16[1,2,128,128]{3,2,1,0:T(8,128)(2,1)}, u32[]{:S(2)}) copy-start(bf16[1,2,128,128]{3,2,1,0:T(8,128)(2,1)} %k_ref.3) | copy-start | bytes 196612
  3.0 12.1 %copy-start = (bf16[1,2,128,512]{3,2,1,0:T(8,128)(2,1)S(1)}, bf16[1,2,128,512]{3,2,1,0:T(8,128)(2,1)}, u32[]{:S(2)}) copy-start(bf16[1,2,128,512]{3,2,1,0:T(8,128)(2,1)} %q_ref.3) | copy-start | bytes 786436
  3.0 16.2 %all-to-all-start = ((f32[4,264,128]{2,1,0:T(8,128)}), f32[4,264,128]{2,1,0:T(8,128)S(1)}, u32[]{:S(2)}, u32[]{:S(2)}) async-start(f32[4,264,128]{2,1,0:T(8,128)} %teacher.1), calls=%async_computation | async-start | bytes 1081344 | tf_op jit(solution)/shard_map/all_to_all | solution.py:242
  15.0 2.3 %copy-start.2 = (f32[8,4]{0,1:T(4,128)S(1)}, f32[8,4]{0,1:T(4,128)}, u32[]{:S(2)}) copy-start(f32[8,4]{0,1:T(4,128)} %param.11) | copy-start | bytes 388
  17.3 0.7 %copy-start.3 = (s32[8]{0:T(128)S(1)}, s32[8]{0:T(128)}, u32[]{:S(2)}) copy-start(s32[8]{0:T(128)} %pairing.7) | copy-start | bytes 100
  17.3 0.7 %copy-start.4 = (s32[8]{0:T(128)S(1)}, s32[8]{0:T(128)}, u32[]{:S(2)}) copy-start(s32[8]{0:T(128)} %placement.7) | copy-start | bytes 100
  24.5 13.7 %all-to-all-start.1 = ((f32[32,1,128]{2,1,0:T(1,128)}), f32[32,1,128]{2,1,0:T(1,128)S(1)}, u32[]{:S(2)}, u32[]{:S(2)}) async-start(f32[32,1,128]{2,1,0:T(1,128)} %bitcast.4), calls=%async_computation.1 | async-start | bytes 32768 | tf_op jit(solution)/shard_map/all_to_all | solution.py:285

commit v5 on v4

--- a/solution.py
+++ b/solution.py
@@ -39,19 +39,34 @@
     return shifted - jnp.log(jnp.sum(jnp.exp(shifted), axis=axis, keepdims=True))
 
 
-def teacher_kernel(pairing, placement, q_ref, k_ref, out_ref):
+def teacher_kernel(
+    pairing, placement, q_hbm, k_hbm, out_ref, q_ref, k_ref, packed, in_sems, out_sems
+):
+    def part(head):
+        lanes = slice(2 * head * HEAD_WIDTH, 2 * (head + 1) * HEAD_WIDTH)
+        return pltpu.make_async_copy(
+            q_hbm.at[0, :, lanes], q_ref.at[head], in_sems.at[head]
+        )
+
+    keys = pltpu.make_async_copy(k_hbm.at[0], k_ref, in_sems.at[HEADS])
+    keys.start()
+    for head in range(HEADS):
+        part(head).start()
+
     me = lax.axis_index("section")
     home = jnp.int32(0)
     for layer in range(LAYERS):
         home = jnp.where(pairing[layer] == me, placement[layer], home)
     chip = home // 2
     row, col = masks()
-    key = k_ref[0]
+    keys.wait()
+    key = k_ref[...]
 
     def target(head, turned):
+        part(head).wait()
         logps = []
-        for twin in (2 * head, 2 * head + 1):
-            query = q_ref[0, :, twin * HEAD_WIDTH : (twin + 1) * HEAD_WIDTH]
+        for twin in range(2):
+            query = q_ref[head, :, twin * HEAD_WIDTH : (twin + 1) * HEAD_WIDTH]
             if turned:
                 scores = dot(key, query, 1, 1) * INVERSE
                 logps.append(log_softmax(scores, row <= col, 0))
@@ -62,15 +77,26 @@
         high = jnp.maximum(one, two)
         return high + jnp.log1p(jnp.exp(-jnp.abs(one - two))) - math.log(2.0)
 
-    for pair in range(HEADS // 2):
+    pairs = HEADS // 2
+    packed[pairs * TOKENS :, :] = jnp.zeros((PACKED - pairs * TOKENS, TOKENS), jnp.float32)
+    started = []
+    for pair in range(pairs):
         plain = target(2 * pair, False)
         turned = target(2 * pair + 1, True)
-        out_ref[chip, pair * TOKENS : (pair + 1) * TOKENS, :] = jnp.where(
-            col <= row, plain, turned
+        packed[pair * TOKENS : (pair + 1) * TOKENS, :] = jnp.where(col <= row, plain, turned)
+        at = pairs * TOKENS + pair
+        packed[at : at + 1, :] = jnp.sum(
+            jnp.where(row == col, turned, 0.0), axis=0, keepdims=True
         )
-        diagonal = jnp.sum(jnp.where(row == col, turned, 0.0), axis=0, keepdims=True)
-        at = 2 * TOKENS + pair
-        out_ref[chip, at : at + 1, :] = diagonal
+        end = (pair + 1) * TOKENS if pair < pairs - 1 else PACKED
+        rows = slice(pair * TOKENS, end)
+        copy = pltpu.make_async_copy(
+            packed.at[rows, :], out_ref.at[chip, rows, :], out_sems.at[pair]
+        )
+        copy.start()
+        started.append(copy)
+    for copy in started:
+        copy.wait()
 
 
 def for_my_layers(pairing, placement, work):
@@ -152,7 +178,8 @@
                 found,
             )
             grads.append((difference * (scale * INVERSE)).astype(jnp.bfloat16))
-        sums_ref[...] += jnp.where(lane == layer, jnp.sum(divergence), found)
+        found = jnp.where(lane == layer, jnp.sum(divergence), found)
+        sums_ref[...] += jnp.broadcast_to(found, sums_ref.shape)
 
         @pl.when(home_core == core)
         def _():
@@ -165,10 +192,6 @@
                 sent_ref[slot, head] = grads[head]
 
     for_my_layers(pairing, placement, work)
-
-
-def spread_kernel(pair_ref, out_ref):
-    out_ref[...] = jnp.broadcast_to(pair_ref[0] + pair_ref[1], out_ref.shape)
 
 
 def gradient_kernel(pairing, placement, grad_ref, sent_ref, q_ref, k_ref, q_out, k_out):
@@ -186,11 +209,11 @@
         @pl.when(slot < held)
         def _():
             direct = lax.rem(pairing[layers[slot]], 2) == core
-            key = k_ref[0, slot]
+            key = k_ref[core, slot]
             total = jnp.zeros((TOKENS, HEAD_WIDTH), jnp.float32)
             for head in range(HEADS):
                 lanes = slice(head * HEAD_WIDTH, (head + 1) * HEAD_WIDTH)
-                query = q_ref[0, slot, :, lanes]
+                query = q_ref[core, slot, :, lanes]
                 grad = jnp.where(direct, grad_ref[slot, head], sent_ref[1 - core, slot, head])
                 over = head % 2
                 q_out[0, slot, :, lanes] = dot(grad, key, 1 - over, 0).astype(jnp.bfloat16)
@@ -213,8 +236,13 @@
 
 
 VMEM = pl.BlockSpec(memory_space=pltpu.VMEM)
+ANY = pl.BlockSpec(memory_space=pl.ANY)
 SMEM = pl.BlockSpec(memory_space=pltpu.SMEM)
 SMALL = pltpu.CompilerParams(vmem_limit_bytes=16 * 2**20)
+
+
+def far(array):
+    return pltpu.with_memory_space_constraint(array, pltpu.HBM)
 
 
 def kept(array):
@@ -231,11 +259,19 @@
     of_chip = [[2 * x, 2 * x + 1] for x in range(chips)]
     members = len(groups[0])
 
+    pairing, placement, scales = map(far, (pairing, placement, student_scale.T))
     packed = pl.pallas_call(
         teacher_kernel,
-        out_shape=pltpu.VMEM((chips, PACKED, TOKENS), f32),
-        in_specs=[SMEM, SMEM, VMEM, VMEM],
-        out_specs=VMEM,
+        out_shape=jax.ShapeDtypeStruct((chips, PACKED, TOKENS), f32),
+        in_specs=[SMEM, SMEM, ANY, ANY],
+        out_specs=ANY,
+        scratch_shapes=[
+            pltpu.VMEM((HEADS, TOKENS, 2 * HEAD_WIDTH), bf16),
+            pltpu.VMEM((TOKENS, HEAD_WIDTH), bf16),
+            pltpu.VMEM((PACKED, TOKENS), f32),
+            pltpu.SemaphoreType.DMA((HEADS + 1,)),
+            pltpu.SemaphoreType.DMA((HEADS // 2,)),
+        ],
         cost_estimate=cost(8 * 2 * TOKENS**3, 400_000),
         name="teacher",
     )(pairing, placement, teacher_q, teacher_k)
@@ -245,6 +281,7 @@
     def of_both_cores(array):
         return lax.all_gather(array, "section", axis_index_groups=of_chip)
 
+    chip_q, chip_k = (kept(of_both_cores(a[0])) for a in (student_q, student_k))
     at_once = 2 * SLOTS
     square = pltpu.VMEM((at_once, HEADS, TOKENS, TOKENS), f32)
     raw, logp = pl.pallas_call(
@@ -258,30 +295,23 @@
     )(
         pairing,
         placement,
-        student_scale.T,
-        kept(of_both_cores(student_q[0])),
-        kept(of_both_cores(student_k[0])),
+        scales,
+        chip_q,
+        chip_k,
     )
 
     grad_shape = pltpu.VMEM((SLOTS, HEADS, TOKENS, TOKENS), bf16)
     sums, grads, sent = pl.pallas_call(
         student_kernel,
-        out_shape=(pltpu.VMEM((1, TOKENS), f32), grad_shape, grad_shape),
+        out_shape=(pltpu.HBM((members, TOKENS), f32), grad_shape, pltpu.HBM(grad_shape.shape, bf16)),
         in_specs=[SMEM, SMEM, SMEM, VMEM, VMEM, VMEM],
         out_specs=(VMEM, VMEM, VMEM),
         cost_estimate=cost(8 * 2 * TOKENS**3, 1_800_000),
         compiler_params=SMALL,
         name="student",
-    )(pairing, placement, student_scale.T, *map(kept, (arrived, raw, logp)))
-
-    sums = pl.pallas_call(
-        spread_kernel,
-        out_shape=pltpu.VMEM((members, TOKENS), f32),
-        in_specs=[VMEM],
-        out_specs=VMEM,
-        compiler_params=SMALL,
-        name="spread",
-    )(kept(of_both_cores(sums)))
+    )(pairing, placement, scales, *map(kept, (arrived, raw, logp)))
+
+    sums = lax.psum(sums, "section", axis_index_groups=of_chip)
     rows = lax.all_to_all(
         sums.reshape(members, 1, TOKENS), AXES, 0, 0, tiled=True, axis_index_groups=groups
     )
@@ -296,7 +326,7 @@
         cost_estimate=cost(16 * 2 * TOKENS**3, 900_000),
         compiler_params=SMALL,
         name="gradient",
-    )(pairing, placement, kept(grads), kept(of_both_cores(sent)), student_q, student_k)
+    )(pairing, placement, kept(grads), kept(of_both_cores(sent)), chip_q, chip_k)
 
     both = of_both_cores(rows.reshape(members, TOKENS))
     layer_kl, scale_grad = pl.pallas_call(

time: 45.6 us -> 49.7 us (1.090)
  blocking collectives: 25 us -> 29 us
  Pallas kernels: 7.24 us -> 9.18 us
  starting transfers between devices: 10.1 us -> 9.14 us
  local copies, waits for them, and re-layouts: 0.68 us -> 0.01 us
    psum x0 -> x1, blocking collectives: none -> 7.82 us  [local(): sums = lax.psum(sums, 'section', axis_index_groups=of_chip)]
    all_gather x5 -> x4, blocking collectives: 25 us -> 21.2 us  [of_both_cores(): return lax.all_gather(array, 'section', axis_index_groups=of_chip)]
    pallas_call x3 -> x2, Pallas kernels: 4.04 us -> 5.49 us  [the longest x1 3.56 us: local(): pl.pallas_call(teacher_kernel, out_shape=jax.ShapeDtypeStruct((chips, PAC...]
    all_to_all x1, starting transfers between devices: 5.08 us -> 4.15 us  [local(): lax.all_to_all(sums.reshape(members, 1, TOKENS), AXES, 0, 0, tiled=True,...]
    unnamed x10 -> x4, local copies, waits for them, and re-layouts: 0.68 us -> 0.01 us
  transfers between devices with their start and end apart: 2 -> 2, of which waited for: 1 -> 1; matrix products, arithmetic and copies ran while one was open for 0% -> 0% of each run, Pallas kernels for 5% -> 6%
where the time goes in v5:
time: 49.7 us; the launch traced here: 49.3 us
  blocking collectives  29 us (58%)
  Pallas kernels  9.18 us (18%)
  starting transfers between devices  9.14 us (18%)
  waiting for transfers between devices  1.26 us (3%)
  between operations  0.68 us (1%)
    all_gather x4, blocking collectives, of_both_cores(): return lax.all_gather(array, 'section', axis_index_groups=of_chip)  21.2 us
    psum x1, blocking collectives, local(): sums = lax.psum(sums, 'section', axis_index_groups=of_chip)  7.82 us
    all_to_all x1, starting transfers between devices, local(): lax.all_to_all(packed, 'section', 0, 0, tiled=True, axis_index_groups=ove...  4.99 us
    all_to_all x1, starting transfers between devices, local(): lax.all_to_all(sums.reshape(members, 1, TOKENS), AXES, 0, 0, tiled=True,...  4.15 us
    pallas_call x1, Pallas kernels, local(): pl.pallas_call(teacher_kernel, out_shape=jax.ShapeDtypeStruct((chips, PAC...  3.56 us
    pallas_call x1, Pallas kernels, local(): pl.pallas_call(student_kernel, out_shape=(pltpu.HBM((members, TOKENS), f3...  1.93 us
    pallas_call x1, Pallas kernels, local(): pl.pallas_call(gradient_kernel, out_shape=(jax.ShapeDtypeStruct(student_q...  1.69 us
    pallas_call x1, Pallas kernels, local(): pl.pallas_call(scores_kernel, out_shape=(square, square), in_specs=[SMEM,...  1.28 us
  transfers between devices with their start and end apart: 2, of which 1 were waited for; matrix products, arithmetic and copies ran while one was open for 0% of the time, Pallas kernels for 6%

profile of v5, /device:TPU:1, one launch (start us, length us, event | category | flops | bytes accessed | tf_op | source)
XLA Modules:
  0.0 49.3 jit_solution(13547270000124076638)
XLA Ops:
  0.6 3.6 %teacher.1 = f32[4,264,128]{2,1,0:T(8,128)} custom-call(s32[8]{0:T(128)} %pairing.7, s32[8]{0:T(128)} %placement.7, bf16[1,128,1024]{2,1,0:T(8,128)(2,1)} %q_hbm.1, bf16[1,128,128]{2,1,0:T(8,128)(2,1)} %k_hbm.1), custom_call_target="tpu_custom_call" | custom-call | flops 33554432 | bytes 400000 | tf_op jit(solution)/shard_map/teacher/pallas_call | solution.py:263
  4.2 0.0 copy-start.1
  4.2 0.0 copy-start
  4.2 5.0 %all-to-all-start = ((f32[4,264,128]{2,1,0:T(8,128)}), f32[4,264,128]{2,1,0:T(8,128)S(1)}, u32[]{:S(2)}, u32[]{:S(2)}) async-start(f32[4,264,128]{2,1,0:T(8,128)} %teacher.1), calls=%async_computation | async-start | bytes 1081344 | tf_op jit(solution)/shard_map/all_to_all | solution.py:278
  9.2 0.0 copy-done.1
  9.2 7.1 %all_gather.16.k_ref = bf16[2,2,128,128]{3,2,1,0:T(8,128)(2,1)S(1)} all-gather(bf16[1,2,128,128]{3,2,1,0:T(8,128)(2,1)S(1)} %copy-done.1), channel_id=1, replica_groups={{0,64},{128,192},{256,320},{384,448},{1,65},{129,193},{257,321},{385,44..., dimensions={0}, use_global_device_ids=true | all-gather | bytes 196608 | tf_op jit(solution)/shard_map/all_gather | solution.py:282
  16.3 0.0 copy-done
  16.3 2.2 %all_gather.15.q_ref = bf16[2,2,128,512]{3,2,1,0:T(8,128)(2,1)S(1)} all-gather(bf16[1,2,128,512]{3,2,1,0:T(8,128)(2,1)S(1)} %copy-done), channel_id=1, replica_groups={{0,64},{128,192},{256,320},{384,448},{1,65},{129,193},{257,321},{385,44..., dimensions={0}, use_global_device_ids=true | all-gather | bytes 786432 | tf_op jit(solution)/shard_map/all_gather | solution.py:282
  18.5 1.3 %scores.1 = (f32[4,4,128,128]{3,2,1,0:T(8,128)S(1)}, f32[4,4,128,128]{3,2,1,0:T(8,128)S(1)}) custom-call(s32[8]{0:T(128)} %pairing.7, s32[8]{0:T(128)} %placement.7, f32[4,8]{1,0:T(4,128)} %bitcast.9, bf16[2,2,128,512]{3,2,1,0:T(8,128)(2,1)S(1)} %all_gather.15.q_ref, bf16[2,2,128,128]{3,2,1,0:T(8,128)(2,1)S(1)} %all_gather.16.k_ref), custom_call_target="tpu_custom_call" | custom-call | flops 33554432 | bytes 1400000 | tf_op jit(solution)/shard_map/scores/pallas_call | solution.py:287
  19.7 0.0 all-to-all-done.arrived_ref
  19.8 1.9 %student.1 = (f32[32,128]{1,0:T(8,128)}, bf16[2,4,128,128]{3,2,1,0:T(8,128)(2,1)S(1)}, bf16[2,4,128,128]{3,2,1,0:T(8,128)(2,1)}) custom-call(s32[8]{0:T(128)} %pairing.7, s32[8]{0:T(128)} %placement.7, f32[4,8]{1,0:T(4,128)} %bitcast.10, f32[4,264,128]{2,1,0:T(8,128)S(1)} %all-to-all-done.arrived_ref, f32[4,4,128,128]{3,2,1,0:T(8,128)S(1)} %get-tuple-element.13.raw_ref, ...), custom_call_target="tpu_custom_call" | custom-call | flops 33554432 | bytes 1800000 | tf_op jit(solution)/shard_map/student/pallas_call | solution.py:304
  21.7 7.8 %psum.7 = f32[32,1,128]{2,0,1:T(8,128)} all-reduce(f32[32,1,128]{2,0,1:T(8,128)} %bitcast.8), channel_id=1, replica_groups={{0,64},{128,192},{256,320},{384,448},{1,65},{129,193},{257,321},{385,44..., use_global_device_ids=true, to_apply=%region_0.0 | all-reduce | flops 4096 | bytes 32768 | tf_op jit(solution)/shard_map/psum | solution.py:314
  29.5 4.2 %all-to-all-start.1 = ((f32[32,1,128]{2,1,0:T(1,128)}), f32[32,1,128]{2,1,0:T(1,128)S(1)}, u32[]{:S(2)}, u32[]{:S(2)}) async-start(f32[32,1,128]{2,1,0:T(1,128)} %bitcast.3), calls=%async_computation.1 | async-start | bytes 32768 | tf_op jit(solution)/shard_map/all_to_all | solution.py:315
  33.7 5.7 %all-gather = bf16[4,4,128,128]{3,2,1,0:T(8,128)(2,1)S(1)} all-gather(bf16[2,4,128,128]{3,2,1,0:T(8,128)(2,1)} %get-tuple-element.16), channel_id=2, replica_groups={{0,64},{128,192},{256,320},{384,448},{1,65},{129,193},{257,321},{385,44..., dimensions={0}, use_global_device_ids=true | all-gather | bytes 786432 | tf_op jit(solution)/shard_map/all_gather | solution.py:282
  39.4 1.7 %gradient.1 = (bf16[1,2,128,512]{3,2,1,0:T(8,128)(2,1)}, bf16[1,2,128,128]{3,2,1,0:T(8,128)(2,1)}) custom-call(s32[8]{0:T(128)} %pairing.7, s32[8]{0:T(128)} %placement.7, bf16[2,4,128,128]{3,2,1,0:T(8,128)(2,1)S(1)} %get-tuple-element.15.grad_ref, bf16[2,2,4,128,128]{4,3,2,1,0:T(8,128)(2,1)S(1)} %bitcast.6, bf16[2,2,128,512]{3,2,1,0:T(8,128)(2,1)S(1)} %all_gather.15.q_ref, ...), custom_call_target="tpu_custom_call" | custom-call | flops 67108864 | bytes 900000 | tf_op jit(solution)/shard_map/gradient/pallas_call | solution.py:318
  41.0 1.3 %all-to-all-done.1 = f32[32,1,128]{2,1,0:T(1,128)S(1)} async-done(((f32[32,1,128]{2,1,0:T(1,128)}), f32[32,1,128]{2,1,0:T(1,128)S(1)}, u32[]{:S(2)}, u32[]{:S(2)}) %all-to-all-start.1) | async-done | bytes 16416 | tf_op jit(solution)/shard_map/all_to_all | solution.py:315
  42.3 6.3 %all-gather.1 = f32[64,1,128]{2,1,0:T(1,128)S(1)} all-gather(f32[32,1,128]{2,1,0:T(1,128)S(1)} %all-to-all-done.1), channel_id=3, replica_groups={{0,64},{128,192},{256,320},{384,448},{1,65},{129,193},{257,321},{385,44..., dimensions={0}, use_global_device_ids=true | all-gather | bytes 49152 | tf_op jit(solution)/shard_map/all_gather | solution.py:282
  48.6 0.7 %final.1 = (f32[1,8]{1,0:T(1,128)}, f32[4,8]{1,0:T(4,128)}) custom-call(f32[2,32,128]{2,1,0:T(8,128)S(1)} %bitcast.7), custom_call_target="tpu_custom_call" | custom-call | tf_op jit(solution)/shard_map/final/pallas_call | solution.py:332
Async XLA Ops:
  4.2 5.0 %copy-start.1 = (bf16[1,2,128,128]{3,2,1,0:T(8,128)(2,1)S(1)}, bf16[1,2,128,128]{3,2,1,0:T(8,128)(2,1)}, u32[]{:S(2)}) copy-start(bf16[1,2,128,128]{3,2,1,0:T(8,128)(2,1)} %param.10) | copy-start | bytes 196612
  4.2 12.1 %copy-start = (bf16[1,2,128,512]{3,2,1,0:T(8,128)(2,1)S(1)}, bf16[1,2,128,512]{3,2,1,0:T(8,128)(2,1)}, u32[]{:S(2)}) copy-start(bf16[1,2,128,512]{3,2,1,0:T(8,128)(2,1)} %param.9) | copy-start | bytes 786436
  4.2 15.5 %all-to-all-start = ((f32[4,264,128]{2,1,0:T(8,128)}), f32[4,264,128]{2,1,0:T(8,128)S(1)}, u32[]{:S(2)}, u32[]{:S(2)}) async-start(f32[4,264,128]{2,1,0:T(8,128)} %teacher.1), calls=%async_computation | async-start | bytes 1081344 | tf_op jit(solution)/shard_map/all_to_all | solution.py:278
  29.5 12.8 %all-to-all-start.1 = ((f32[32,1,128]{2,1,0:T(1,128)}), f32[32,1,128]{2,1,0:T(1,128)S(1)}, u32[]{:S(2)}, u32[]{:S(2)}) async-start(f32[32,1,128]{2,1,0:T(1,128)} %bitcast.3), calls=%async_computation.1 | async-start | bytes 32768 | tf_op jit(solution)/shard_map/all_to_all | solution.py:315

commit v6 on v4

v6 whole, which is shorter than its diff:
```python
import functools
import math

import jax
import jax.numpy as jnp
from jax import lax
from jax.experimental import pallas as pl
from jax.experimental.pallas import tpu as pltpu
from jax.sharding import PartitionSpec as P

STUDENT_HEADS = 32
HEAD_WIDTH = 128
TOKENS = 128
LAYERS = 8
SLOTS = 2
HEADS = 4
PACKED = HEADS // 2 * TOKENS + 8
SCALE_LANE = 32
PAIRS = HEADS // 2
TAIL = 16
SLOT_ROWS = PAIRS * TOKENS + TAIL
SENT = SLOTS * SLOT_ROWS
INVERSE = 1.0 / math.sqrt(HEAD_WIDTH)
HIDDEN = -1e30
AXES = ("section", "head", "dp")


def dot(a, b, over_a, over_b):
    return lax.dot_general(
        a, b, (((over_a,), (over_b,)), ((), ())), preferred_element_type=jnp.float32
    )


def masks():
    row = lax.broadcasted_iota(jnp.int32, (TOKENS, TOKENS), 0)
    col = lax.broadcasted_iota(jnp.int32, (TOKENS, TOKENS), 1)
    return row, col


def log_softmax(scores, visible, axis):
    scores = jnp.where(visible, scores, HIDDEN)
    shifted = scores - jnp.max(scores, axis=axis, keepdims=True)
    return shifted - jnp.log(jnp.sum(jnp.exp(shifted), axis=axis, keepdims=True))


def teacher_kernel(
    pairing, placement, scale_ref, q_ref, k_ref, out_ref, table_ref, scale_out, packed, sems
):
    me = lax.axis_index("section")
    home = jnp.int32(0)
    for layer in range(LAYERS):
        home = jnp.where(pairing[layer] == me, placement[layer], home)
    chip = home // 2
    row, col = masks()
    key = k_ref[0]

    scale_out[...] = scale_ref[...]
    at_row = lax.broadcasted_iota(jnp.int32, (8, TOKENS), 0)
    at_lane = lax.broadcasted_iota(jnp.int32, (8, TOKENS), 1)
    table = jnp.zeros((8, TOKENS), jnp.int32)
    for layer in range(LAYERS):
        entry = jnp.where(at_row == 0, pairing[layer], placement[layer])
        table = jnp.where(at_lane == layer, entry, table)
    table_ref[...] = table

    def target(head, turned):
        logps = []
        for twin in (2 * head, 2 * head + 1):
            query = q_ref[0, :, twin * HEAD_WIDTH : (twin + 1) * HEAD_WIDTH]
            if turned:
                scores = dot(key, query, 1, 1) * INVERSE
                logps.append(log_softmax(scores, row <= col, 0))
            else:
                scores = dot(query, key, 1, 1) * INVERSE
                logps.append(log_softmax(scores, col <= row, 1))
        one, two = logps
        high = jnp.maximum(one, two)
        return high + jnp.log1p(jnp.exp(-jnp.abs(one - two))) - math.log(2.0)

    packed[PAIRS * TOKENS :, :] = jnp.zeros((PACKED - PAIRS * TOKENS, TOKENS), jnp.float32)
    started = []
    for pair in range(PAIRS):
        plain = target(2 * pair, False)
        turned = target(2 * pair + 1, True)
        packed[pair * TOKENS : (pair + 1) * TOKENS, :] = jnp.where(col <= row, plain, turned)
        at = PAIRS * TOKENS + pair
        packed[at : at + 1, :] = jnp.sum(
            jnp.where(row == col, turned, 0.0), axis=0, keepdims=True
        )
        end = (pair + 1) * TOKENS if pair < PAIRS - 1 else PACKED
        rows = slice(pair * TOKENS, end)
        copy = pltpu.make_async_copy(
            packed.at[rows, :], out_ref.at[chip, rows, :], sems.at[pair]
        )
        copy.start()
        started.append(copy)
    for copy in started:
        copy.wait()


def for_my_layers(table, work):
    me = lax.axis_index("section")
    chip, core = me // 2, lax.rem(me, 2)

    def step(layer, carry):
        slots, rank = carry[:2], carry[2]
        source, home = table[0, layer], table[1, layer]
        home_core = lax.rem(home, 2)
        here = home // 2 == chip
        mine = here & (lax.rem(source, 2) == core)
        slot = jnp.where(home_core == 0, slots[0], slots[1])

        @pl.when(mine)
        def _():
            work(layer, source // 2, home_core, slot, rank)

        return (
            slots[0] + (here & (home_core == 0)).astype(jnp.int32),
            slots[1] + (here & (home_core == 1)).astype(jnp.int32),
            rank + mine.astype(jnp.int32),
        )

    lax.fori_loop(0, LAYERS, step, (jnp.int32(0),) * 3)


def pack(ref, rank, pair, plain, turned):
    row, col = masks()
    ref[rank, pair * TOKENS : (pair + 1) * TOKENS, :] = jnp.where(col <= row, plain, turned)
    at = PAIRS * TOKENS + pair
    ref[rank, at : at + 1, :] = jnp.sum(
        jnp.where(row == col, turned, 0.0), axis=0, keepdims=True
    )


def scores_kernel(table, scale_ref, q_ref, k_ref, raw_ref, logp_ref):
    row, col = masks()

    def work(layer, source_chip, home_core, slot, rank):
        key = k_ref[home_core, slot]

        def query(head):
            return q_ref[home_core, slot, :, head * HEAD_WIDTH : (head + 1) * HEAD_WIDTH]

        empty = jnp.zeros((PACKED - PAIRS * TOKENS, TOKENS), jnp.float32)
        raw_ref[rank, PAIRS * TOKENS :, :] = empty
        logp_ref[rank, PAIRS * TOKENS :, :] = empty
        for pair in range(PAIRS):
            plain = dot(query(2 * pair), key, 1, 1) * INVERSE
            turned = dot(key, query(2 * pair + 1), 1, 1) * INVERSE
            pack(raw_ref, rank, pair, plain, turned)
            plain = log_softmax(scale_ref[2 * pair, layer] * plain, col <= row, 1)
            turned = log_softmax(scale_ref[2 * pair + 1, layer] * turned, row <= col, 0)
            pack(logp_ref, rank, pair, plain, turned)

    for_my_layers(table, work)


def student_kernel(table, scale_ref, arrived_ref, raw_ref, logp_ref, grad_ref, sent_ref, sums_ref):
    core = lax.rem(lax.axis_index("section"), 2)
    row, col = masks()
    lower = col <= row
    place = lax.broadcasted_iota(jnp.int32, (8, TOKENS), 0)
    lane = lax.broadcasted_iota(jnp.int32, (8, TOKENS), 1)
    tail_row = lax.broadcasted_iota(jnp.int32, (TAIL, TOKENS), 0)
    sums_ref[...] = jnp.zeros_like(sums_ref)

    def work(layer, source_chip, home_core, slot, rank):
        def terms(rows):
            target_logp = arrived_ref[source_chip, rows, :]
            student_logp = logp_ref[rank, rows, :]
            target = jnp.exp(target_logp)
            difference = jnp.exp(student_logp) - target
            return (
                jnp.sum(target * (target_logp - student_logp), axis=0, keepdims=True),
                difference,
                difference * raw_ref[rank, rows, :],
            )

        last, last_difference, last_moved = terms(slice(PAIRS * TOKENS, PACKED))
        found = jnp.zeros((8, TOKENS), jnp.float32)
        divergence = last
        tail = jnp.zeros((TAIL, TOKENS), jnp.float32)
        pieces = []
        for pair in range(PAIRS):
            one, difference, moved = terms(slice(pair * TOKENS, (pair + 1) * TOKENS))
            divergence += one
            first = scale_ref[2 * pair, layer] * INVERSE
            second = scale_ref[2 * pair + 1, layer] * INVERSE
            pieces.append(difference * jnp.where(lower, first, second))
            tail = jnp.where(tail_row == pair, last_difference[pair : pair + 1] * second, tail)
            of_first = jnp.sum(jnp.where(lower, moved, 0.0), axis=0, keepdims=True)
            of_second = jnp.sum(jnp.where(lower, 0.0, moved), axis=0, keepdims=True)
            of_second += last_moved[pair : pair + 1]
            found = jnp.where(place == 1 + 2 * pair, of_first, found)
            found = jnp.where(place == 2 + 2 * pair, of_second, found)
        found = jnp.where(place == 0, divergence, found)
        found = jnp.sum(found, axis=1, keepdims=True)
        goes_to = jnp.where(place == 0, layer, SCALE_LANE + LAYERS * (place - 1) + layer)
        found = jnp.where((lane == goes_to) & (place <= HEADS), found, 0.0)
        sums_ref[...] += jnp.sum(found, axis=0, keepdims=True)
        pieces.append(tail)

        def put(ref, at):
            for n, piece in enumerate(pieces):
                to = pl.multiple_of(at + n * TOKENS, TAIL)
                ref[pl.ds(to, piece.shape[0]), :] = piece.astype(jnp.bfloat16)

        @pl.when(home_core == core)
        def _():
            put(grad_ref, slot * SLOT_ROWS)

        @pl.when(home_core != core)
        def _():
            put(sent_ref, slot * SLOT_ROWS)

    for_my_layers(table, work)
    left, tile = sums_ref[...], jnp.zeros((TAIL, TOKENS), jnp.float32)
    for term in range(3):
        part = left.astype(jnp.bfloat16).astype(jnp.float32)
        tile = jnp.where(tail_row == term, part, tile)
        left -= part
    sent_ref[SENT:, :] = tile.astype(jnp.bfloat16)


def spread_kernel(pair_ref, out_ref):
    terms = pair_ref[:, SENT:, :].astype(jnp.float32)
    total = jnp.zeros((1, TOKENS), jnp.float32)
    for core in range(2):
        total += (terms[core, 0:1] + terms[core, 1:2]) + terms[core, 2:3]
    out_ref[...] = jnp.broadcast_to(total, out_ref.shape)


def gradient_kernel(table, grad_ref, sent_ref, q_ref, k_ref, q_out, k_out):
    me = lax.axis_index("section")
    core = lax.rem(me, 2)
    row, col = masks()
    held, layers = jnp.int32(0), [jnp.int32(0)] * SLOTS
    for layer in range(LAYERS):
        here = table[1, layer] == me
        layers = [
            jnp.where(here & (held == slot), layer, had) for slot, had in enumerate(layers)
        ]
        held += here.astype(jnp.int32)
    for slot in range(SLOTS):

        @pl.when(slot < held)
        def _():
            direct = lax.rem(table[0, layers[slot]], 2) == core
            key = k_ref[core, slot]
            total = jnp.zeros((TOKENS, HEAD_WIDTH), jnp.float32)

            def rows(at, count):
                at = slot * SLOT_ROWS + at
                near = grad_ref[at : at + count, :].astype(jnp.float32)
                other = sent_ref[1 - core, at : at + count, :].astype(jnp.float32)
                return jnp.where(direct, near, other)

            tail = rows(PAIRS * TOKENS, TAIL)
            for head in range(HEADS):
                pair, over = head // 2, head % 2
                square = rows(pair * TOKENS, TOKENS)
                if over:
                    diagonal = jnp.where(row == col, tail[pair : pair + 1], 0.0)
                    grad = jnp.where(row < col, square, diagonal)
                else:
                    grad = jnp.where(col <= row, square, 0.0)
                grad = grad.astype(jnp.bfloat16)
                lanes = slice(head * HEAD_WIDTH, (head + 1) * HEAD_WIDTH)
                query = q_ref[core, slot, :, lanes]
                q_out[0, slot, :, lanes] = dot(grad, key, 1 - over, 0).astype(jnp.bfloat16)
                total += dot(grad, query, over, 0)
            k_out[0, slot] = total.astype(jnp.bfloat16)

        @pl.when(slot >= held)
        def _():
            q_out[0, slot] = jnp.zeros(q_out.shape[2:], jnp.bfloat16)
            k_out[0, slot] = jnp.zeros(k_out.shape[2:], jnp.bfloat16)


def final_kernel(rows_ref, kl_ref, scale_ref):
    divergence = jnp.sum(rows_ref[0], axis=0, keepdims=True)
    kl_ref[...] = divergence[:, :LAYERS] / (STUDENT_HEADS * TOKENS)
    terms = jnp.sum(rows_ref[1], axis=0, keepdims=True)
    scale_ref[...] = jnp.concatenate(
        [terms[:, SCALE_LANE + LAYERS * h : SCALE_LANE + LAYERS * (h + 1)] for h in range(HEADS)], axis=0
    )


VMEM = pl.BlockSpec(memory_space=pltpu.VMEM)
ANY = pl.BlockSpec(memory_space=pl.ANY)
SMEM = pl.BlockSpec(memory_space=pltpu.SMEM)
SMALL = pltpu.CompilerParams(vmem_limit_bytes=16 * 2**20)


def kept(array):
    return pltpu.with_memory_space_constraint(array, pltpu.VMEM)


def cost(flops, moved):
    return pl.CostEstimate(flops=flops, bytes_accessed=moved, transcendentals=0)


def local(chips, groups, teacher_q, teacher_k, student_q, student_k, student_scale, pairing, placement):
    f32, bf16 = jnp.float32, jnp.bfloat16
    over_x = [[2 * x + core for x in range(chips)] for core in range(2)]
    of_chip = [[2 * x, 2 * x + 1] for x in range(chips)]
    members = len(groups[0])

    packed, table, scales = pl.pallas_call(
        teacher_kernel,
        out_shape=(
            jax.ShapeDtypeStruct((chips, PACKED, TOKENS), f32),
            pltpu.VMEM((8, TOKENS), jnp.int32),
            pltpu.VMEM((HEADS, LAYERS), f32),
        ),
        in_specs=[SMEM, SMEM, VMEM, VMEM, VMEM],
        out_specs=(ANY, VMEM, VMEM),
        scratch_shapes=[
            pltpu.VMEM((PACKED, TOKENS), f32),
            pltpu.SemaphoreType.DMA((PAIRS,)),
        ],
        cost_estimate=cost(8 * 2 * TOKENS**3, 400_000),
        name="teacher",
    )(pairing, placement, student_scale.T, teacher_q, teacher_k)
    table, scales = kept(table), kept(scales)
    arrived = lax.all_to_all(
        packed, "section", 0, 0, tiled=True, axis_index_groups=over_x
    )
    def of_both_cores(array):
        return lax.all_gather(array, "section", axis_index_groups=of_chip)

    chip_q, chip_k = (kept(of_both_cores(a[0])) for a in (student_q, student_k))
    at_once = 2 * SLOTS
    squares = pltpu.VMEM((at_once, PACKED, TOKENS), f32)
    raw, logp = pl.pallas_call(
        scores_kernel,
        out_shape=(squares, squares),
        in_specs=[SMEM, SMEM, VMEM, VMEM],
        out_specs=(VMEM, VMEM),
        cost_estimate=cost(8 * 2 * TOKENS**3, 1_400_000),
        compiler_params=SMALL,
        name="scores",
    )(table, scales, chip_q, chip_k)

    grads, sent = pl.pallas_call(
        student_kernel,
        out_shape=(
            pltpu.VMEM((SENT, TOKENS), bf16),
            pltpu.VMEM((SENT + TAIL, TOKENS), bf16),
        ),
        in_specs=[SMEM, SMEM, VMEM, VMEM, VMEM],
        out_specs=(VMEM, VMEM),
        scratch_shapes=[pltpu.VMEM((1, TOKENS), f32)],
        cost_estimate=cost(8 * 2 * TOKENS**3, 1_800_000),
        compiler_params=SMALL,
        name="student",
    )(table, scales, *map(kept, (arrived, raw, logp)))

    chip_sent = kept(of_both_cores(sent))
    sums = pl.pallas_call(
        spread_kernel,
        out_shape=jax.ShapeDtypeStruct((members, TOKENS), f32),
        in_specs=[VMEM],
        out_specs=VMEM,
        compiler_params=SMALL,
        name="spread",
    )(chip_sent)
    rows = lax.all_to_all(
        sums.reshape(members, 1, TOKENS), AXES, 0, 0, tiled=True, axis_index_groups=groups
    )
    q_grad, k_grad = pl.pallas_call(
        gradient_kernel,
        out_shape=(
            jax.ShapeDtypeStruct(student_q.shape, bf16),
            jax.ShapeDtypeStruct(student_k.shape, bf16),
        ),
        in_specs=[SMEM, VMEM, VMEM, VMEM, VMEM],
        out_specs=(VMEM, VMEM),
        cost_estimate=cost(16 * 2 * TOKENS**3, 900_000),
        compiler_params=SMALL,
        name="gradient",
    )(table, kept(grads), chip_sent, chip_q, chip_k)

    both = of_both_cores(rows.reshape(members, TOKENS))
    layer_kl, scale_grad = pl.pallas_call(
        final_kernel,
        out_shape=(
            jax.ShapeDtypeStruct((1, LAYERS), f32),
            jax.ShapeDtypeStruct((HEADS, LAYERS), f32),
        ),
        in_specs=[VMEM],
        out_specs=(VMEM, VMEM),
        compiler_params=SMALL,
        name="final",
    )(kept(both))
    return (q_grad, k_grad, layer_kl, scale_grad.T)


def reduction_groups(sections, heads, replicas):
    def flat(section, head, replica):
        return (section * heads + head) * replicas + replica

    chips = range(sections // 2)
    first = [
        [flat(2 * x, h, d) for x in chips for h in range(heads)] for d in range(replicas)
    ]
    second = [
        [flat(2 * x + 1, h, d) for x in chips for d in range(replicas)] for h in range(heads)
    ]
    return first + second


def solution(mesh):
    sections, heads, replicas = (mesh.shape[a] for a in AXES)
    return jax.shard_map(
        functools.partial(local, sections // 2, reduction_groups(sections, heads, replicas)),
        mesh=mesh,
        in_specs=(
            P("section", "dp", "head"),
            P("section", "dp", "head"),
            P("section", None, "dp", "head"),
            P("section", None, "dp", "head"),
            P(None, "head"),
            P(),
            P(),
        ),
        out_specs=(
            P("section", None, "dp", "head"),
            P("section", None, "dp", "head"),
            P("dp", None),
            P(None, "head"),
        ),
        check_vma=False,
    )
```

time: 45.6 us -> 45.5 us (level)
  waiting for transfers between devices: 1.7 us -> 7.25 us
  blocking collectives: 25 us -> 20.5 us
  local copies, waits for them, and re-layouts: 0.68 us -> 0.01 us
  starting transfers between devices: 10.1 us -> 9.63 us
    all_to_all x1, waiting for transfers between devices: 1.69 us -> 7.24 us  [local(): lax.all_to_all(sums.reshape(members, 1, TOKENS), AXES, 0, 0, tiled=True,...]
    all_gather x5 -> x4, blocking collectives: 25 us -> 20.5 us  [of_both_cores(): return lax.all_gather(array, 'section', axis_index_groups=of_chip)]
    unnamed x10 -> x4, local copies, waits for them, and re-layouts: 0.68 us -> 0.01 us
  transfers between devices with their start and end apart: 2 -> 2, of which waited for: 1 -> 1; matrix products, arithmetic and copies ran while one was open for 0% -> 0% of each run, Pallas kernels for 5% -> 6%
where the time goes in v6:
time: 45.5 us; the launch traced here: 45.2 us
  blocking collectives  20.5 us (45%)
  starting transfers between devices  9.63 us (21%)
  waiting for transfers between devices  7.25 us (16%)
  Pallas kernels  7.17 us (16%)
  between operations  0.69 us (2%)
    all_gather x4, blocking collectives, of_both_cores(): return lax.all_gather(array, 'section', axis_index_groups=of_chip)  20.5 us
    all_to_all x1, waiting for transfers between devices, local(): lax.all_to_all(sums.reshape(members, 1, TOKENS), AXES, 0, 0, tiled=True,...  7.24 us
    all_to_all x1, starting transfers between devices, local(): lax.all_to_all(packed, 'section', 0, 0, tiled=True, axis_index_groups=ove...  4.98 us
    all_to_all x1, starting transfers between devices, local(): lax.all_to_all(sums.reshape(members, 1, TOKENS), AXES, 0, 0, tiled=True,...  4.65 us
    pallas_call x1, Pallas kernels, local(): pl.pallas_call(teacher_kernel, out_shape=(jax.ShapeDtypeStruct((chips, PA...  2.18 us
    pallas_call x1, Pallas kernels, local(): pl.pallas_call(gradient_kernel, out_shape=(jax.ShapeDtypeStruct(student_q...  1.39 us
    pallas_call x1, Pallas kernels, local(): pl.pallas_call(scores_kernel, out_shape=(squares, squares), in_specs=[SME...  1.23 us
    pallas_call x1, Pallas kernels, local(): pl.pallas_call(student_kernel, out_shape=(pltpu.VMEM((SENT, TOKENS), bf16...  1.03 us
  transfers between devices with their start and end apart: 2, of which 1 were waited for; matrix products, arithmetic and copies ran while one was open for 0% of the time, Pallas kernels for 6%

profile of v6, /device:TPU:1, one launch (start us, length us, event | category | flops | bytes accessed | tf_op | source)
XLA Modules:
  0.0 45.2 jit_solution(17864131936833125269)
XLA Ops:
  0.6 2.2 %teacher.1 = (f32[4,264,128]{2,1,0:T(8,128)}, s32[8,128]{1,0:T(8,128)S(1)}, f32[4,8]{1,0:T(4,128)S(1)}) custom-call(s32[8]{0:T(128)} %pairing.1, s32[8]{0:T(128)} %placement.1, f32[4,8]{1,0:T(4,128)} %bitcast.10, bf16[1,128,1024]{2,1,0:T(8,128)(2,1)} %q_ref.1, bf16[1,128,128]{2,1,0:T(8,128)(2,1)} %k_ref.1), custom_call_target="tpu_custom_call" | custom-call | flops 33554432 | bytes 400000 | tf_op jit(solution)/shard_map/teacher/pallas_call | solution.py:309
  2.8 0.0 copy-start.1
  2.8 0.0 copy-start
  2.8 5.0 %all-to-all-start = ((f32[4,264,128]{2,1,0:T(8,128)}), f32[4,264,128]{2,1,0:T(8,128)S(1)}, u32[]{:S(2)}, u32[]{:S(2)}) async-start(f32[4,264,128]{2,1,0:T(8,128)} %get-tuple-element.17), calls=%async_computation | async-start | bytes 1081344 | tf_op jit(solution)/shard_map/all_to_all | solution.py:326
  7.8 0.0 copy-done.1
  7.8 7.1 %all_gather.16.k_ref = bf16[2,2,128,128]{3,2,1,0:T(8,128)(2,1)S(1)} all-gather(bf16[1,2,128,128]{3,2,1,0:T(8,128)(2,1)S(1)} %copy-done.1), channel_id=1, replica_groups={{0,64},{128,192},{256,320},{384,448},{1,65},{129,193},{257,321},{385,44..., dimensions={0}, use_global_device_ids=true | all-gather | bytes 196608 | tf_op jit(solution)/shard_map/all_gather | solution.py:330
  14.9 0.0 copy-done
  14.9 2.2 %all_gather.15.q_ref = bf16[2,2,128,512]{3,2,1,0:T(8,128)(2,1)S(1)} all-gather(bf16[1,2,128,512]{3,2,1,0:T(8,128)(2,1)S(1)} %copy-done), channel_id=1, replica_groups={{0,64},{128,192},{256,320},{384,448},{1,65},{129,193},{257,321},{385,44..., dimensions={0}, use_global_device_ids=true | all-gather | bytes 786432 | tf_op jit(solution)/shard_map/all_gather | solution.py:330
  17.1 1.2 %scores.1 = (f32[4,264,128]{2,1,0:T(8,128)S(1)}, f32[4,264,128]{2,1,0:T(8,128)S(1)}) custom-call(s32[8,128]{1,0:T(8,128)S(1)} %get-tuple-element.15.table, f32[4,8]{1,0:T(4,128)S(1)} %get-tuple-element.16.scale_ref, bf16[2,2,128,512]{3,2,1,0:T(8,128)(2,1)S(1)} %all_gather.15.q_ref, bf16[2,2,128,128]{3,2,1,0:T(8,128)(2,1)S(1)} %all_gather.16.k_ref), custom_call_target="tpu_custom_call" | custom-call | flops 33554432 | bytes 1400000 | tf_op jit(solution)/shard_map/scores/pallas_call | solution.py:335
  18.3 0.0 all-to-all-done.arrived_ref
  18.3 1.0 %student.1 = (bf16[544,128]{1,0:T(8,128)(2,1)S(1)}, bf16[560,128]{1,0:T(8,128)(2,1)S(1)}) custom-call(s32[8,128]{1,0:T(8,128)S(1)} %get-tuple-element.15.table, f32[4,8]{1,0:T(4,128)S(1)} %get-tuple-element.16.scale_ref, f32[4,264,128]{2,1,0:T(8,128)S(1)} %all-to-all-done.arrived_ref, f32[4,264,128]{2,1,0:T(8,128)S(1)} %get-tuple-element.18.raw_ref, ...), custom_call_target="tpu_custom_call" | custom-call | flops 33554432 | bytes 1800000 | tf_op jit(solution)/shard_map/student/pallas_call | solution.py:345
  19.4 4.7 %all-gather = bf16[1120,128]{1,0:T(8,128)(2,1)S(1)} all-gather(bf16[560,128]{1,0:T(8,128)(2,1)S(1)} %get-tuple-element.21), channel_id=2, replica_groups={{0,64},{128,192},{256,320},{384,448},{1,65},{129,193},{257,321},{385,44..., dimensions={0}, use_global_device_ids=true | all-gather | bytes 430080 | tf_op jit(solution)/shard_map/all_gather | solution.py:330
  24.1 0.6 %spread.1 = f32[32,128]{1,0:T(8,128)} custom-call(bf16[2,560,128]{2,1,0:T(8,128)(2,1)S(1)} %bitcast.7), custom_call_target="tpu_custom_call" | custom-call | tf_op jit(solution)/shard_map/spread/pallas_call | solution.py:360
  24.7 4.6 %all-to-all-start.1 = ((f32[32,1,128]{2,1,0:T(1,128)}), f32[32,1,128]{2,1,0:T(1,128)S(1)}, u32[]{:S(2)}, u32[]{:S(2)}) async-start(f32[32,1,128]{2,1,0:T(1,128)} %bitcast.3), calls=%async_computation.1 | async-start | bytes 32768 | tf_op jit(solution)/shard_map/all_to_all | solution.py:368
  29.4 1.4 %gradient.1 = (bf16[1,2,128,512]{3,2,1,0:T(8,128)(2,1)}, bf16[1,2,128,128]{3,2,1,0:T(8,128)(2,1)}) custom-call(s32[8,128]{1,0:T(8,128)S(1)} %get-tuple-element.15.table, bf16[544,128]{1,0:T(8,128)(2,1)S(1)} %get-tuple-element.20.grad_ref, bf16[2,560,128]{2,1,0:T(8,128)(2,1)S(1)} %bitcast.8, bf16[2,2,128,512]{3,2,1,0:T(8,128)(2,1)S(1)} %all_gather.15.q_ref, ...), custom_call_target="tpu_custom_call" | custom-call | flops 67108864 | bytes 900000 | tf_op jit(solution)/shard_map/gradient/pallas_call | solution.py:371
  30.8 7.2 %all-to-all-done.1 = f32[32,1,128]{2,1,0:T(1,128)S(1)} async-done(((f32[32,1,128]{2,1,0:T(1,128)}), f32[32,1,128]{2,1,0:T(1,128)S(1)}, u32[]{:S(2)}, u32[]{:S(2)}) %all-to-all-start.1) | async-done | bytes 16416 | tf_op jit(solution)/shard_map/all_to_all | solution.py:368
  38.0 6.5 %all-gather.1 = f32[64,1,128]{2,1,0:T(1,128)S(1)} all-gather(f32[32,1,128]{2,1,0:T(1,128)S(1)} %all-to-all-done.1), channel_id=3, replica_groups={{0,64},{128,192},{256,320},{384,448},{1,65},{129,193},{257,321},{385,44..., dimensions={0}, use_global_device_ids=true | all-gather | bytes 49152 | tf_op jit(solution)/shard_map/all_gather | solution.py:330
  44.5 0.7 %final.1 = (f32[1,8]{1,0:T(1,128)}, f32[4,8]{1,0:T(4,128)}) custom-call(f32[2,32,128]{2,1,0:T(8,128)S(1)} %bitcast.9), custom_call_target="tpu_custom_call" | custom-call | tf_op jit(solution)/shard_map/final/pallas_call | solution.py:385
Async XLA Ops:
  2.8 5.0 %copy-start.1 = (bf16[1,2,128,128]{3,2,1,0:T(8,128)(2,1)S(1)}, bf16[1,2,128,128]{3,2,1,0:T(8,128)(2,1)}, u32[]{:S(2)}) copy-start(bf16[1,2,128,128]{3,2,1,0:T(8,128)(2,1)} %param.10) | copy-start | bytes 196612
  2.8 12.1 %copy-start = (bf16[1,2,128,512]{3,2,1,0:T(8,128)(2,1)S(1)}, bf16[1,2,128,512]{3,2,1,0:T(8,128)(2,1)}, u32[]{:S(2)}) copy-start(bf16[1,2,128,512]{3,2,1,0:T(8,128)(2,1)} %param.9) | copy-start | bytes 786436
  2.8 15.5 %all-to-all-start = ((f32[4,264,128]{2,1,0:T(8,128)}), f32[4,264,128]{2,1,0:T(8,128)S(1)}, u32[]{:S(2)}, u32[]{:S(2)}) async-start(f32[4,264,128]{2,1,0:T(8,128)} %get-tuple-element.17), calls=%async_computation | async-start | bytes 1081344 | tf_op jit(solution)/shard_map/all_to_all | solution.py:326
  24.7 13.3 %all-to-all-start.1 = ((f32[32,1,128]{2,1,0:T(1,128)}), f32[32,1,128]{2,1,0:T(1,128)S(1)}, u32[]{:S(2)}, u32[]{:S(2)}) async-start(f32[32,1,128]{2,1,0:T(1,128)} %bitcast.3), calls=%async_computation.1 | async-start | bytes 32768 | tf_op jit(solution)/shard_map/all_to_all | solution.py:368

commit v7 on v6

--- a/solution.py
+++ b/solution.py
@@ -22,6 +22,7 @@
 SENT = SLOTS * SLOT_ROWS
 INVERSE = 1.0 / math.sqrt(HEAD_WIDTH)
 HIDDEN = -1e30
+SMALLEST = 1.2e-38
 AXES = ("section", "head", "dp")
 
 
@@ -41,6 +42,12 @@
     scores = jnp.where(visible, scores, HIDDEN)
     shifted = scores - jnp.max(scores, axis=axis, keepdims=True)
     return shifted - jnp.log(jnp.sum(jnp.exp(shifted), axis=axis, keepdims=True))
+
+
+def softmax(scores, visible, axis):
+    scores = jnp.where(visible, scores, HIDDEN)
+    powers = jnp.exp(scores - jnp.max(scores, axis=axis, keepdims=True))
+    return powers * (1.0 / jnp.sum(powers, axis=axis, keepdims=True))
 
 
 def teacher_kernel(
@@ -55,27 +62,23 @@
     key = k_ref[0]
 
     scale_out[...] = scale_ref[...]
-    at_row = lax.broadcasted_iota(jnp.int32, (8, TOKENS), 0)
-    at_lane = lax.broadcasted_iota(jnp.int32, (8, TOKENS), 1)
-    table = jnp.zeros((8, TOKENS), jnp.int32)
+    at_row = lax.broadcasted_iota(jnp.int32, (2, LAYERS), 0)
+    at_lane = lax.broadcasted_iota(jnp.int32, (2, LAYERS), 1)
+    table = jnp.zeros((2, LAYERS), jnp.int32)
     for layer in range(LAYERS):
         entry = jnp.where(at_row == 0, pairing[layer], placement[layer])
         table = jnp.where(at_lane == layer, entry, table)
     table_ref[...] = table
 
     def target(head, turned):
-        logps = []
+        total = jnp.zeros((TOKENS, TOKENS), jnp.float32)
         for twin in (2 * head, 2 * head + 1):
             query = q_ref[0, :, twin * HEAD_WIDTH : (twin + 1) * HEAD_WIDTH]
             if turned:
-                scores = dot(key, query, 1, 1) * INVERSE
-                logps.append(log_softmax(scores, row <= col, 0))
+                total += softmax(dot(key, query, 1, 1) * INVERSE, row <= col, 0)
             else:
-                scores = dot(query, key, 1, 1) * INVERSE
-                logps.append(log_softmax(scores, col <= row, 1))
-        one, two = logps
-        high = jnp.maximum(one, two)
-        return high + jnp.log1p(jnp.exp(-jnp.abs(one - two))) - math.log(2.0)
+                total += softmax(dot(query, key, 1, 1) * INVERSE, col <= row, 1)
+        return total * 0.5
 
     packed[PAIRS * TOKENS :, :] = jnp.zeros((PACKED - PAIRS * TOKENS, TOKENS), jnp.float32)
     started = []
@@ -132,14 +135,14 @@
     )
 
 
-def scores_kernel(table, scale_ref, q_ref, k_ref, raw_ref, logp_ref):
+def scores_kernel(table, scale_ref, qk_ref, raw_ref, logp_ref):
     row, col = masks()
 
     def work(layer, source_chip, home_core, slot, rank):
-        key = k_ref[home_core, slot]
+        key = qk_ref[home_core, slot, :, HEADS * HEAD_WIDTH :]
 
         def query(head):
-            return q_ref[home_core, slot, :, head * HEAD_WIDTH : (head + 1) * HEAD_WIDTH]
+            return qk_ref[home_core, slot, :, head * HEAD_WIDTH : (head + 1) * HEAD_WIDTH]
 
         empty = jnp.zeros((PACKED - PAIRS * TOKENS, TOKENS), jnp.float32)
         raw_ref[rank, PAIRS * TOKENS :, :] = empty
@@ -166,9 +169,9 @@
 
     def work(layer, source_chip, home_core, slot, rank):
         def terms(rows):
-            target_logp = arrived_ref[source_chip, rows, :]
+            target = arrived_ref[source_chip, rows, :]
+            target_logp = jnp.log(jnp.maximum(target, SMALLEST))
             student_logp = logp_ref[rank, rows, :]
-            target = jnp.exp(target_logp)
             difference = jnp.exp(student_logp) - target
             return (
                 jnp.sum(target * (target_logp - student_logp), axis=0, keepdims=True),
@@ -230,7 +233,7 @@
     out_ref[...] = jnp.broadcast_to(total, out_ref.shape)
 
 
-def gradient_kernel(table, grad_ref, sent_ref, q_ref, k_ref, q_out, k_out):
+def gradient_kernel(table, grad_ref, sent_ref, qk_ref, q_out, k_out):
     me = lax.axis_index("section")
     core = lax.rem(me, 2)
     row, col = masks()
@@ -246,7 +249,7 @@
         @pl.when(slot < held)
         def _():
             direct = lax.rem(table[0, layers[slot]], 2) == core
-            key = k_ref[core, slot]
+            key = qk_ref[core, slot, :, HEADS * HEAD_WIDTH :]
             total = jnp.zeros((TOKENS, HEAD_WIDTH), jnp.float32)
 
             def rows(at, count):
@@ -266,7 +269,7 @@
                     grad = jnp.where(col <= row, square, 0.0)
                 grad = grad.astype(jnp.bfloat16)
                 lanes = slice(head * HEAD_WIDTH, (head + 1) * HEAD_WIDTH)
-                query = q_ref[core, slot, :, lanes]
+                query = qk_ref[core, slot, :, lanes]
                 q_out[0, slot, :, lanes] = dot(grad, key, 1 - over, 0).astype(jnp.bfloat16)
                 total += dot(grad, query, over, 0)
             k_out[0, slot] = total.astype(jnp.bfloat16)
@@ -310,7 +313,7 @@
         teacher_kernel,
         out_shape=(
             jax.ShapeDtypeStruct((chips, PACKED, TOKENS), f32),
-            pltpu.VMEM((8, TOKENS), jnp.int32),
+            pltpu.VMEM((2, LAYERS), jnp.int32),
             pltpu.VMEM((HEADS, LAYERS), f32),
         ),
         in_specs=[SMEM, SMEM, VMEM, VMEM, VMEM],
@@ -329,18 +332,18 @@
     def of_both_cores(array):
         return lax.all_gather(array, "section", axis_index_groups=of_chip)
 
-    chip_q, chip_k = (kept(of_both_cores(a[0])) for a in (student_q, student_k))
+    chip_qk = kept(of_both_cores(jnp.concatenate((student_q[0], student_k[0]), axis=2)))
     at_once = 2 * SLOTS
     squares = pltpu.VMEM((at_once, PACKED, TOKENS), f32)
     raw, logp = pl.pallas_call(
         scores_kernel,
         out_shape=(squares, squares),
-        in_specs=[SMEM, SMEM, VMEM, VMEM],
+        in_specs=[SMEM, SMEM, VMEM],
         out_specs=(VMEM, VMEM),
         cost_estimate=cost(8 * 2 * TOKENS**3, 1_400_000),
         compiler_params=SMALL,
         name="scores",
-    )(table, scales, chip_q, chip_k)
+    )(table, scales, chip_qk)
 
     grads, sent = pl.pallas_call(
         student_kernel,
@@ -374,12 +377,12 @@
             jax.ShapeDtypeStruct(student_q.shape, bf16),
             jax.ShapeDtypeStruct(student_k.shape, bf16),
         ),
-        in_specs=[SMEM, VMEM, VMEM, VMEM, VMEM],
+        in_specs=[SMEM, VMEM, VMEM, VMEM],
         out_specs=(VMEM, VMEM),
         cost_estimate=cost(16 * 2 * TOKENS**3, 900_000),
         compiler_params=SMALL,
         name="gradient",
-    )(table, kept(grads), chip_sent, chip_q, chip_k)
+    )(table, kept(grads), chip_sent, chip_qk)
 
     both = of_both_cores(rows.reshape(members, TOKENS))
     layer_kl, scale_grad = pl.pallas_call(

time: 45.5 us -> 45.3 us (level)
    all_gather x4 -> x3, blocking collectives: 20.5 us -> 20.5 us  [of_both_cores(): return lax.all_gather(array, 'section', axis_index_groups=of_chip)]
where the time goes in v7:
time: 45.3 us; the launch traced here: 45.1 us
  blocking collectives  20.5 us (45%)
  starting transfers between devices  9.57 us (21%)
  Pallas kernels  7.17 us (16%)
  waiting for transfers between devices  7.06 us (16%)
  between operations  0.69 us (2%)
    all_gather x3, blocking collectives, of_both_cores(): return lax.all_gather(array, 'section', axis_index_groups=of_chip)  20.5 us
    all_to_all x1, waiting for transfers between devices, local(): lax.all_to_all(sums.reshape(members, 1, TOKENS), AXES, 0, 0, tiled=True,...  7.05 us
    all_to_all x1, starting transfers between devices, local(): lax.all_to_all(packed, 'section', 0, 0, tiled=True, axis_index_groups=ove...  4.98 us
    all_to_all x1, starting transfers between devices, local(): lax.all_to_all(sums.reshape(members, 1, TOKENS), AXES, 0, 0, tiled=True,...  4.59 us
    pallas_call x1, Pallas kernels, local(): pl.pallas_call(teacher_kernel, out_shape=(jax.ShapeDtypeStruct((chips, PA...  2.08 us
    pallas_call x1, Pallas kernels, local(): pl.pallas_call(gradient_kernel, out_shape=(jax.ShapeDtypeStruct(student_q...  1.58 us
    pallas_call x1, Pallas kernels, local(): pl.pallas_call(scores_kernel, out_shape=(squares, squares), in_specs=[SME...  1.18 us
    pallas_call x1, Pallas kernels, local(): pl.pallas_call(student_kernel, out_shape=(pltpu.VMEM((SENT, TOKENS), bf16...  0.98 us
  transfers between devices with their start and end apart: 2, of which 1 were waited for; matrix products, arithmetic and copies ran while one was open for 0% of the time, Pallas kernels for 6%

profile of v7, /device:TPU:1, one launch (start us, length us, event | category | flops | bytes accessed | tf_op | source)
XLA Modules:
  0.0 45.1 jit_solution(3934586652384363741)
XLA Ops:
  0.6 2.1 %teacher.1 = (f32[4,264,128]{2,1,0:T(8,128)}, s32[2,8]{1,0:T(2,128)S(1)}, f32[4,8]{1,0:T(4,128)S(1)}) custom-call(s32[8]{0:T(128)} %pairing.1, s32[8]{0:T(128)} %placement.1, f32[4,8]{1,0:T(4,128)} %bitcast.17, bf16[1,128,1024]{2,1,0:T(8,128)(2,1)} %q_ref.1, bf16[1,128,128]{2,1,0:T(8,128)(2,1)} %k_ref.1), custom_call_target="tpu_custom_call" | custom-call | flops 33554432 | bytes 400000 | tf_op jit(solution)/shard_map/teacher/pallas_call | solution.py:312
  2.7 0.0 copy-start
  2.7 0.0 copy-start.1
  2.7 5.0 %all-to-all-start = ((f32[4,264,128]{2,1,0:T(8,128)}), f32[4,264,128]{2,1,0:T(8,128)S(1)}, u32[]{:S(2)}, u32[]{:S(2)}) async-start(f32[4,264,128]{2,1,0:T(8,128)} %get-tuple-element.17), calls=%async_computation | async-start | bytes 1081344 | tf_op jit(solution)/shard_map/all_to_all | solution.py:329
  7.7 0.0 copy-done
  7.7 0.0 copy-done.1
  7.8 7.4 %all-gather = bf16[4,128,640]{2,1,0:T(8,128)(2,1)S(1)} all-gather(bf16[2,128,640]{2,1,0:T(8,128)(2,1)S(1)} %pad_maximum_fusion), channel_id=2, replica_groups={{0,64},{128,192},{256,320},{384,448},{1,65},{129,193},{257,321},{385,44..., dimensions={0}, use_global_device_ids=true | all-gather | bytes 983040 | tf_op jit(solution)/shard_map/all_gather | solution.py:333
  15.2 1.2 %scores.1 = (f32[4,264,128]{2,1,0:T(8,128)S(1)}, f32[4,264,128]{2,1,0:T(8,128)S(1)}) custom-call(s32[2,8]{1,0:T(2,128)S(1)} %get-tuple-element.15.table, f32[4,8]{1,0:T(4,128)S(1)} %get-tuple-element.16.scale_ref, bf16[2,2,128,640]{3,2,1,0:T(8,128)(2,1)S(1)} %bitcast.10), custom_call_target="tpu_custom_call" | custom-call | flops 33554432 | bytes 1400000 | tf_op jit(solution)/shard_map/scores/pallas_call | solution.py:338
  16.4 0.0 all-to-all-done.arrived_ref
  16.4 1.0 %student.1 = (bf16[544,128]{1,0:T(8,128)(2,1)S(1)}, bf16[560,128]{1,0:T(8,128)(2,1)S(1)}) custom-call(s32[2,8]{1,0:T(2,128)S(1)} %get-tuple-element.15.table, f32[4,8]{1,0:T(4,128)S(1)} %get-tuple-element.16.scale_ref, f32[4,264,128]{2,1,0:T(8,128)S(1)} %all-to-all-done.arrived_ref, f32[4,264,128]{2,1,0:T(8,128)S(1)} %get-tuple-element.18.raw_ref, ...), custom_call_target="tpu_custom_call" | custom-call | flops 33554432 | bytes 1800000 | tf_op jit(solution)/shard_map/student/pallas_call | solution.py:348
  17.4 6.6 %all-gather.1 = bf16[1120,128]{1,0:T(8,128)(2,1)S(1)} all-gather(bf16[560,128]{1,0:T(8,128)(2,1)S(1)} %get-tuple-element.21), channel_id=3, replica_groups={{0,64},{128,192},{256,320},{384,448},{1,65},{129,193},{257,321},{385,44..., dimensions={0}, use_global_device_ids=true | all-gather | bytes 430080 | tf_op jit(solution)/shard_map/all_gather | solution.py:333
  24.0 0.6 %spread.1 = f32[32,128]{1,0:T(8,128)} custom-call(bf16[2,560,128]{2,1,0:T(8,128)(2,1)S(1)} %bitcast.12), custom_call_target="tpu_custom_call" | custom-call | tf_op jit(solution)/shard_map/spread/pallas_call | solution.py:363
  24.6 4.6 %all-to-all-start.1 = ((f32[32,1,128]{2,1,0:T(1,128)}), f32[32,1,128]{2,1,0:T(1,128)S(1)}, u32[]{:S(2)}, u32[]{:S(2)}) async-start(f32[32,1,128]{2,1,0:T(1,128)} %bitcast.6), calls=%async_computation.1 | async-start | bytes 32768 | tf_op jit(solution)/shard_map/all_to_all | solution.py:371
  29.2 1.6 %gradient.1 = (bf16[1,2,128,512]{3,2,1,0:T(8,128)(2,1)}, bf16[1,2,128,128]{3,2,1,0:T(8,128)(2,1)}) custom-call(s32[2,8]{1,0:T(2,128)S(1)} %get-tuple-element.15.table, bf16[544,128]{1,0:T(8,128)(2,1)S(1)} %get-tuple-element.20.grad_ref, bf16[2,560,128]{2,1,0:T(8,128)(2,1)S(1)} %bitcast.13, bf16[2,2,128,640]{3,2,1,0:T(8,128)(2,1)S(1)} %bitcast.11), custom_call_target="tpu_custom_call" | custom-call | flops 67108864 | bytes 900000 | tf_op jit(solution)/shard_map/gradient/pallas_call | solution.py:374
  30.8 7.1 %all-to-all-done.1 = f32[32,1,128]{2,1,0:T(1,128)S(1)} async-done(((f32[32,1,128]{2,1,0:T(1,128)}), f32[32,1,128]{2,1,0:T(1,128)S(1)}, u32[]{:S(2)}, u32[]{:S(2)}) %all-to-all-start.1) | async-done | bytes 16416 | tf_op jit(solution)/shard_map/all_to_all | solution.py:371
  37.9 6.5 %all-gather.2 = f32[64,1,128]{2,1,0:T(1,128)S(1)} all-gather(f32[32,1,128]{2,1,0:T(1,128)S(1)} %all-to-all-done.1), channel_id=4, replica_groups={{0,64},{128,192},{256,320},{384,448},{1,65},{129,193},{257,321},{385,44..., dimensions={0}, use_global_device_ids=true | all-gather | bytes 49152 | tf_op jit(solution)/shard_map/all_gather | solution.py:333
  44.3 0.7 %final.1 = (f32[1,8]{1,0:T(1,128)}, f32[4,8]{1,0:T(4,128)}) custom-call(f32[2,32,128]{2,1,0:T(8,128)S(1)} %bitcast.14), custom_call_target="tpu_custom_call" | custom-call | tf_op jit(solution)/shard_map/final/pallas_call | solution.py:388
  (1 shorter events, 0.0 us)
Async XLA Ops:
  2.7 5.0 %copy-start = (bf16[1,2,128,512]{3,2,1,0:T(8,128)(2,1)S(1)}, bf16[1,2,128,512]{3,2,1,0:T(8,128)(2,1)}, u32[]{:S(2)}) copy-start(bf16[1,2,128,512]{3,2,1,0:T(8,128)(2,1)} %param.9) | copy-start | bytes 786436
  2.7 5.0 %copy-start.1 = (bf16[1,2,128,128]{3,2,1,0:T(8,128)(2,1)S(1)}, bf16[1,2,128,128]{3,2,1,0:T(8,128)(2,1)}, u32[]{:S(2)}) copy-start(bf16[1,2,128,128]{3,2,1,0:T(8,128)(2,1)} %param.10) | copy-start | bytes 196612
  2.7 13.7 %all-to-all-start = ((f32[4,264,128]{2,1,0:T(8,128)}), f32[4,264,128]{2,1,0:T(8,128)S(1)}, u32[]{:S(2)}, u32[]{:S(2)}) async-start(f32[4,264,128]{2,1,0:T(8,128)} %get-tuple-element.17), calls=%async_computation | async-start | bytes 1081344 | tf_op jit(solution)/shard_map/all_to_all | solution.py:329
  24.6 13.2 %all-to-all-start.1 = ((f32[32,1,128]{2,1,0:T(1,128)}), f32[32,1,128]{2,1,0:T(1,128)S(1)}, u32[]{:S(2)}, u32[]{:S(2)}) async-start(f32[32,1,128]{2,1,0:T(1,128)} %bitcast.6), calls=%async_computation.1 | async-start | bytes 32768 | tf_op jit(solution)/shard_map/all_to_all | solution.py:371

commit v8 on v7

--- a/solution.py
+++ b/solution.py
@@ -50,9 +50,7 @@
     return powers * (1.0 / jnp.sum(powers, axis=axis, keepdims=True))
 
 
-def teacher_kernel(
-    pairing, placement, scale_ref, q_ref, k_ref, out_ref, table_ref, scale_out, packed, sems
-):
+def teacher_kernel(pairing, placement, q_ref, k_ref, out_ref, packed, sems):
     me = lax.axis_index("section")
     home = jnp.int32(0)
     for layer in range(LAYERS):
@@ -60,15 +58,6 @@
     chip = home // 2
     row, col = masks()
     key = k_ref[0]
-
-    scale_out[...] = scale_ref[...]
-    at_row = lax.broadcasted_iota(jnp.int32, (2, LAYERS), 0)
-    at_lane = lax.broadcasted_iota(jnp.int32, (2, LAYERS), 1)
-    table = jnp.zeros((2, LAYERS), jnp.int32)
-    for layer in range(LAYERS):
-        entry = jnp.where(at_row == 0, pairing[layer], placement[layer])
-        table = jnp.where(at_lane == layer, entry, table)
-    table_ref[...] = table
 
     def target(head, turned):
         total = jnp.zeros((TOKENS, TOKENS), jnp.float32)
@@ -101,13 +90,13 @@
         copy.wait()
 
 
-def for_my_layers(table, work):
+def for_my_layers(pairing, placement, work):
     me = lax.axis_index("section")
     chip, core = me // 2, lax.rem(me, 2)
 
     def step(layer, carry):
         slots, rank = carry[:2], carry[2]
-        source, home = table[0, layer], table[1, layer]
+        home, source = placement[layer], pairing[layer]
         home_core = lax.rem(home, 2)
         here = home // 2 == chip
         mine = here & (lax.rem(source, 2) == core)
@@ -135,17 +124,30 @@
     )
 
 
-def scores_kernel(table, scale_ref, qk_ref, raw_ref, logp_ref):
+def scores_kernel(pairing, placement, scale_ref, qk_ref, raw_ref, logp_ref, table_ref):
     row, col = masks()
+    at_row = lax.broadcasted_iota(jnp.int32, (2, LAYERS), 0)
+    at_lane = lax.broadcasted_iota(jnp.int32, (2, LAYERS), 1)
+    table = jnp.full((2, LAYERS), -1, jnp.int32)
+    for layer in range(LAYERS):
+        belongs = placement[layer] + LAYERS * pairing[layer]
+        table = jnp.where((at_row == 1) & (at_lane == layer), belongs, table)
+    table_ref[...] = table
 
     def work(layer, source_chip, home_core, slot, rank):
+        code = layer + 8 * source_chip + 32 * home_core + 64 * slot
+        table_ref[...] = jnp.where((at_row == 0) & (at_lane == rank), code, table_ref[...])
         key = qk_ref[home_core, slot, :, HEADS * HEAD_WIDTH :]
 
         def query(head):
             return qk_ref[home_core, slot, :, head * HEAD_WIDTH : (head + 1) * HEAD_WIDTH]
 
-        empty = jnp.zeros((PACKED - PAIRS * TOKENS, TOKENS), jnp.float32)
-        raw_ref[rank, PAIRS * TOKENS :, :] = empty
+        tail_row = lax.broadcasted_iota(jnp.int32, (PACKED - PAIRS * TOKENS, TOKENS), 0)
+        empty = jnp.zeros(tail_row.shape, jnp.float32)
+        scales = empty
+        for head in range(HEADS):
+            scales = jnp.where(tail_row == HEADS + head, scale_ref[head, layer] * INVERSE, scales)
+        raw_ref[rank, PAIRS * TOKENS :, :] = scales
         logp_ref[rank, PAIRS * TOKENS :, :] = empty
         for pair in range(PAIRS):
             plain = dot(query(2 * pair), key, 1, 1) * INVERSE
@@ -155,10 +157,10 @@
             turned = log_softmax(scale_ref[2 * pair + 1, layer] * turned, row <= col, 0)
             pack(logp_ref, rank, pair, plain, turned)
 
-    for_my_layers(table, work)
-
-
-def student_kernel(table, scale_ref, arrived_ref, raw_ref, logp_ref, grad_ref, sent_ref, sums_ref):
+    for_my_layers(pairing, placement, work)
+
+
+def student_kernel(table, arrived_ref, raw_ref, logp_ref, grad_ref, sent_ref, sums_ref):
     core = lax.rem(lax.axis_index("section"), 2)
     row, col = masks()
     lower = col <= row
@@ -167,7 +169,15 @@
     tail_row = lax.broadcasted_iota(jnp.int32, (TAIL, TOKENS), 0)
     sums_ref[...] = jnp.zeros_like(sums_ref)
 
-    def work(layer, source_chip, home_core, slot, rank):
+    held = jnp.int32(0)
+    for rank in range(2 * SLOTS):
+        held += (table[0, rank] >= 0).astype(jnp.int32)
+
+    def work(rank, carry):
+        code = table[0, rank]
+        layer, source_chip = code & 7, (code >> 3) & 3
+        home_core, slot = (code >> 5) & 1, code >> 6
+
         def terms(rows):
             target = arrived_ref[source_chip, rows, :]
             target_logp = jnp.log(jnp.maximum(target, SMALLEST))
@@ -179,6 +189,10 @@
                 difference * raw_ref[rank, rows, :],
             )
 
+        def scale_of(head):
+            at = PAIRS * TOKENS + HEADS + head
+            return raw_ref[rank, at : at + 1, :]
+
         last, last_difference, last_moved = terms(slice(PAIRS * TOKENS, PACKED))
         found = jnp.zeros((8, TOKENS), jnp.float32)
         divergence = last
@@ -187,8 +201,8 @@
         for pair in range(PAIRS):
             one, difference, moved = terms(slice(pair * TOKENS, (pair + 1) * TOKENS))
             divergence += one
-            first = scale_ref[2 * pair, layer] * INVERSE
-            second = scale_ref[2 * pair + 1, layer] * INVERSE
+            first = scale_of(2 * pair)
+            second = scale_of(2 * pair + 1)
             pieces.append(difference * jnp.where(lower, first, second))
             tail = jnp.where(tail_row == pair, last_difference[pair : pair + 1] * second, tail)
             of_first = jnp.sum(jnp.where(lower, moved, 0.0), axis=0, keepdims=True)
@@ -216,7 +230,9 @@
         def _():
             put(sent_ref, slot * SLOT_ROWS)
 
-    for_my_layers(table, work)
+        return carry
+
+    lax.fori_loop(0, held, work, 0)
     left, tile = sums_ref[...], jnp.zeros((TAIL, TOKENS), jnp.float32)
     for term in range(3):
         part = left.astype(jnp.bfloat16).astype(jnp.float32)
@@ -239,7 +255,7 @@
     row, col = masks()
     held, layers = jnp.int32(0), [jnp.int32(0)] * SLOTS
     for layer in range(LAYERS):
-        here = table[1, layer] == me
+        here = (table[1, layer] & (LAYERS - 1)) == me
         layers = [
             jnp.where(here & (held == slot), layer, had) for slot, had in enumerate(layers)
         ]
@@ -248,7 +264,7 @@
 
         @pl.when(slot < held)
         def _():
-            direct = lax.rem(table[0, layers[slot]], 2) == core
+            direct = ((table[1, layers[slot]] >> 3) & 1) == core
             key = qk_ref[core, slot, :, HEADS * HEAD_WIDTH :]
             total = jnp.zeros((TOKENS, HEAD_WIDTH), jnp.float32)
 
@@ -309,23 +325,18 @@
     of_chip = [[2 * x, 2 * x + 1] for x in range(chips)]
     members = len(groups[0])
 
-    packed, table, scales = pl.pallas_call(
+    packed = pl.pallas_call(
         teacher_kernel,
-        out_shape=(
-            jax.ShapeDtypeStruct((chips, PACKED, TOKENS), f32),
-            pltpu.VMEM((2, LAYERS), jnp.int32),
-            pltpu.VMEM((HEADS, LAYERS), f32),
-        ),
-        in_specs=[SMEM, SMEM, VMEM, VMEM, VMEM],
-        out_specs=(ANY, VMEM, VMEM),
+        out_shape=jax.ShapeDtypeStruct((chips, PACKED, TOKENS), f32),
+        in_specs=[SMEM, SMEM, VMEM, VMEM],
+        out_specs=ANY,
         scratch_shapes=[
             pltpu.VMEM((PACKED, TOKENS), f32),
             pltpu.SemaphoreType.DMA((PAIRS,)),
         ],
         cost_estimate=cost(8 * 2 * TOKENS**3, 400_000),
         name="teacher",
-    )(pairing, placement, student_scale.T, teacher_q, teacher_k)
-    table, scales = kept(table), kept(scales)
+    )(pairing, placement, teacher_q, teacher_k)
     arrived = lax.all_to_all(
         packed, "section", 0, 0, tiled=True, axis_index_groups=over_x
     )
@@ -335,15 +346,16 @@
     chip_qk = kept(of_both_cores(jnp.concatenate((student_q[0], student_k[0]), axis=2)))
     at_once = 2 * SLOTS
     squares = pltpu.VMEM((at_once, PACKED, TOKENS), f32)
-    raw, logp = pl.pallas_call(
+    raw, logp, table = pl.pallas_call(
         scores_kernel,
-        out_shape=(squares, squares),
-        in_specs=[SMEM, SMEM, VMEM],
-        out_specs=(VMEM, VMEM),
+        out_shape=(squares, squares, pltpu.VMEM((2, LAYERS), jnp.int32)),
+        in_specs=[SMEM, SMEM, SMEM, VMEM],
+        out_specs=(VMEM, VMEM, VMEM),
         cost_estimate=cost(8 * 2 * TOKENS**3, 1_400_000),
         compiler_params=SMALL,
         name="scores",
-    )(table, scales, chip_qk)
+    )(pairing, placement, student_scale.T, chip_qk)
+    table = kept(table)
 
     grads, sent = pl.pallas_call(
         student_kernel,
@@ -351,13 +363,13 @@
             pltpu.VMEM((SENT, TOKENS), bf16),
             pltpu.VMEM((SENT + TAIL, TOKENS), bf16),
         ),
-        in_specs=[SMEM, SMEM, VMEM, VMEM, VMEM],
+        in_specs=[SMEM, VMEM, VMEM, VMEM],
         out_specs=(VMEM, VMEM),
         scratch_shapes=[pltpu.VMEM((1, TOKENS), f32)],
         cost_estimate=cost(8 * 2 * TOKENS**3, 1_800_000),
         compiler_params=SMALL,
         name="student",
-    )(table, scales, *map(kept, (arrived, raw, logp)))
+    )(table, *map(kept, (arrived, raw, logp)))
 
     chip_sent = kept(of_both_cores(sent))
     sums = pl.pallas_call(

time: 45.3 us -> 45.3 us (level)
  local copies, waits for them, and re-layouts: 0.01 us -> 0.7 us
  blocking collectives: 20.5 us -> 19.9 us
    unnamed x4 -> x10, local copies, waits for them, and re-layouts: 0.01 us -> 0.7 us
    all_gather x3, blocking collectives: 20.5 us -> 19.9 us  [of_both_cores(): return lax.all_gather(array, 'section', axis_index_groups=of_chip)]
  transfers between devices with their start and end apart: 2 -> 2, of which waited for: 1 -> 1; matrix products, arithmetic and copies ran while one was open for 0% -> 0% of each run, Pallas kernels for 6% -> 7%
where the time goes in v8:
time: 45.3 us; the launch traced here: 45 us
  blocking collectives  19.9 us (44%)
  starting transfers between devices  9.75 us (22%)
  Pallas kernels  7.21 us (16%)
  waiting for transfers between devices  6.81 us (15%)
  local copies, waits for them, and re-layouts  0.7 us (2%)
  between operations  0.69 us (2%)
    all_gather x3, blocking collectives, of_both_cores(): return lax.all_gather(array, 'section', axis_index_groups=of_chip)  19.9 us
    all_to_all x1, waiting for transfers between devices, local(): lax.all_to_all(sums.reshape(members, 1, TOKENS), AXES, 0, 0, tiled=True,...  6.81 us
    all_to_all x1, starting transfers between devices, local(): lax.all_to_all(packed, 'section', 0, 0, tiled=True, axis_index_groups=ove...  4.99 us
    all_to_all x1, starting transfers between devices, local(): lax.all_to_all(sums.reshape(members, 1, TOKENS), AXES, 0, 0, tiled=True,...  4.76 us
    pallas_call x1, Pallas kernels, local(): pl.pallas_call(teacher_kernel, out_shape=jax.ShapeDtypeStruct((chips, PAC...  2.1 us
    pallas_call x1, Pallas kernels, local(): pl.pallas_call(gradient_kernel, out_shape=(jax.ShapeDtypeStruct(student_q...  1.82 us
    pallas_call x1, Pallas kernels, local(): pl.pallas_call(scores_kernel, out_shape=(squares, squares, pltpu.VMEM((2,...  1.18 us
  transfers between devices with their start and end apart: 2, of which 1 were waited for; matrix products, arithmetic and copies ran while one was open for 0% of the time, Pallas kernels for 7%

profile of v8, /device:TPU:1, one launch (start us, length us, event | category | flops | bytes accessed | tf_op | source)
XLA Modules:
  0.0 45.0 jit_solution(7243821628884234525)
XLA Ops:
  0.6 2.1 %teacher.1 = f32[4,264,128]{2,1,0:T(8,128)} custom-call(s32[8]{0:T(128)} %pairing.3, s32[8]{0:T(128)} %placement.3, bf16[1,128,1024]{2,1,0:T(8,128)(2,1)} %q_ref.1, bf16[1,128,128]{2,1,0:T(8,128)(2,1)} %k_ref.1), custom_call_target="tpu_custom_call" | custom-call | flops 33554432 | bytes 400000 | tf_op jit(solution)/shard_map/teacher/pallas_call | solution.py:328
  2.7 0.0 copy-start.3
  2.7 0.0 copy-start.4
  2.8 5.0 %all-to-all-start = ((f32[4,264,128]{2,1,0:T(8,128)}), f32[4,264,128]{2,1,0:T(8,128)S(1)}, u32[]{:S(2)}, u32[]{:S(2)}) async-start(f32[4,264,128]{2,1,0:T(8,128)} %teacher.1), calls=%async_computation | async-start | bytes 1081344 | tf_op jit(solution)/shard_map/all_to_all | solution.py:340
  7.7 0.0 copy-done.3
  7.7 0.0 copy-done.4
  7.8 7.4 %all-gather = bf16[4,128,640]{2,1,0:T(8,128)(2,1)S(1)} all-gather(bf16[2,128,640]{2,1,0:T(8,128)(2,1)S(1)} %pad_maximum_fusion), channel_id=2, replica_groups={{0,64},{128,192},{256,320},{384,448},{1,65},{129,193},{257,321},{385,44..., dimensions={0}, use_global_device_ids=true | all-gather | bytes 983040 | tf_op jit(solution)/shard_map/all_gather | solution.py:344
  15.2 0.0 copy-start
  15.2 0.0 copy-start.1
  15.2 0.0 copy-start.2
  15.2 0.7 %copy-done = f32[8,4]{0,1:T(4,128)S(1)} copy-done((f32[8,4]{0,1:T(4,128)S(1)}, f32[8,4]{0,1:T(4,128)}, u32[]{:S(2)}) %copy-start) | copy-done | bytes 152
  15.9 0.0 copy-done.1
  15.9 0.0 copy-done.2
  15.9 1.2 %scores.1 = (f32[4,264,128]{2,1,0:T(8,128)S(1)}, f32[4,264,128]{2,1,0:T(8,128)S(1)}, s32[2,8]{1,0:T(2,128)S(1)}) custom-call(s32[8]{0:T(128)S(1)} %copy-done.1, s32[8]{0:T(128)S(1)} %copy-done.2, f32[4,8]{1,0:T(4,128)S(1)} %bitcast.15, bf16[2,2,128,640]{3,2,1,0:T(8,128)(2,1)S(1)} %bitcast.10), custom_call_target="tpu_custom_call" | custom-call | flops 33554432 | bytes 1400000 | tf_op jit(solution)/shard_map/scores/pallas_call | solution.py:349
  17.1 0.0 all-to-all-done.arrived_ref
  17.1 0.8 %student.1 = (bf16[544,128]{1,0:T(8,128)(2,1)S(1)}, bf16[560,128]{1,0:T(8,128)(2,1)S(1)}) custom-call(s32[2,8]{1,0:T(2,128)S(1)} %get-tuple-element.13.table, f32[4,264,128]{2,1,0:T(8,128)S(1)} %all-to-all-done.arrived_ref, f32[4,264,128]{2,1,0:T(8,128)S(1)} %get-tuple-element.14.raw_ref, f32[4,264,128]{2,1,0:T(8,128)S(1)} %get-tuple-element.15.logp_ref), custom_call_target="tpu_custom_call" | custom-call | flops 33554432 | bytes 1800000 | tf_op jit(solution)/shard_map/student/pallas_call | solution.py:360
  17.9 5.9 %all-gather.1 = bf16[1120,128]{1,0:T(8,128)(2,1)S(1)} all-gather(bf16[560,128]{1,0:T(8,128)(2,1)S(1)} %get-tuple-element.17), channel_id=3, replica_groups={{0,64},{128,192},{256,320},{384,448},{1,65},{129,193},{257,321},{385,44..., dimensions={0}, use_global_device_ids=true | all-gather | bytes 430080 | tf_op jit(solution)/shard_map/all_gather | solution.py:344
  23.8 0.6 %spread.1 = f32[32,128]{1,0:T(8,128)} custom-call(bf16[2,560,128]{2,1,0:T(8,128)(2,1)S(1)} %bitcast.12), custom_call_target="tpu_custom_call" | custom-call | tf_op jit(solution)/shard_map/spread/pallas_call | solution.py:375
  24.4 4.8 %all-to-all-start.1 = ((f32[32,1,128]{2,1,0:T(1,128)}), f32[32,1,128]{2,1,0:T(1,128)S(1)}, u32[]{:S(2)}, u32[]{:S(2)}) async-start(f32[32,1,128]{2,1,0:T(1,128)} %bitcast.6), calls=%async_computation.1 | async-start | bytes 32768 | tf_op jit(solution)/shard_map/all_to_all | solution.py:383
  29.2 1.8 %gradient.1 = (bf16[1,2,128,512]{3,2,1,0:T(8,128)(2,1)}, bf16[1,2,128,128]{3,2,1,0:T(8,128)(2,1)}) custom-call(s32[2,8]{1,0:T(2,128)S(1)} %get-tuple-element.13.table, bf16[544,128]{1,0:T(8,128)(2,1)S(1)} %get-tuple-element.16.grad_ref, bf16[2,560,128]{2,1,0:T(8,128)(2,1)S(1)} %bitcast.13, bf16[2,2,128,640]{3,2,1,0:T(8,128)(2,1)S(1)} %bitcast.11), custom_call_target="tpu_custom_call" | custom-call | flops 67108864 | bytes 900000 | tf_op jit(solution)/shard_map/gradient/pallas_call | solution.py:386
  31.0 6.8 %all-to-all-done.1 = f32[32,1,128]{2,1,0:T(1,128)S(1)} async-done(((f32[32,1,128]{2,1,0:T(1,128)}), f32[32,1,128]{2,1,0:T(1,128)S(1)}, u32[]{:S(2)}, u32[]{:S(2)}) %all-to-all-start.1) | async-done | bytes 16416 | tf_op jit(solution)/shard_map/all_to_all | solution.py:383
  37.8 6.5 %all-gather.2 = f32[64,1,128]{2,1,0:T(1,128)S(1)} all-gather(f32[32,1,128]{2,1,0:T(1,128)S(1)} %all-to-all-done.1), channel_id=4, replica_groups={{0,64},{128,192},{256,320},{384,448},{1,65},{129,193},{257,321},{385,44..., dimensions={0}, use_global_device_ids=true | all-gather | bytes 49152 | tf_op jit(solution)/shard_map/all_gather | solution.py:344
  44.3 0.7 %final.1 = (f32[1,8]{1,0:T(1,128)}, f32[4,8]{1,0:T(4,128)}) custom-call(f32[2,32,128]{2,1,0:T(8,128)S(1)} %bitcast.14), custom_call_target="tpu_custom_call" | custom-call | tf_op jit(solution)/shard_map/final/pallas_call | solution.py:400
  (1 shorter events, 0.0 us)
Async XLA Ops:
  2.7 5.0 %copy-start.3 = (bf16[1,2,128,512]{3,2,1,0:T(8,128)(2,1)S(1)}, bf16[1,2,128,512]{3,2,1,0:T(8,128)(2,1)}, u32[]{:S(2)}) copy-start(bf16[1,2,128,512]{3,2,1,0:T(8,128)(2,1)} %param.9) | copy-start | bytes 786436
  2.7 5.0 %copy-start.4 = (bf16[1,2,128,128]{3,2,1,0:T(8,128)(2,1)S(1)}, bf16[1,2,128,128]{3,2,1,0:T(8,128)(2,1)}, u32[]{:S(2)}) copy-start(bf16[1,2,128,128]{3,2,1,0:T(8,128)(2,1)} %param.10) | copy-start | bytes 196612
  2.8 14.3 %all-to-all-start = ((f32[4,264,128]{2,1,0:T(8,128)}), f32[4,264,128]{2,1,0:T(8,128)S(1)}, u32[]{:S(2)}, u32[]{:S(2)}) async-start(f32[4,264,128]{2,1,0:T(8,128)} %teacher.1), calls=%async_computation | async-start | bytes 1081344 | tf_op jit(solution)/shard_map/all_to_all | solution.py:340
  15.2 0.7 %copy-start = (f32[8,4]{0,1:T(4,128)S(1)}, f32[8,4]{0,1:T(4,128)}, u32[]{:S(2)}) copy-start(f32[8,4]{0,1:T(4,128)} %param.11) | copy-start | bytes 388
  15.2 0.7 %copy-start.1 = (s32[8]{0:T(128)S(1)}, s32[8]{0:T(128)}, u32[]{:S(2)}) copy-start(s32[8]{0:T(128)} %pairing.3) | copy-start | bytes 100
  15.2 0.7 %copy-start.2 = (s32[8]{0:T(128)S(1)}, s32[8]{0:T(128)}, u32[]{:S(2)}) copy-start(s32[8]{0:T(128)} %placement.3) | copy-start | bytes 100
  24.4 13.4 %all-to-all-start.1 = ((f32[32,1,128]{2,1,0:T(1,128)}), f32[32,1,128]{2,1,0:T(1,128)S(1)}, u32[]{:S(2)}, u32[]{:S(2)}) async-start(f32[32,1,128]{2,1,0:T(1,128)} %bitcast.6), calls=%async_computation.1 | async-start | bytes 32768 | tf_op jit(solution)/shard_map/all_to_all | solution.py:383

commit v9 on v8

--- a/solution.py
+++ b/solution.py
@@ -20,6 +20,7 @@
 TAIL = 16
 SLOT_ROWS = PAIRS * TOKENS + TAIL
 SENT = SLOTS * SLOT_ROWS
+SUM_ROWS = 8
 INVERSE = 1.0 / math.sqrt(HEAD_WIDTH)
 HIDDEN = -1e30
 SMALLEST = 1.2e-38
@@ -160,7 +161,7 @@
     for_my_layers(pairing, placement, work)
 
 
-def student_kernel(table, arrived_ref, raw_ref, logp_ref, grad_ref, sent_ref, sums_ref):
+def student_kernel(table, arrived_ref, raw_ref, logp_ref, out_ref, grad_ref, sent_ref, sums_ref):
     core = lax.rem(lax.axis_index("section"), 2)
     row, col = masks()
     lower = col <= row
@@ -233,20 +234,7 @@
         return carry
 
     lax.fori_loop(0, held, work, 0)
-    left, tile = sums_ref[...], jnp.zeros((TAIL, TOKENS), jnp.float32)
-    for term in range(3):
-        part = left.astype(jnp.bfloat16).astype(jnp.float32)
-        tile = jnp.where(tail_row == term, part, tile)
-        left -= part
-    sent_ref[SENT:, :] = tile.astype(jnp.bfloat16)
-
-
-def spread_kernel(pair_ref, out_ref):
-    terms = pair_ref[:, SENT:, :].astype(jnp.float32)
-    total = jnp.zeros((1, TOKENS), jnp.float32)
-    for core in range(2):
-        total += (terms[core, 0:1] + terms[core, 1:2]) + terms[core, 2:3]
-    out_ref[...] = jnp.broadcast_to(total, out_ref.shape)
+    out_ref[...] = jnp.broadcast_to(sums_ref[...][None], out_ref.shape)
 
 
 def gradient_kernel(table, grad_ref, sent_ref, qk_ref, q_out, k_out):
@@ -297,9 +285,13 @@
 
 
 def final_kernel(rows_ref, kl_ref, scale_ref):
-    divergence = jnp.sum(rows_ref[0], axis=0, keepdims=True)
+    def total(core):
+        each = jnp.sum(rows_ref[core], axis=0)
+        return each[0:1] + each[SUM_ROWS : SUM_ROWS + 1]
+
+    divergence = total(0)
     kl_ref[...] = divergence[:, :LAYERS] / (STUDENT_HEADS * TOKENS)
-    terms = jnp.sum(rows_ref[1], axis=0, keepdims=True)
+    terms = total(1)
     scale_ref[...] = jnp.concatenate(
         [terms[:, SCALE_LANE + LAYERS * h : SCALE_LANE + LAYERS * (h + 1)] for h in range(HEADS)], axis=0
     )
@@ -357,32 +349,24 @@
     )(pairing, placement, student_scale.T, chip_qk)
     table = kept(table)
 
-    grads, sent = pl.pallas_call(
+    sums, grads, sent = pl.pallas_call(
         student_kernel,
         out_shape=(
+            pltpu.VMEM((members, SUM_ROWS, TOKENS), f32),
             pltpu.VMEM((SENT, TOKENS), bf16),
-            pltpu.VMEM((SENT + TAIL, TOKENS), bf16),
+            pltpu.VMEM((SENT, TOKENS), bf16),
         ),
         in_specs=[SMEM, VMEM, VMEM, VMEM],
-        out_specs=(VMEM, VMEM),
+        out_specs=(VMEM, VMEM, VMEM),
         scratch_shapes=[pltpu.VMEM((1, TOKENS), f32)],
         cost_estimate=cost(8 * 2 * TOKENS**3, 1_800_000),
         compiler_params=SMALL,
         name="student",
     )(table, *map(kept, (arrived, raw, logp)))
 
+    sums = lax.all_gather(sums, "section", axis=1, tiled=True, axis_index_groups=of_chip)
+    rows = lax.all_to_all(sums, AXES, 0, 0, tiled=True, axis_index_groups=groups)
     chip_sent = kept(of_both_cores(sent))
-    sums = pl.pallas_call(
-        spread_kernel,
-        out_shape=jax.ShapeDtypeStruct((members, TOKENS), f32),
-        in_specs=[VMEM],
-        out_specs=VMEM,
-        compiler_params=SMALL,
-        name="spread",
-    )(chip_sent)
-    rows = lax.all_to_all(
-        sums.reshape(members, 1, TOKENS), AXES, 0, 0, tiled=True, axis_index_groups=groups
-    )
     q_grad, k_grad = pl.pallas_call(
         gradient_kernel,
         out_shape=(
@@ -396,7 +380,7 @@
         name="gradient",
     )(table, kept(grads), chip_sent, chip_qk)
 
-    both = of_both_cores(rows.reshape(members, TOKENS))
+    both = of_both_cores(rows)
     layer_kl, scale_grad = pl.pallas_call(
         final_kernel,
         out_shape=(

time: 45.3 us -> 46.2 us (1.020)
  blocking collectives: 19.9 us -> 26.3 us
  waiting for transfers between devices: 6.81 us -> 2.61 us
  Pallas kernels: 7.21 us -> 5.78 us
    all_gather x0 -> x1, blocking collectives: none -> 6.64 us  [local(): lax.all_gather(sums, 'section', axis=1, tiled=True, axis_index_groups=of_...]
    all_to_all x1, waiting for transfers between devices: 6.81 us -> 2.61 us  [local(): lax.all_to_all(sums, AXES, 0, 0, tiled=True, axis_index_groups=groups)]
    pallas_call x2 -> x1, Pallas kernels: 1.38 us -> 0.58 us  [local(): pl.pallas_call(student_kernel, out_shape=(pltpu.VMEM((members, SUM_ROWS,...]
  transfers between devices with their start and end apart: 2 -> 2, of which waited for: 1 -> 1; matrix products, arithmetic and copies ran while one was open for 0% -> 0% of each run, Pallas kernels for 7% -> 5%
where the time goes in v9:
time: 46.2 us; the launch traced here: 45.9 us
  blocking collectives  26.3 us (57%)
  starting transfers between devices  9.77 us (21%)
  Pallas kernels  5.78 us (13%)
  waiting for transfers between devices  2.61 us (6%)
  local copies, waits for them, and re-layouts  0.7 us (2%)
  between operations  0.7 us (2%)
    all_gather x3, blocking collectives, of_both_cores(): return lax.all_gather(array, 'section', axis_index_groups=of_chip)  19.7 us
    all_gather x1, blocking collectives, local(): lax.all_gather(sums, 'section', axis=1, tiled=True, axis_index_groups=of_...  6.64 us
    all_to_all x1, starting transfers between devices, local(): lax.all_to_all(packed, 'section', 0, 0, tiled=True, axis_index_groups=ove...  4.99 us
    all_to_all x1, starting transfers between devices, local(): lax.all_to_all(sums, AXES, 0, 0, tiled=True, axis_index_groups=groups)  4.77 us
    all_to_all x1, waiting for transfers between devices, local(): lax.all_to_all(sums, AXES, 0, 0, tiled=True, axis_index_groups=groups)  2.61 us
    pallas_call x1, Pallas kernels, local(): pl.pallas_call(teacher_kernel, out_shape=jax.ShapeDtypeStruct((chips, PAC...  2.09 us
    pallas_call x1, Pallas kernels, local(): pl.pallas_call(gradient_kernel, out_shape=(jax.ShapeDtypeStruct(student_q...  1.58 us
  transfers between devices with their start and end apart: 2, of which 1 were waited for; matrix products, arithmetic and copies ran while one was open for 0% of the time, Pallas kernels for 5%

profile of v9, /device:TPU:1, one launch (start us, length us, event | category | flops | bytes accessed | tf_op | source)
XLA Modules:
  0.0 45.9 jit_solution(14319163146149456386)
XLA Ops:
  0.6 2.1 %teacher.1 = f32[4,264,128]{2,1,0:T(8,128)} custom-call(s32[8]{0:T(128)} %pairing.3, s32[8]{0:T(128)} %placement.3, bf16[1,128,1024]{2,1,0:T(8,128)(2,1)} %q_ref.1, bf16[1,128,128]{2,1,0:T(8,128)(2,1)} %k_ref.1), custom_call_target="tpu_custom_call" | custom-call | flops 33554432 | bytes 400000 | tf_op jit(solution)/shard_map/teacher/pallas_call | solution.py:320
  2.7 0.0 copy-start.3
  2.7 0.0 copy-start.4
  2.8 5.0 %all-to-all-start = ((f32[4,264,128]{2,1,0:T(8,128)}), f32[4,264,128]{2,1,0:T(8,128)S(1)}, u32[]{:S(2)}, u32[]{:S(2)}) async-start(f32[4,264,128]{2,1,0:T(8,128)} %teacher.1), calls=%async_computation | async-start | bytes 1081344 | tf_op jit(solution)/shard_map/all_to_all | solution.py:332
  7.7 0.0 copy-done.3
  7.7 0.0 copy-done.4
  7.8 7.4 %all-gather = bf16[4,128,640]{2,1,0:T(8,128)(2,1)S(1)} all-gather(bf16[2,128,640]{2,1,0:T(8,128)(2,1)S(1)} %pad_maximum_fusion), channel_id=2, replica_groups={{0,64},{128,192},{256,320},{384,448},{1,65},{129,193},{257,321},{385,44..., dimensions={0}, use_global_device_ids=true | all-gather | bytes 983040 | tf_op jit(solution)/shard_map/all_gather | solution.py:336
  15.2 0.0 copy-start
  15.2 0.0 copy-start.1
  15.2 0.0 copy-start.2
  15.2 0.7 %copy-done = f32[8,4]{0,1:T(4,128)S(1)} copy-done((f32[8,4]{0,1:T(4,128)S(1)}, f32[8,4]{0,1:T(4,128)}, u32[]{:S(2)}) %copy-start) | copy-done | bytes 152
  15.9 0.0 copy-done.1
  15.9 0.0 copy-done.2
  15.9 0.8 %scores.1 = (f32[4,264,128]{2,1,0:T(8,128)S(1)}, f32[4,264,128]{2,1,0:T(8,128)S(1)}, s32[2,8]{1,0:T(2,128)S(1)}) custom-call(s32[8]{0:T(128)S(1)} %copy-done.1, s32[8]{0:T(128)S(1)} %copy-done.2, f32[4,8]{1,0:T(4,128)S(1)} %bitcast.11, bf16[2,2,128,640]{3,2,1,0:T(8,128)(2,1)S(1)} %bitcast.7), custom_call_target="tpu_custom_call" | custom-call | flops 33554432 | bytes 1400000 | tf_op jit(solution)/shard_map/scores/pallas_call | solution.py:341
  16.7 0.0 all-to-all-done.arrived_ref
  16.7 0.6 %student.1 = (f32[32,8,128]{2,1,0:T(8,128)S(1)}, bf16[544,128]{1,0:T(8,128)(2,1)S(1)}, bf16[544,128]{1,0:T(8,128)(2,1)S(1)}) custom-call(s32[2,8]{1,0:T(2,128)S(1)} %get-tuple-element.14.table, f32[4,264,128]{2,1,0:T(8,128)S(1)} %all-to-all-done.arrived_ref, f32[4,264,128]{2,1,0:T(8,128)S(1)} %get-tuple-element.15.raw_ref, ...), custom_call_target="tpu_custom_call" | custom-call | flops 33554432 | bytes 1800000 | tf_op jit(solution)/shard_map/student/pallas_call | solution.py:352
  17.3 6.6 %all_gather.25 = f32[32,16,128]{2,1,0:T(8,128)} all-gather(f32[32,8,128]{2,1,0:T(8,128)S(1)} %get-tuple-element.21), channel_id=1, replica_groups={{0,64},{128,192},{256,320},{384,448},{1,65},{129,193},{257,321},{385,44..., dimensions={1}, use_global_device_ids=true | all-gather | bytes 393216 | tf_op jit(solution)/shard_map/all_gather | solution.py:367
  23.9 4.8 %all-to-all-start.1 = ((f32[32,16,128]{2,1,0:T(8,128)}), f32[32,16,128]{2,1,0:T(8,128)S(1)}, u32[]{:S(2)}, u32[]{:S(2)}) async-start(f32[32,16,128]{2,1,0:T(8,128)} %all_gather.25), calls=%async_computation.1 | async-start | bytes 524288 | tf_op jit(solution)/shard_map/all_to_all | solution.py:368
  28.7 5.5 %all-gather.1 = bf16[1088,128]{1,0:T(8,128)(2,1)S(1)} all-gather(bf16[544,128]{1,0:T(8,128)(2,1)S(1)} %get-tuple-element.18), channel_id=3, replica_groups={{0,64},{128,192},{256,320},{384,448},{1,65},{129,193},{257,321},{385,44..., dimensions={0}, use_global_device_ids=true | all-gather | bytes 417792 | tf_op jit(solution)/shard_map/all_gather | solution.py:336
  34.2 1.6 %gradient.1 = (bf16[1,2,128,512]{3,2,1,0:T(8,128)(2,1)}, bf16[1,2,128,128]{3,2,1,0:T(8,128)(2,1)}) custom-call(s32[2,8]{1,0:T(2,128)S(1)} %get-tuple-element.14.table, bf16[544,128]{1,0:T(8,128)(2,1)S(1)} %get-tuple-element.17.grad_ref, bf16[2,544,128]{2,1,0:T(8,128)(2,1)S(1)} %bitcast.10, bf16[2,2,128,640]{3,2,1,0:T(8,128)(2,1)S(1)} %bitcast.8), custom_call_target="tpu_custom_call" | custom-call | flops 67108864 | bytes 900000 | tf_op jit(solution)/shard_map/gradient/pallas_call | solution.py:370
  35.8 2.6 %all-to-all-done.1 = f32[32,16,128]{2,1,0:T(8,128)S(1)} async-done(((f32[32,16,128]{2,1,0:T(8,128)}), f32[32,16,128]{2,1,0:T(8,128)S(1)}, u32[]{:S(2)}, u32[]{:S(2)}) %all-to-all-start.1) | async-done | bytes 262176 | tf_op jit(solution)/shard_map/all_to_all | solution.py:368
  38.4 6.8 %all-gather.2 = f32[64,16,128]{2,1,0:T(8,128)S(1)} all-gather(f32[32,16,128]{2,1,0:T(8,128)S(1)} %all-to-all-done.1), channel_id=4, replica_groups={{0,64},{128,192},{256,320},{384,448},{1,65},{129,193},{257,321},{385,44..., dimensions={0}, use_global_device_ids=true | all-gather | bytes 786432 | tf_op jit(solution)/shard_map/all_gather | solution.py:336
  45.2 0.8 %final.1 = (f32[1,8]{1,0:T(1,128)}, f32[4,8]{1,0:T(4,128)}) custom-call(f32[2,32,16,128]{3,2,1,0:T(8,128)S(1)} %bitcast.9), custom_call_target="tpu_custom_call" | custom-call | tf_op jit(solution)/shard_map/final/pallas_call | solution.py:384
  (1 shorter events, 0.0 us)
Async XLA Ops:
  2.7 5.0 %copy-start.3 = (bf16[1,2,128,512]{3,2,1,0:T(8,128)(2,1)S(1)}, bf16[1,2,128,512]{3,2,1,0:T(8,128)(2,1)}, u32[]{:S(2)}) copy-start(bf16[1,2,128,512]{3,2,1,0:T(8,128)(2,1)} %param.9) | copy-start | bytes 786436
  2.7 5.0 %copy-start.4 = (bf16[1,2,128,128]{3,2,1,0:T(8,128)(2,1)S(1)}, bf16[1,2,128,128]{3,2,1,0:T(8,128)(2,1)}, u32[]{:S(2)}) copy-start(bf16[1,2,128,128]{3,2,1,0:T(8,128)(2,1)} %param.10) | copy-start | bytes 196612
  2.8 14.0 %all-to-all-start = ((f32[4,264,128]{2,1,0:T(8,128)}), f32[4,264,128]{2,1,0:T(8,128)S(1)}, u32[]{:S(2)}, u32[]{:S(2)}) async-start(f32[4,264,128]{2,1,0:T(8,128)} %teacher.1), calls=%async_computation | async-start | bytes 1081344 | tf_op jit(solution)/shard_map/all_to_all | solution.py:332
  15.2 0.7 %copy-start = (f32[8,4]{0,1:T(4,128)S(1)}, f32[8,4]{0,1:T(4,128)}, u32[]{:S(2)}) copy-start(f32[8,4]{0,1:T(4,128)} %param.11) | copy-start | bytes 388
  15.2 0.7 %copy-start.1 = (s32[8]{0:T(128)S(1)}, s32[8]{0:T(128)}, u32[]{:S(2)}) copy-start(s32[8]{0:T(128)} %pairing.3) | copy-start | bytes 100
  15.2 0.7 %copy-start.2 = (s32[8]{0:T(128)S(1)}, s32[8]{0:T(128)}, u32[]{:S(2)}) copy-start(s32[8]{0:T(128)} %placement.3) | copy-start | bytes 100
  23.9 14.5 %all-to-all-start.1 = ((f32[32,16,128]{2,1,0:T(8,128)}), f32[32,16,128]{2,1,0:T(8,128)S(1)}, u32[]{:S(2)}, u32[]{:S(2)}) async-start(f32[32,16,128]{2,1,0:T(8,128)} %all_gather.25), calls=%async_computation.1 | async-start | bytes 524288 | tf_op jit(solution)/shard_map/all_to_all | solution.py:368

commit v10 on v8

--- a/solution.py
+++ b/solution.py
@@ -160,7 +160,7 @@
     for_my_layers(pairing, placement, work)
 
 
-def student_kernel(table, arrived_ref, raw_ref, logp_ref, grad_ref, sent_ref, sums_ref):
+def student_kernel(table, arrived_ref, raw_ref, logp_ref, sums_ref, grad_ref, sent_ref):
     core = lax.rem(lax.axis_index("section"), 2)
     row, col = masks()
     lower = col <= row
@@ -233,20 +233,10 @@
         return carry
 
     lax.fori_loop(0, held, work, 0)
-    left, tile = sums_ref[...], jnp.zeros((TAIL, TOKENS), jnp.float32)
-    for term in range(3):
-        part = left.astype(jnp.bfloat16).astype(jnp.float32)
-        tile = jnp.where(tail_row == term, part, tile)
-        left -= part
-    sent_ref[SENT:, :] = tile.astype(jnp.bfloat16)
 
 
 def spread_kernel(pair_ref, out_ref):
-    terms = pair_ref[:, SENT:, :].astype(jnp.float32)
-    total = jnp.zeros((1, TOKENS), jnp.float32)
-    for core in range(2):
-        total += (terms[core, 0:1] + terms[core, 1:2]) + terms[core, 2:3]
-    out_ref[...] = jnp.broadcast_to(total, out_ref.shape)
+    out_ref[...] = jnp.broadcast_to(pair_ref[0] + pair_ref[1], out_ref.shape)
 
 
 def gradient_kernel(table, grad_ref, sent_ref, qk_ref, q_out, k_out):
@@ -357,21 +347,20 @@
     )(pairing, placement, student_scale.T, chip_qk)
     table = kept(table)
 
-    grads, sent = pl.pallas_call(
+    sums, grads, sent = pl.pallas_call(
         student_kernel,
         out_shape=(
+            pltpu.VMEM((1, TOKENS), f32),
             pltpu.VMEM((SENT, TOKENS), bf16),
-            pltpu.VMEM((SENT + TAIL, TOKENS), bf16),
+            pltpu.VMEM((SENT, TOKENS), bf16),
         ),
         in_specs=[SMEM, VMEM, VMEM, VMEM],
-        out_specs=(VMEM, VMEM),
-        scratch_shapes=[pltpu.VMEM((1, TOKENS), f32)],
+        out_specs=(VMEM, VMEM, VMEM),
         cost_estimate=cost(8 * 2 * TOKENS**3, 1_800_000),
         compiler_params=SMALL,
         name="student",
     )(table, *map(kept, (arrived, raw, logp)))
 
-    chip_sent = kept(of_both_cores(sent))
     sums = pl.pallas_call(
         spread_kernel,
         out_shape=jax.ShapeDtypeStruct((members, TOKENS), f32),
@@ -379,7 +368,8 @@
         out_specs=VMEM,
         compiler_params=SMALL,
         name="spread",
-    )(chip_sent)
+    )(kept(of_both_cores(sums)))
+    chip_sent = kept(of_both_cores(sent))
     rows = lax.all_to_all(
         sums.reshape(members, 1, TOKENS), AXES, 0, 0, tiled=True, axis_index_groups=groups
     )

time: 45.3 us -> 45 us (level)
  blocking collectives: 19.9 us -> 25.4 us
  waiting for transfers between devices: 6.81 us -> 1.86 us
  Pallas kernels: 7.21 us -> 6.11 us
    all_gather x3 -> x4, blocking collectives: 19.9 us -> 25.4 us  [of_both_cores(): return lax.all_gather(array, 'section', axis_index_groups=of_chip)]
    all_to_all x1, waiting for transfers between devices: 6.81 us -> 1.86 us  [local(): lax.all_to_all(sums.reshape(members, 1, TOKENS), AXES, 0, 0, tiled=True,...]
    pallas_call x1, Pallas kernels: 1.82 us -> 1.33 us  [local(): pl.pallas_call(gradient_kernel, out_shape=(jax.ShapeDtypeStruct(student_q...]
  transfers between devices with their start and end apart: 2 -> 2, of which waited for: 1 -> 1; matrix products, arithmetic and copies ran while one was open for 0% -> 0% of each run, Pallas kernels for 7% -> 5%
where the time goes in v10:
time: 45 us; the launch traced here: 44.8 us
  blocking collectives  25.4 us (56%)
  starting transfers between devices  9.91 us (22%)
  Pallas kernels  6.11 us (14%)
  waiting for transfers between devices  1.86 us (4%)
  local copies, waits for them, and re-layouts  0.7 us (2%)
  between operations  0.7 us (2%)
    all_gather x4, blocking collectives, of_both_cores(): return lax.all_gather(array, 'section', axis_index_groups=of_chip)  25.4 us
    all_to_all x1, starting transfers between devices, local(): lax.all_to_all(packed, 'section', 0, 0, tiled=True, axis_index_groups=ove...  4.97 us
    all_to_all x1, starting transfers between devices, local(): lax.all_to_all(sums.reshape(members, 1, TOKENS), AXES, 0, 0, tiled=True,...  4.94 us
    pallas_call x1, Pallas kernels, local(): pl.pallas_call(teacher_kernel, out_shape=jax.ShapeDtypeStruct((chips, PAC...  2.1 us
    all_to_all x1, waiting for transfers between devices, local(): lax.all_to_all(sums.reshape(members, 1, TOKENS), AXES, 0, 0, tiled=True,...  1.86 us
    pallas_call x1, Pallas kernels, local(): pl.pallas_call(gradient_kernel, out_shape=(jax.ShapeDtypeStruct(student_q...  1.33 us
  transfers between devices with their start and end apart: 2, of which 1 were waited for; matrix products, arithmetic and copies ran while one was open for 0% of the time, Pallas kernels for 5%

profile of v10, /device:TPU:1, one launch (start us, length us, event | category | flops | bytes accessed | tf_op | source)
XLA Modules:
  0.0 44.8 jit_solution(5221100774671857307)
XLA Ops:
  0.6 2.1 %teacher.1 = f32[4,264,128]{2,1,0:T(8,128)} custom-call(s32[8]{0:T(128)} %pairing.3, s32[8]{0:T(128)} %placement.3, bf16[1,128,1024]{2,1,0:T(8,128)(2,1)} %q_ref.1, bf16[1,128,128]{2,1,0:T(8,128)(2,1)} %k_ref.1), custom_call_target="tpu_custom_call" | custom-call | flops 33554432 | bytes 400000 | tf_op jit(solution)/shard_map/teacher/pallas_call | solution.py:318
  2.7 0.0 copy-start.3
  2.7 0.0 copy-start.4
  2.8 5.0 %all-to-all-start = ((f32[4,264,128]{2,1,0:T(8,128)}), f32[4,264,128]{2,1,0:T(8,128)S(1)}, u32[]{:S(2)}, u32[]{:S(2)}) async-start(f32[4,264,128]{2,1,0:T(8,128)} %teacher.1), calls=%async_computation | async-start | bytes 1081344 | tf_op jit(solution)/shard_map/all_to_all | solution.py:330
  7.7 0.0 copy-done.3
  7.7 0.0 copy-done.4
  7.8 7.4 %all-gather = bf16[4,128,640]{2,1,0:T(8,128)(2,1)S(1)} all-gather(bf16[2,128,640]{2,1,0:T(8,128)(2,1)S(1)} %pad_maximum_fusion), channel_id=2, replica_groups={{0,64},{128,192},{256,320},{384,448},{1,65},{129,193},{257,321},{385,44..., dimensions={0}, use_global_device_ids=true | all-gather | bytes 983040 | tf_op jit(solution)/shard_map/all_gather | solution.py:334
  15.2 0.0 copy-start
  15.2 0.0 copy-start.1
  15.2 0.0 copy-start.2
  15.2 0.7 %copy-done = f32[8,4]{0,1:T(4,128)S(1)} copy-done((f32[8,4]{0,1:T(4,128)S(1)}, f32[8,4]{0,1:T(4,128)}, u32[]{:S(2)}) %copy-start) | copy-done | bytes 152
  15.9 0.0 copy-done.1
  15.9 0.0 copy-done.2
  15.9 0.8 %scores.1 = (f32[4,264,128]{2,1,0:T(8,128)S(1)}, f32[4,264,128]{2,1,0:T(8,128)S(1)}, s32[2,8]{1,0:T(2,128)S(1)}) custom-call(s32[8]{0:T(128)S(1)} %copy-done.1, s32[8]{0:T(128)S(1)} %copy-done.2, f32[4,8]{1,0:T(4,128)S(1)} %bitcast.15, bf16[2,2,128,640]{3,2,1,0:T(8,128)(2,1)S(1)} %bitcast.11), custom_call_target="tpu_custom_call" | custom-call | flops 33554432 | bytes 1400000 | tf_op jit(solution)/shard_map/scores/pallas_call | solution.py:339
  16.7 0.0 all-to-all-done.arrived_ref
  16.7 0.6 %student.1 = (f32[1,128]{1,0:T(1,128)S(1)}, bf16[544,128]{1,0:T(8,128)(2,1)S(1)}, bf16[544,128]{1,0:T(8,128)(2,1)S(1)}) custom-call(s32[2,8]{1,0:T(2,128)S(1)} %get-tuple-element.14.table, f32[4,264,128]{2,1,0:T(8,128)S(1)} %all-to-all-done.arrived_ref, f32[4,264,128]{2,1,0:T(8,128)S(1)} %get-tuple-element.15.raw_ref, ...), custom_call_target="tpu_custom_call" | custom-call | flops 33554432 | bytes 1800000 | tf_op jit(solution)/shard_map/student/pallas_call | solution.py:350
  17.3 6.1 %all-gather.4.pair_ref = f32[2,1,128]{2,1,0:T(1,128)S(1)} all-gather(f32[1,1,128]{2,1,0:T(1,128)S(1)} %bitcast.16), channel_id=4, replica_groups={{0,64},{128,192},{256,320},{384,448},{1,65},{129,193},{257,321},{385,44..., dimensions={0}, use_global_device_ids=true | all-gather | bytes 1536 | tf_op jit(solution)/shard_map/all_gather | solution.py:334
  23.4 0.6 %spread.1 = f32[32,128]{1,0:T(8,128)} custom-call(f32[2,1,128]{2,1,0:T(1,128)S(1)} %all-gather.4.pair_ref), custom_call_target="tpu_custom_call" | custom-call | tf_op jit(solution)/shard_map/spread/pallas_call | solution.py:364
  24.0 4.9 %all-to-all-start.1 = ((f32[32,1,128]{2,1,0:T(1,128)}), f32[32,1,128]{2,1,0:T(1,128)S(1)}, u32[]{:S(2)}, u32[]{:S(2)}) async-start(f32[32,1,128]{2,1,0:T(1,128)} %bitcast.7), calls=%async_computation.1 | async-start | bytes 32768 | tf_op jit(solution)/shard_map/all_to_all | solution.py:373
  29.0 5.4 %all-gather.1 = bf16[1088,128]{1,0:T(8,128)(2,1)S(1)} all-gather(bf16[544,128]{1,0:T(8,128)(2,1)S(1)} %get-tuple-element.18), channel_id=3, replica_groups={{0,64},{128,192},{256,320},{384,448},{1,65},{129,193},{257,321},{385,44..., dimensions={0}, use_global_device_ids=true | all-gather | bytes 417792 | tf_op jit(solution)/shard_map/all_gather | solution.py:334
  34.4 1.3 %gradient.1 = (bf16[1,2,128,512]{3,2,1,0:T(8,128)(2,1)}, bf16[1,2,128,128]{3,2,1,0:T(8,128)(2,1)}) custom-call(s32[2,8]{1,0:T(2,128)S(1)} %get-tuple-element.14.table, bf16[544,128]{1,0:T(8,128)(2,1)S(1)} %get-tuple-element.17.grad_ref, bf16[2,544,128]{2,1,0:T(8,128)(2,1)S(1)} %bitcast.13, bf16[2,2,128,640]{3,2,1,0:T(8,128)(2,1)S(1)} %bitcast.12), custom_call_target="tpu_custom_call" | custom-call | flops 67108864 | bytes 900000 | tf_op jit(solution)/shard_map/gradient/pallas_call | solution.py:376
  35.8 1.9 %all-to-all-done.1 = f32[32,1,128]{2,1,0:T(1,128)S(1)} async-done(((f32[32,1,128]{2,1,0:T(1,128)}), f32[32,1,128]{2,1,0:T(1,128)S(1)}, u32[]{:S(2)}, u32[]{:S(2)}) %all-to-all-start.1) | async-done | bytes 16416 | tf_op jit(solution)/shard_map/all_to_all | solution.py:373
  37.6 6.4 %all-gather.3 = f32[64,1,128]{2,1,0:T(1,128)S(1)} all-gather(f32[32,1,128]{2,1,0:T(1,128)S(1)} %all-to-all-done.1), channel_id=5, replica_groups={{0,64},{128,192},{256,320},{384,448},{1,65},{129,193},{257,321},{385,44..., dimensions={0}, use_global_device_ids=true | all-gather | bytes 49152 | tf_op jit(solution)/shard_map/all_gather | solution.py:334
  44.0 0.7 %final.1 = (f32[1,8]{1,0:T(1,128)}, f32[4,8]{1,0:T(4,128)}) custom-call(f32[2,32,128]{2,1,0:T(8,128)S(1)} %bitcast.14), custom_call_target="tpu_custom_call" | custom-call | tf_op jit(solution)/shard_map/final/pallas_call | solution.py:390
  (1 shorter events, 0.0 us)
Async XLA Ops:
  2.7 5.0 %copy-start.3 = (bf16[1,2,128,512]{3,2,1,0:T(8,128)(2,1)S(1)}, bf16[1,2,128,512]{3,2,1,0:T(8,128)(2,1)}, u32[]{:S(2)}) copy-start(bf16[1,2,128,512]{3,2,1,0:T(8,128)(2,1)} %param.9) | copy-start | bytes 786436
  2.7 5.0 %copy-start.4 = (bf16[1,2,128,128]{3,2,1,0:T(8,128)(2,1)S(1)}, bf16[1,2,128,128]{3,2,1,0:T(8,128)(2,1)}, u32[]{:S(2)}) copy-start(bf16[1,2,128,128]{3,2,1,0:T(8,128)(2,1)} %param.10) | copy-start | bytes 196612
  2.8 13.9 %all-to-all-start = ((f32[4,264,128]{2,1,0:T(8,128)}), f32[4,264,128]{2,1,0:T(8,128)S(1)}, u32[]{:S(2)}, u32[]{:S(2)}) async-start(f32[4,264,128]{2,1,0:T(8,128)} %teacher.1), calls=%async_computation | async-start | bytes 1081344 | tf_op jit(solution)/shard_map/all_to_all | solution.py:330
  15.2 0.7 %copy-start = (f32[8,4]{0,1:T(4,128)S(1)}, f32[8,4]{0,1:T(4,128)}, u32[]{:S(2)}) copy-start(f32[8,4]{0,1:T(4,128)} %param.11) | copy-start | bytes 388
  15.2 0.7 %copy-start.1 = (s32[8]{0:T(128)S(1)}, s32[8]{0:T(128)}, u32[]{:S(2)}) copy-start(s32[8]{0:T(128)} %pairing.3) | copy-start | bytes 100
  15.2 0.7 %copy-start.2 = (s32[8]{0:T(128)S(1)}, s32[8]{0:T(128)}, u32[]{:S(2)}) copy-start(s32[8]{0:T(128)} %placement.3) | copy-start | bytes 100
  24.0 13.6 %all-to-all-start.1 = ((f32[32,1,128]{2,1,0:T(1,128)}), f32[32,1,128]{2,1,0:T(1,128)S(1)}, u32[]{:S(2)}, u32[]{:S(2)}) async-start(f32[32,1,128]{2,1,0:T(1,128)} %bitcast.7), calls=%async_computation.1 | async-start | bytes 32768 | tf_op jit(solution)/shard_map/all_to_all | solution.py:373

commit v11 on v10

--- a/solution.py
+++ b/solution.py
@@ -160,13 +160,11 @@
     for_my_layers(pairing, placement, work)
 
 
-def student_kernel(table, arrived_ref, raw_ref, logp_ref, sums_ref, grad_ref, sent_ref):
-    core = lax.rem(lax.axis_index("section"), 2)
+def student_kernel(table, arrived_ref, raw_ref, logp_ref, sums_ref):
     row, col = masks()
     lower = col <= row
     place = lax.broadcasted_iota(jnp.int32, (8, TOKENS), 0)
     lane = lax.broadcasted_iota(jnp.int32, (8, TOKENS), 1)
-    tail_row = lax.broadcasted_iota(jnp.int32, (TAIL, TOKENS), 0)
     sums_ref[...] = jnp.zeros_like(sums_ref)
 
     held = jnp.int32(0)
@@ -176,7 +174,6 @@
     def work(rank, carry):
         code = table[0, rank]
         layer, source_chip = code & 7, (code >> 3) & 3
-        home_core, slot = (code >> 5) & 1, code >> 6
 
         def terms(rows):
             target = arrived_ref[source_chip, rows, :]
@@ -185,26 +182,15 @@
             difference = jnp.exp(student_logp) - target
             return (
                 jnp.sum(target * (target_logp - student_logp), axis=0, keepdims=True),
-                difference,
                 difference * raw_ref[rank, rows, :],
             )
 
-        def scale_of(head):
-            at = PAIRS * TOKENS + HEADS + head
-            return raw_ref[rank, at : at + 1, :]
-
-        last, last_difference, last_moved = terms(slice(PAIRS * TOKENS, PACKED))
+        last, last_moved = terms(slice(PAIRS * TOKENS, PACKED))
         found = jnp.zeros((8, TOKENS), jnp.float32)
         divergence = last
-        tail = jnp.zeros((TAIL, TOKENS), jnp.float32)
-        pieces = []
         for pair in range(PAIRS):
-            one, difference, moved = terms(slice(pair * TOKENS, (pair + 1) * TOKENS))
+            one, moved = terms(slice(pair * TOKENS, (pair + 1) * TOKENS))
             divergence += one
-            first = scale_of(2 * pair)
-            second = scale_of(2 * pair + 1)
-            pieces.append(difference * jnp.where(lower, first, second))
-            tail = jnp.where(tail_row == pair, last_difference[pair : pair + 1] * second, tail)
             of_first = jnp.sum(jnp.where(lower, moved, 0.0), axis=0, keepdims=True)
             of_second = jnp.sum(jnp.where(lower, 0.0, moved), axis=0, keepdims=True)
             of_second += last_moved[pair : pair + 1]
@@ -215,6 +201,39 @@
         goes_to = jnp.where(place == 0, layer, SCALE_LANE + LAYERS * (place - 1) + layer)
         found = jnp.where((lane == goes_to) & (place <= HEADS), found, 0.0)
         sums_ref[...] += jnp.sum(found, axis=0, keepdims=True)
+        return carry
+
+    lax.fori_loop(0, held, work, 0)
+
+
+def slope_kernel(table, arrived_ref, raw_ref, logp_ref, grad_ref, sent_ref):
+    core = lax.rem(lax.axis_index("section"), 2)
+    row, col = masks()
+    lower = col <= row
+    tail_row = lax.broadcasted_iota(jnp.int32, (TAIL, TOKENS), 0)
+    held = jnp.int32(0)
+    for rank in range(2 * SLOTS):
+        held += (table[0, rank] >= 0).astype(jnp.int32)
+
+    def work(rank, carry):
+        code = table[0, rank]
+        source_chip, home_core, slot = (code >> 3) & 3, (code >> 5) & 1, code >> 6
+
+        def difference(rows):
+            return jnp.exp(logp_ref[rank, rows, :]) - arrived_ref[source_chip, rows, :]
+
+        def scale_of(head):
+            at = PAIRS * TOKENS + HEADS + head
+            return raw_ref[rank, at : at + 1, :]
+
+        last = difference(slice(PAIRS * TOKENS, PACKED))
+        tail = jnp.zeros((TAIL, TOKENS), jnp.float32)
+        pieces = []
+        for pair in range(PAIRS):
+            first, second = scale_of(2 * pair), scale_of(2 * pair + 1)
+            square = difference(slice(pair * TOKENS, (pair + 1) * TOKENS))
+            pieces.append(square * jnp.where(lower, first, second))
+            tail = jnp.where(tail_row == pair, last[pair : pair + 1] * second, tail)
         pieces.append(tail)
 
         def put(ref, at):
@@ -347,19 +366,26 @@
     )(pairing, placement, student_scale.T, chip_qk)
     table = kept(table)
 
-    sums, grads, sent = pl.pallas_call(
+    work_on = (table, *map(kept, (arrived, raw, logp)))
+    sums = pl.pallas_call(
         student_kernel,
-        out_shape=(
-            pltpu.VMEM((1, TOKENS), f32),
-            pltpu.VMEM((SENT, TOKENS), bf16),
-            pltpu.VMEM((SENT, TOKENS), bf16),
-        ),
+        out_shape=pltpu.VMEM((1, TOKENS), f32),
         in_specs=[SMEM, VMEM, VMEM, VMEM],
-        out_specs=(VMEM, VMEM, VMEM),
+        out_specs=VMEM,
         cost_estimate=cost(8 * 2 * TOKENS**3, 1_800_000),
         compiler_params=SMALL,
         name="student",
-    )(table, *map(kept, (arrived, raw, logp)))
+    )(*work_on)
+    packed_grads = pltpu.VMEM((SENT, TOKENS), bf16)
+    grads, sent = pl.pallas_call(
+        slope_kernel,
+        out_shape=(packed_grads, packed_grads),
+        in_specs=[SMEM, VMEM, VMEM, VMEM],
+        out_specs=(VMEM, VMEM),
+        cost_estimate=cost(8 * 2 * TOKENS**3, 1_800_000),
+        compiler_params=SMALL,
+        name="slope",
+    )(*work_on)
 
     sums = pl.pallas_call(
         spread_kernel,

time: 45 us -> 44.9 us (level)
  Pallas kernels: 6.11 us -> 8.13 us
  blocking collectives: 25.4 us -> 24.2 us
  waiting for transfers between devices: 1.86 us -> 1.04 us
    all_gather x4, blocking collectives: 25.4 us -> 24.2 us  [of_both_cores(): return lax.all_gather(array, 'section', axis_index_groups=of_chip)]
    pallas_call x1 -> x2, Pallas kernels: 0.57 us -> 1.55 us  [the longest x1 0.9 us: local(): pl.pallas_call(student_kernel, out_shape=pltpu.VMEM((1, TOKENS), f32), in...]
    all_to_all x1, waiting for transfers between devices: 1.86 us -> 1.04 us  [local(): lax.all_to_all(sums.reshape(members, 1, TOKENS), AXES, 0, 0, tiled=True,...]
    pallas_call x1, Pallas kernels: 0.78 us -> 1.58 us  [local(): pl.pallas_call(scores_kernel, out_shape=(squares, squares, pltpu.VMEM((2,...]
  transfers between devices with their start and end apart: 2 -> 2, of which waited for: 1 -> 1; matrix products, arithmetic and copies ran while one was open for 0% -> 0% of each run, Pallas kernels for 5% -> 9%
where the time goes in v11:
time: 44.9 us; the launch traced here: 44.6 us
  blocking collectives  24.2 us (54%)
  starting transfers between devices  9.77 us (22%)
  Pallas kernels  8.13 us (18%)
  waiting for transfers between devices  1.04 us (2%)
  local copies, waits for them, and re-layouts  0.7 us (2%)
  between operations  0.7 us (2%)
    all_gather x4, blocking collectives, of_both_cores(): return lax.all_gather(array, 'section', axis_index_groups=of_chip)  24.2 us
    all_to_all x1, starting transfers between devices, local(): lax.all_to_all(packed, 'section', 0, 0, tiled=True, axis_index_groups=ove...  4.99 us
    all_to_all x1, starting transfers between devices, local(): lax.all_to_all(sums.reshape(members, 1, TOKENS), AXES, 0, 0, tiled=True,...  4.78 us
    pallas_call x1, Pallas kernels, local(): pl.pallas_call(teacher_kernel, out_shape=jax.ShapeDtypeStruct((chips, PAC...  2.1 us
    pallas_call x1, Pallas kernels, local(): pl.pallas_call(scores_kernel, out_shape=(squares, squares, pltpu.VMEM((2,...  1.58 us
    pallas_call x1, Pallas kernels, local(): pl.pallas_call(gradient_kernel, out_shape=(jax.ShapeDtypeStruct(student_q...  1.57 us
    all_to_all x1, waiting for transfers between devices, local(): lax.all_to_all(sums.reshape(members, 1, TOKENS), AXES, 0, 0, tiled=True,...  1.04 us
  transfers between devices with their start and end apart: 2, of which 1 were waited for; matrix products, arithmetic and copies ran while one was open for 0% of the time, Pallas kernels for 9%

profile of v11, /device:TPU:1, one launch (start us, length us, event | category | flops | bytes accessed | tf_op | source)
XLA Modules:
  0.0 44.6 jit_solution(6580552254166200431)
XLA Ops:
  0.6 2.1 %teacher.1 = f32[4,264,128]{2,1,0:T(8,128)} custom-call(s32[8]{0:T(128)} %pairing.3, s32[8]{0:T(128)} %placement.3, bf16[1,128,1024]{2,1,0:T(8,128)(2,1)} %q_ref.1, bf16[1,128,128]{2,1,0:T(8,128)(2,1)} %k_ref.1), custom_call_target="tpu_custom_call" | custom-call | flops 33554432 | bytes 400000 | tf_op jit(solution)/shard_map/teacher/pallas_call | solution.py:337
  2.7 0.0 copy-start.3
  2.8 0.0 copy-start.4
  2.8 5.0 %all-to-all-start = ((f32[4,264,128]{2,1,0:T(8,128)}), f32[4,264,128]{2,1,0:T(8,128)S(1)}, u32[]{:S(2)}, u32[]{:S(2)}) async-start(f32[4,264,128]{2,1,0:T(8,128)} %teacher.1), calls=%async_computation | async-start | bytes 1081344 | tf_op jit(solution)/shard_map/all_to_all | solution.py:349
  7.8 0.0 copy-done.3
  7.8 0.0 copy-done.4
  7.8 7.4 %all-gather = bf16[4,128,640]{2,1,0:T(8,128)(2,1)S(1)} all-gather(bf16[2,128,640]{2,1,0:T(8,128)(2,1)S(1)} %pad_maximum_fusion), channel_id=2, replica_groups={{0,64},{128,192},{256,320},{384,448},{1,65},{129,193},{257,321},{385,44..., dimensions={0}, use_global_device_ids=true | all-gather | bytes 983040 | tf_op jit(solution)/shard_map/all_gather | solution.py:353
  15.2 0.0 copy-start
  15.2 0.0 copy-start.1
  15.2 0.0 copy-start.2
  15.2 0.7 %copy-done = f32[8,4]{0,1:T(4,128)S(1)} copy-done((f32[8,4]{0,1:T(4,128)S(1)}, f32[8,4]{0,1:T(4,128)}, u32[]{:S(2)}) %copy-start) | copy-done | bytes 152
  15.9 0.0 copy-done.1
  15.9 0.0 copy-done.2
  15.9 1.6 %scores.1 = (f32[4,264,128]{2,1,0:T(8,128)S(1)}, f32[4,264,128]{2,1,0:T(8,128)S(1)}, s32[2,8]{1,0:T(2,128)S(1)}) custom-call(s32[8]{0:T(128)S(1)} %copy-done.1, s32[8]{0:T(128)S(1)} %copy-done.2, f32[4,8]{1,0:T(4,128)S(1)} %bitcast.15, bf16[2,2,128,640]{3,2,1,0:T(8,128)(2,1)S(1)} %bitcast.11), custom_call_target="tpu_custom_call" | custom-call | flops 33554432 | bytes 1400000 | tf_op jit(solution)/shard_map/scores/pallas_call | solution.py:358
  17.5 0.0 all-to-all-done.arrived_ref
  17.5 0.9 %student.1 = f32[1,128]{1,0:T(1,128)S(1)} custom-call(s32[2,8]{1,0:T(2,128)S(1)} %get-tuple-element.13.table, f32[4,264,128]{2,1,0:T(8,128)S(1)} %all-to-all-done.arrived_ref, f32[4,264,128]{2,1,0:T(8,128)S(1)} %get-tuple-element.14.raw_ref, f32[4,264,128]{2,1,0:T(8,128)S(1)} %get-tuple-element.15.logp_ref), custom_call_target="tpu_custom_call" | custom-call | flops 33554432 | bytes 1800000 | tf_op jit(solution)/shard_map/student/pallas_call | solution.py:370
  18.4 5.0 %all-gather.4.pair_ref = f32[2,1,128]{2,1,0:T(1,128)S(1)} all-gather(f32[1,1,128]{2,1,0:T(1,128)S(1)} %bitcast.16), channel_id=4, replica_groups={{0,64},{128,192},{256,320},{384,448},{1,65},{129,193},{257,321},{385,44..., dimensions={0}, use_global_device_ids=true | all-gather | bytes 1536 | tf_op jit(solution)/shard_map/all_gather | solution.py:353
  23.4 0.6 %spread.1 = f32[32,128]{1,0:T(8,128)} custom-call(f32[2,1,128]{2,1,0:T(1,128)S(1)} %all-gather.4.pair_ref), custom_call_target="tpu_custom_call" | custom-call | tf_op jit(solution)/shard_map/spread/pallas_call | solution.py:390
  24.0 4.8 %all-to-all-start.1 = ((f32[32,1,128]{2,1,0:T(1,128)}), f32[32,1,128]{2,1,0:T(1,128)S(1)}, u32[]{:S(2)}, u32[]{:S(2)}) async-start(f32[32,1,128]{2,1,0:T(1,128)} %bitcast.7), calls=%async_computation.1 | async-start | bytes 32768 | tf_op jit(solution)/shard_map/all_to_all | solution.py:399
  28.8 0.7 %slope.1 = (bf16[544,128]{1,0:T(8,128)(2,1)S(1)}, bf16[544,128]{1,0:T(8,128)(2,1)S(1)}) custom-call(s32[2,8]{1,0:T(2,128)S(1)} %get-tuple-element.13.table, f32[4,264,128]{2,1,0:T(8,128)S(1)} %all-to-all-done.arrived_ref, f32[4,264,128]{2,1,0:T(8,128)S(1)} %get-tuple-element.14.raw_ref, f32[4,264,128]{2,1,0:T(8,128)S(1)} %get-tuple-element.15.logp_ref), custom_call_target="tpu_custom_call" | custom-call | flops 33554432 | bytes 1800000 | tf_op jit(solution)/shard_map/slope/pallas_call | solution.py:380
  29.5 5.4 %all-gather.1 = bf16[1088,128]{1,0:T(8,128)(2,1)S(1)} all-gather(bf16[544,128]{1,0:T(8,128)(2,1)S(1)} %get-tuple-element.17), channel_id=3, replica_groups={{0,64},{128,192},{256,320},{384,448},{1,65},{129,193},{257,321},{385,44..., dimensions={0}, use_global_device_ids=true | all-gather | bytes 417792 | tf_op jit(solution)/shard_map/all_gather | solution.py:353
  34.8 1.6 %gradient.1 = (bf16[1,2,128,512]{3,2,1,0:T(8,128)(2,1)}, bf16[1,2,128,128]{3,2,1,0:T(8,128)(2,1)}) custom-call(s32[2,8]{1,0:T(2,128)S(1)} %get-tuple-element.13.table, bf16[544,128]{1,0:T(8,128)(2,1)S(1)} %get-tuple-element.16.grad_ref, bf16[2,544,128]{2,1,0:T(8,128)(2,1)S(1)} %bitcast.13, bf16[2,2,128,640]{3,2,1,0:T(8,128)(2,1)S(1)} %bitcast.12), custom_call_target="tpu_custom_call" | custom-call | flops 67108864 | bytes 900000 | tf_op jit(solution)/shard_map/gradient/pallas_call | solution.py:402
  36.4 1.0 %all-to-all-done.1 = f32[32,1,128]{2,1,0:T(1,128)S(1)} async-done(((f32[32,1,128]{2,1,0:T(1,128)}), f32[32,1,128]{2,1,0:T(1,128)S(1)}, u32[]{:S(2)}, u32[]{:S(2)}) %all-to-all-start.1) | async-done | bytes 16416 | tf_op jit(solution)/shard_map/all_to_all | solution.py:399
  37.5 6.4 %all-gather.3 = f32[64,1,128]{2,1,0:T(1,128)S(1)} all-gather(f32[32,1,128]{2,1,0:T(1,128)S(1)} %all-to-all-done.1), channel_id=5, replica_groups={{0,64},{128,192},{256,320},{384,448},{1,65},{129,193},{257,321},{385,44..., dimensions={0}, use_global_device_ids=true | all-gather | bytes 49152 | tf_op jit(solution)/shard_map/all_gather | solution.py:353
  43.9 0.7 %final.1 = (f32[1,8]{1,0:T(1,128)}, f32[4,8]{1,0:T(4,128)}) custom-call(f32[2,32,128]{2,1,0:T(8,128)S(1)} %bitcast.14), custom_call_target="tpu_custom_call" | custom-call | tf_op jit(solution)/shard_map/final/pallas_call | solution.py:416
  (1 shorter events, 0.0 us)
Async XLA Ops:
  2.7 5.0 %copy-start.3 = (bf16[1,2,128,512]{3,2,1,0:T(8,128)(2,1)S(1)}, bf16[1,2,128,512]{3,2,1,0:T(8,128)(2,1)}, u32[]{:S(2)}) copy-start(bf16[1,2,128,512]{3,2,1,0:T(8,128)(2,1)} %param.9) | copy-start | bytes 786436
  2.8 5.0 %copy-start.4 = (bf16[1,2,128,128]{3,2,1,0:T(8,128)(2,1)S(1)}, bf16[1,2,128,128]{3,2,1,0:T(8,128)(2,1)}, u32[]{:S(2)}) copy-start(bf16[1,2,128,128]{3,2,1,0:T(8,128)(2,1)} %param.10) | copy-start | bytes 196612
  2.8 14.7 %all-to-all-start = ((f32[4,264,128]{2,1,0:T(8,128)}), f32[4,264,128]{2,1,0:T(8,128)S(1)}, u32[]{:S(2)}, u32[]{:S(2)}) async-start(f32[4,264,128]{2,1,0:T(8,128)} %teacher.1), calls=%async_computation | async-start | bytes 1081344 | tf_op jit(solution)/shard_map/all_to_all | solution.py:349
  15.2 0.7 %copy-start = (f32[8,4]{0,1:T(4,128)S(1)}, f32[8,4]{0,1:T(4,128)}, u32[]{:S(2)}) copy-start(f32[8,4]{0,1:T(4,128)} %param.11) | copy-start | bytes 388
  15.2 0.7 %copy-start.1 = (s32[8]{0:T(128)S(1)}, s32[8]{0:T(128)}, u32[]{:S(2)}) copy-start(s32[8]{0:T(128)} %pairing.3) | copy-start | bytes 100
  15.2 0.7 %copy-start.2 = (s32[8]{0:T(128)S(1)}, s32[8]{0:T(128)}, u32[]{:S(2)}) copy-start(s32[8]{0:T(128)} %placement.3) | copy-start | bytes 100
  24.0 13.4 %all-to-all-start.1 = ((f32[32,1,128]{2,1,0:T(1,128)}), f32[32,1,128]{2,1,0:T(1,128)S(1)}, u32[]{:S(2)}, u32[]{:S(2)}) async-start(f32[32,1,128]{2,1,0:T(1,128)} %bitcast.7), calls=%async_computation.1 | async-start | bytes 32768 | tf_op jit(solution)/shard_map/all_to_all | solution.py:399

commit v12 on v10

--- a/solution.py
+++ b/solution.py
@@ -90,6 +90,10 @@
         copy.wait()
 
 
+def arrival_core(source, chip):
+    return (source ^ (source >> 2) ^ (chip >> 1)) & 1
+
+
 def for_my_layers(pairing, placement, work):
     me = lax.axis_index("section")
     chip, core = me // 2, lax.rem(me, 2)
@@ -99,7 +103,7 @@
         home, source = placement[layer], pairing[layer]
         home_core = lax.rem(home, 2)
         here = home // 2 == chip
-        mine = here & (lax.rem(source, 2) == core)
+        mine = here & (arrival_core(source, chip) == core)
         slot = jnp.where(home_core == 0, slots[0], slots[1])
 
         @pl.when(mine)
@@ -254,7 +258,7 @@
 
         @pl.when(slot < held)
         def _():
-            direct = ((table[1, layers[slot]] >> 3) & 1) == core
+            direct = arrival_core(table[1, layers[slot]] >> 3, me // 2) == core
             key = qk_ref[core, slot, :, HEADS * HEAD_WIDTH :]
             total = jnp.zeros((TOKENS, HEAD_WIDTH), jnp.float32)
 
@@ -311,7 +315,7 @@
 
 def local(chips, groups, teacher_q, teacher_k, student_q, student_k, student_scale, pairing, placement):
     f32, bf16 = jnp.float32, jnp.bfloat16
-    over_x = [[2 * x + core for x in range(chips)] for core in range(2)]
+    over_x = [[2 * x + (core ^ (x // 2 & 1)) for x in range(chips)] for core in range(2)]
     of_chip = [[2 * x, 2 * x + 1] for x in range(chips)]
     members = len(groups[0])
 

time: 45 us -> 45.3 us (level)
  blocking collectives: 25.4 us -> 23.7 us
  starting transfers between devices: 9.91 us -> 11.3 us
  Pallas kernels: 6.11 us -> 6.93 us
    all_gather x4, blocking collectives: 25.4 us -> 23.7 us  [of_both_cores(): return lax.all_gather(array, 'section', axis_index_groups=of_chip)]
    all_to_all x1, starting transfers between devices: 4.94 us -> 5.71 us  [local(): lax.all_to_all(sums.reshape(members, 1, TOKENS), AXES, 0, 0, tiled=True,...]
    all_to_all x1, starting transfers between devices: 4.97 us -> 5.55 us  [local(): lax.all_to_all(packed, 'section', 0, 0, tiled=True, axis_index_groups=ove...]
  transfers between devices with their start and end apart: 2 -> 2, of which waited for: 1 -> 1; matrix products, arithmetic and copies ran while one was open for 0% -> 0% of each run, Pallas kernels for 5% -> 6%
where the time goes in v12:
time: 45.3 us; the launch traced here: 45 us
  blocking collectives  23.7 us (52%)
  starting transfers between devices  11.3 us (25%)
  Pallas kernels  6.93 us (15%)
  waiting for transfers between devices  1.71 us (4%)
  local copies, waits for them, and re-layouts  0.7 us (2%)
  between operations  0.7 us (2%)
    all_gather x4, blocking collectives, of_both_cores(): return lax.all_gather(array, 'section', axis_index_groups=of_chip)  23.7 us
    all_to_all x1, starting transfers between devices, local(): lax.all_to_all(sums.reshape(members, 1, TOKENS), AXES, 0, 0, tiled=True,...  5.71 us
    all_to_all x1, starting transfers between devices, local(): lax.all_to_all(packed, 'section', 0, 0, tiled=True, axis_index_groups=ove...  5.55 us
    pallas_call x1, Pallas kernels, local(): pl.pallas_call(teacher_kernel, out_shape=jax.ShapeDtypeStruct((chips, PAC...  2.08 us
    all_to_all x1, waiting for transfers between devices, local(): lax.all_to_all(sums.reshape(members, 1, TOKENS), AXES, 0, 0, tiled=True,...  1.71 us
    pallas_call x1, Pallas kernels, local(): pl.pallas_call(gradient_kernel, out_shape=(jax.ShapeDtypeStruct(student_q...  1.58 us
    pallas_call x1, Pallas kernels, local(): pl.pallas_call(scores_kernel, out_shape=(squares, squares, pltpu.VMEM((2,...  1.18 us
  transfers between devices with their start and end apart: 2, of which 1 were waited for; matrix products, arithmetic and copies ran while one was open for 0% of the time, Pallas kernels for 6%

profile of v12, /device:TPU:1, one launch (start us, length us, event | category | flops | bytes accessed | tf_op | source)
XLA Modules:
  0.0 45.0 jit_solution(16386163424586834615)
XLA Ops:
  0.6 2.1 %teacher.1 = f32[4,264,128]{2,1,0:T(8,128)} custom-call(s32[8]{0:T(128)} %pairing.3, s32[8]{0:T(128)} %placement.3, bf16[1,128,1024]{2,1,0:T(8,128)(2,1)} %q_ref.1, bf16[1,128,128]{2,1,0:T(8,128)(2,1)} %k_ref.1), custom_call_target="tpu_custom_call" | custom-call | flops 33554432 | bytes 400000 | tf_op jit(solution)/shard_map/teacher/pallas_call | solution.py:322
  2.7 0.0 copy-start.3
  2.7 0.0 copy-start.4
  2.7 5.5 %all-to-all-start = ((f32[4,264,128]{2,1,0:T(8,128)}), f32[4,264,128]{2,1,0:T(8,128)S(1)}, u32[]{:S(2)}, u32[]{:S(2)}) async-start(f32[4,264,128]{2,1,0:T(8,128)} %teacher.1), calls=%async_computation | async-start | bytes 1081344 | tf_op jit(solution)/shard_map/all_to_all | solution.py:334
  8.3 0.0 copy-done.3
  8.3 0.0 copy-done.4
  8.3 6.9 %all-gather = bf16[4,128,640]{2,1,0:T(8,128)(2,1)S(1)} all-gather(bf16[2,128,640]{2,1,0:T(8,128)(2,1)S(1)} %pad_maximum_fusion), channel_id=2, replica_groups={{0,64},{128,192},{256,320},{384,448},{1,65},{129,193},{257,321},{385,44..., dimensions={0}, use_global_device_ids=true | all-gather | bytes 983040 | tf_op jit(solution)/shard_map/all_gather | solution.py:338
  15.2 0.0 copy-start
  15.2 0.0 copy-start.1
  15.2 0.0 copy-start.2
  15.2 0.7 %copy-done = f32[8,4]{0,1:T(4,128)S(1)} copy-done((f32[8,4]{0,1:T(4,128)S(1)}, f32[8,4]{0,1:T(4,128)}, u32[]{:S(2)}) %copy-start) | copy-done | bytes 152
  15.9 0.0 copy-done.1
  15.9 0.0 copy-done.2
  15.9 1.2 %scores.1 = (f32[4,264,128]{2,1,0:T(8,128)S(1)}, f32[4,264,128]{2,1,0:T(8,128)S(1)}, s32[2,8]{1,0:T(2,128)S(1)}) custom-call(s32[8]{0:T(128)S(1)} %copy-done.1, s32[8]{0:T(128)S(1)} %copy-done.2, f32[4,8]{1,0:T(4,128)S(1)} %bitcast.15, bf16[2,2,128,640]{3,2,1,0:T(8,128)(2,1)S(1)} %bitcast.11), custom_call_target="tpu_custom_call" | custom-call | flops 33554432 | bytes 1400000 | tf_op jit(solution)/shard_map/scores/pallas_call | solution.py:343
  17.1 0.0 all-to-all-done.arrived_ref
  17.1 0.8 %student.1 = (f32[1,128]{1,0:T(1,128)S(1)}, bf16[544,128]{1,0:T(8,128)(2,1)S(1)}, bf16[544,128]{1,0:T(8,128)(2,1)S(1)}) custom-call(s32[2,8]{1,0:T(2,128)S(1)} %get-tuple-element.14.table, f32[4,264,128]{2,1,0:T(8,128)S(1)} %all-to-all-done.arrived_ref, f32[4,264,128]{2,1,0:T(8,128)S(1)} %get-tuple-element.15.raw_ref, ...), custom_call_target="tpu_custom_call" | custom-call | flops 33554432 | bytes 1800000 | tf_op jit(solution)/shard_map/student/pallas_call | solution.py:354
  17.9 5.2 %all-gather.4.pair_ref = f32[2,1,128]{2,1,0:T(1,128)S(1)} all-gather(f32[1,1,128]{2,1,0:T(1,128)S(1)} %bitcast.16), channel_id=4, replica_groups={{0,64},{128,192},{256,320},{384,448},{1,65},{129,193},{257,321},{385,44..., dimensions={0}, use_global_device_ids=true | all-gather | bytes 1536 | tf_op jit(solution)/shard_map/all_gather | solution.py:338
  23.0 0.6 %spread.1 = f32[32,128]{1,0:T(8,128)} custom-call(f32[2,1,128]{2,1,0:T(1,128)S(1)} %all-gather.4.pair_ref), custom_call_target="tpu_custom_call" | custom-call | tf_op jit(solution)/shard_map/spread/pallas_call | solution.py:368
  23.6 5.7 %all-to-all-start.1 = ((f32[32,1,128]{2,1,0:T(1,128)}), f32[32,1,128]{2,1,0:T(1,128)S(1)}, u32[]{:S(2)}, u32[]{:S(2)}) async-start(f32[32,1,128]{2,1,0:T(1,128)} %bitcast.7), calls=%async_computation.1 | async-start | bytes 32768 | tf_op jit(solution)/shard_map/all_to_all | solution.py:377
  29.4 5.3 %all-gather.1 = bf16[1088,128]{1,0:T(8,128)(2,1)S(1)} all-gather(bf16[544,128]{1,0:T(8,128)(2,1)S(1)} %get-tuple-element.18), channel_id=3, replica_groups={{0,64},{128,192},{256,320},{384,448},{1,65},{129,193},{257,321},{385,44..., dimensions={0}, use_global_device_ids=true | all-gather | bytes 417792 | tf_op jit(solution)/shard_map/all_gather | solution.py:338
  34.7 1.6 %gradient.1 = (bf16[1,2,128,512]{3,2,1,0:T(8,128)(2,1)}, bf16[1,2,128,128]{3,2,1,0:T(8,128)(2,1)}) custom-call(s32[2,8]{1,0:T(2,128)S(1)} %get-tuple-element.14.table, bf16[544,128]{1,0:T(8,128)(2,1)S(1)} %get-tuple-element.17.grad_ref, bf16[2,544,128]{2,1,0:T(8,128)(2,1)S(1)} %bitcast.13, bf16[2,2,128,640]{3,2,1,0:T(8,128)(2,1)S(1)} %bitcast.12), custom_call_target="tpu_custom_call" | custom-call | flops 67108864 | bytes 900000 | tf_op jit(solution)/shard_map/gradient/pallas_call | solution.py:380
  36.3 1.7 %all-to-all-done.1 = f32[32,1,128]{2,1,0:T(1,128)S(1)} async-done(((f32[32,1,128]{2,1,0:T(1,128)}), f32[32,1,128]{2,1,0:T(1,128)S(1)}, u32[]{:S(2)}, u32[]{:S(2)}) %all-to-all-start.1) | async-done | bytes 16416 | tf_op jit(solution)/shard_map/all_to_all | solution.py:377
  38.0 6.3 %all-gather.3 = f32[64,1,128]{2,1,0:T(1,128)S(1)} all-gather(f32[32,1,128]{2,1,0:T(1,128)S(1)} %all-to-all-done.1), channel_id=5, replica_groups={{0,64},{128,192},{256,320},{384,448},{1,65},{129,193},{257,321},{385,44..., dimensions={0}, use_global_device_ids=true | all-gather | bytes 49152 | tf_op jit(solution)/shard_map/all_gather | solution.py:338
  44.3 0.7 %final.1 = (f32[1,8]{1,0:T(1,128)}, f32[4,8]{1,0:T(4,128)}) custom-call(f32[2,32,128]{2,1,0:T(8,128)S(1)} %bitcast.14), custom_call_target="tpu_custom_call" | custom-call | tf_op jit(solution)/shard_map/final/pallas_call | solution.py:394
  (1 shorter events, 0.0 us)
Async XLA Ops:
  2.7 5.6 %copy-start.3 = (bf16[1,2,128,512]{3,2,1,0:T(8,128)(2,1)S(1)}, bf16[1,2,128,512]{3,2,1,0:T(8,128)(2,1)}, u32[]{:S(2)}) copy-start(bf16[1,2,128,512]{3,2,1,0:T(8,128)(2,1)} %param.9) | copy-start | bytes 786436
  2.7 5.6 %copy-start.4 = (bf16[1,2,128,128]{3,2,1,0:T(8,128)(2,1)S(1)}, bf16[1,2,128,128]{3,2,1,0:T(8,128)(2,1)}, u32[]{:S(2)}) copy-start(bf16[1,2,128,128]{3,2,1,0:T(8,128)(2,1)} %param.10) | copy-start | bytes 196612
  2.7 14.3 %all-to-all-start = ((f32[4,264,128]{2,1,0:T(8,128)}), f32[4,264,128]{2,1,0:T(8,128)S(1)}, u32[]{:S(2)}, u32[]{:S(2)}) async-start(f32[4,264,128]{2,1,0:T(8,128)} %teacher.1), calls=%async_computation | async-start | bytes 1081344 | tf_op jit(solution)/shard_map/all_to_all | solution.py:334
  15.2 0.7 %copy-start = (f32[8,4]{0,1:T(4,128)S(1)}, f32[8,4]{0,1:T(4,128)}, u32[]{:S(2)}) copy-start(f32[8,4]{0,1:T(4,128)} %param.11) | copy-start | bytes 388
  15.2 0.7 %copy-start.1 = (s32[8]{0:T(128)S(1)}, s32[8]{0:T(128)}, u32[]{:S(2)}) copy-start(s32[8]{0:T(128)} %pairing.3) | copy-start | bytes 100
  15.2 0.7 %copy-start.2 = (s32[8]{0:T(128)S(1)}, s32[8]{0:T(128)}, u32[]{:S(2)}) copy-start(s32[8]{0:T(128)} %placement.3) | copy-start | bytes 100
  23.6 14.3 %all-to-all-start.1 = ((f32[32,1,128]{2,1,0:T(1,128)}), f32[32,1,128]{2,1,0:T(1,128)S(1)}, u32[]{:S(2)}, u32[]{:S(2)}) async-start(f32[32,1,128]{2,1,0:T(1,128)} %bitcast.7), calls=%async_computation.1 | async-start | bytes 32768 | tf_op jit(solution)/shard_map/all_to_all | solution.py:377

commit v13 on v10

--- a/solution.py
+++ b/solution.py
@@ -287,9 +287,9 @@
 
 
 def final_kernel(rows_ref, kl_ref, scale_ref):
-    divergence = jnp.sum(rows_ref[0], axis=0, keepdims=True)
+    divergence = jnp.sum(rows_ref[1], axis=0, keepdims=True)
     kl_ref[...] = divergence[:, :LAYERS] / (STUDENT_HEADS * TOKENS)
-    terms = jnp.sum(rows_ref[1], axis=0, keepdims=True)
+    terms = jnp.sum(rows_ref[0], axis=0, keepdims=True)
     scale_ref[...] = jnp.concatenate(
         [terms[:, SCALE_LANE + LAYERS * h : SCALE_LANE + LAYERS * (h + 1)] for h in range(HEADS)], axis=0
     )
@@ -407,10 +407,10 @@
 
     chips = range(sections // 2)
     first = [
-        [flat(2 * x, h, d) for x in chips for h in range(heads)] for d in range(replicas)
+        [flat(2 * x + 1, h, d) for x in chips for h in range(heads)] for d in range(replicas)
     ]
     second = [
-        [flat(2 * x + 1, h, d) for x in chips for d in range(replicas)] for h in range(heads)
+        [flat(2 * x, h, d) for x in chips for d in range(replicas)] for h in range(heads)
     ]
     return first + second
 

time: 45 us -> 43.8 us (0.973)
  blocking collectives: 25.4 us -> 15.6 us
  starting transfers between devices: 9.91 us -> 13.1 us
  waiting for transfers between devices: 1.86 us -> 4.8 us
  Pallas kernels: 6.11 us -> 8.37 us
    all_gather x4, blocking collectives: 25.4 us -> 15.6 us  [of_both_cores(): return lax.all_gather(array, 'section', axis_index_groups=of_chip)]
    all_to_all x1, starting transfers between devices: 4.94 us -> 8.16 us  [local(): lax.all_to_all(sums.reshape(members, 1, TOKENS), AXES, 0, 0, tiled=True,...]
    all_to_all x1, waiting for transfers between devices: 1.86 us -> 4.8 us  [local(): lax.all_to_all(sums.reshape(members, 1, TOKENS), AXES, 0, 0, tiled=True,...]
    pallas_call x1, Pallas kernels: 0.78 us -> 1.98 us  [local(): pl.pallas_call(scores_kernel, out_shape=(squares, squares, pltpu.VMEM((2,...]
    pallas_call x1, Pallas kernels: 0.57 us -> 1.14 us  [local(): pl.pallas_call(student_kernel, out_shape=(pltpu.VMEM((1, TOKENS), f32), p...]
    pallas_call x1, Pallas kernels: 1.33 us -> 1.82 us  [local(): pl.pallas_call(gradient_kernel, out_shape=(jax.ShapeDtypeStruct(student_q...]
  transfers between devices with their start and end apart: 2 -> 2, of which waited for: 1 -> 1; matrix products, arithmetic and copies ran while one was open for 0% -> 0% of each run, Pallas kernels for 5% -> 9%
where the time goes in v13:
time: 43.8 us; the launch traced here: 43.4 us
  blocking collectives  15.6 us (36%)
  starting transfers between devices  13.1 us (30%)
  Pallas kernels  8.37 us (19%)
  waiting for transfers between devices  4.8 us (11%)
  local copies, waits for them, and re-layouts  0.7 us (2%)
  between operations  0.69 us (2%)
    all_gather x4, blocking collectives, of_both_cores(): return lax.all_gather(array, 'section', axis_index_groups=of_chip)  15.6 us
    all_to_all x1, starting transfers between devices, local(): lax.all_to_all(sums.reshape(members, 1, TOKENS), AXES, 0, 0, tiled=True,...  8.16 us
    all_to_all x1, starting transfers between devices, local(): lax.all_to_all(packed, 'section', 0, 0, tiled=True, axis_index_groups=ove...  4.97 us
    all_to_all x1, waiting for transfers between devices, local(): lax.all_to_all(sums.reshape(members, 1, TOKENS), AXES, 0, 0, tiled=True,...  4.8 us
    pallas_call x1, Pallas kernels, local(): pl.pallas_call(teacher_kernel, out_shape=jax.ShapeDtypeStruct((chips, PAC...  2.1 us
    pallas_call x1, Pallas kernels, local(): pl.pallas_call(scores_kernel, out_shape=(squares, squares, pltpu.VMEM((2,...  1.98 us
    pallas_call x1, Pallas kernels, local(): pl.pallas_call(gradient_kernel, out_shape=(jax.ShapeDtypeStruct(student_q...  1.82 us
    pallas_call x1, Pallas kernels, local(): pl.pallas_call(student_kernel, out_shape=(pltpu.VMEM((1, TOKENS), f32), p...  1.14 us
  transfers between devices with their start and end apart: 2, of which 1 were waited for; matrix products, arithmetic and copies ran while one was open for 0% of the time, Pallas kernels for 9%

profile of v13, /device:TPU:1, one launch (start us, length us, event | category | flops | bytes accessed | tf_op | source)
XLA Modules:
  0.0 43.4 jit_solution(10936970153926064160)
XLA Ops:
  0.6 2.1 %teacher.1 = f32[4,264,128]{2,1,0:T(8,128)} custom-call(s32[8]{0:T(128)} %pairing.3, s32[8]{0:T(128)} %placement.3, bf16[1,128,1024]{2,1,0:T(8,128)(2,1)} %q_ref.1, bf16[1,128,128]{2,1,0:T(8,128)(2,1)} %k_ref.1), custom_call_target="tpu_custom_call" | custom-call | flops 33554432 | bytes 400000 | tf_op jit(solution)/shard_map/teacher/pallas_call | solution.py:318
  2.7 0.0 copy-start.3
  2.8 0.0 copy-start.4
  2.8 5.0 %all-to-all-start = ((f32[4,264,128]{2,1,0:T(8,128)}), f32[4,264,128]{2,1,0:T(8,128)S(1)}, u32[]{:S(2)}, u32[]{:S(2)}) async-start(f32[4,264,128]{2,1,0:T(8,128)} %teacher.1), calls=%async_computation | async-start | bytes 1081344 | tf_op jit(solution)/shard_map/all_to_all | solution.py:330
  7.7 0.0 copy-done.3
  7.7 0.0 copy-done.4
  7.8 7.4 %all-gather = bf16[4,128,640]{2,1,0:T(8,128)(2,1)S(1)} all-gather(bf16[2,128,640]{2,1,0:T(8,128)(2,1)S(1)} %pad_maximum_fusion), channel_id=2, replica_groups={{0,64},{128,192},{256,320},{384,448},{1,65},{129,193},{257,321},{385,44..., dimensions={0}, use_global_device_ids=true | all-gather | bytes 983040 | tf_op jit(solution)/shard_map/all_gather | solution.py:334
  15.2 0.0 copy-start
  15.2 0.0 copy-start.1
  15.2 0.0 copy-start.2
  15.2 0.7 %copy-done = f32[8,4]{0,1:T(4,128)S(1)} copy-done((f32[8,4]{0,1:T(4,128)S(1)}, f32[8,4]{0,1:T(4,128)}, u32[]{:S(2)}) %copy-start) | copy-done | bytes 152
  15.9 0.0 copy-done.1
  15.9 0.0 copy-done.2
  15.9 2.0 %scores.1 = (f32[4,264,128]{2,1,0:T(8,128)S(1)}, f32[4,264,128]{2,1,0:T(8,128)S(1)}, s32[2,8]{1,0:T(2,128)S(1)}) custom-call(s32[8]{0:T(128)S(1)} %copy-done.1, s32[8]{0:T(128)S(1)} %copy-done.2, f32[4,8]{1,0:T(4,128)S(1)} %bitcast.15, bf16[2,2,128,640]{3,2,1,0:T(8,128)(2,1)S(1)} %bitcast.11), custom_call_target="tpu_custom_call" | custom-call | flops 33554432 | bytes 1400000 | tf_op jit(solution)/shard_map/scores/pallas_call | solution.py:339
  17.9 0.0 all-to-all-done.arrived_ref
  17.9 1.1 %student.1 = (f32[1,128]{1,0:T(1,128)S(1)}, bf16[544,128]{1,0:T(8,128)(2,1)S(1)}, bf16[544,128]{1,0:T(8,128)(2,1)S(1)}) custom-call(s32[2,8]{1,0:T(2,128)S(1)} %get-tuple-element.14.table, f32[4,264,128]{2,1,0:T(8,128)S(1)} %all-to-all-done.arrived_ref, f32[4,264,128]{2,1,0:T(8,128)S(1)} %get-tuple-element.15.raw_ref, ...), custom_call_target="tpu_custom_call" | custom-call | flops 33554432 | bytes 1800000 | tf_op jit(solution)/shard_map/student/pallas_call | solution.py:350
  19.0 4.4 %all-gather.4.pair_ref = f32[2,1,128]{2,1,0:T(1,128)S(1)} all-gather(f32[1,1,128]{2,1,0:T(1,128)S(1)} %bitcast.16), channel_id=4, replica_groups={{0,64},{128,192},{256,320},{384,448},{1,65},{129,193},{257,321},{385,44..., dimensions={0}, use_global_device_ids=true | all-gather | bytes 1536 | tf_op jit(solution)/shard_map/all_gather | solution.py:334
  23.4 0.6 %spread.1 = f32[32,128]{1,0:T(8,128)} custom-call(f32[2,1,128]{2,1,0:T(1,128)S(1)} %all-gather.4.pair_ref), custom_call_target="tpu_custom_call" | custom-call | tf_op jit(solution)/shard_map/spread/pallas_call | solution.py:364
  24.0 8.2 %all-to-all-start.1 = ((f32[32,1,128]{2,1,0:T(1,128)}), f32[32,1,128]{2,1,0:T(1,128)S(1)}, u32[]{:S(2)}, u32[]{:S(2)}) async-start(f32[32,1,128]{2,1,0:T(1,128)} %bitcast.7), calls=%async_computation.1 | async-start | bytes 32768 | tf_op jit(solution)/shard_map/all_to_all | solution.py:373
  32.2 2.0 %all-gather.1 = bf16[1088,128]{1,0:T(8,128)(2,1)S(1)} all-gather(bf16[544,128]{1,0:T(8,128)(2,1)S(1)} %get-tuple-element.18), channel_id=3, replica_groups={{0,64},{128,192},{256,320},{384,448},{1,65},{129,193},{257,321},{385,44..., dimensions={0}, use_global_device_ids=true | all-gather | bytes 417792 | tf_op jit(solution)/shard_map/all_gather | solution.py:334
  34.2 1.8 %gradient.1 = (bf16[1,2,128,512]{3,2,1,0:T(8,128)(2,1)}, bf16[1,2,128,128]{3,2,1,0:T(8,128)(2,1)}) custom-call(s32[2,8]{1,0:T(2,128)S(1)} %get-tuple-element.14.table, bf16[544,128]{1,0:T(8,128)(2,1)S(1)} %get-tuple-element.17.grad_ref, bf16[2,544,128]{2,1,0:T(8,128)(2,1)S(1)} %bitcast.13, bf16[2,2,128,640]{3,2,1,0:T(8,128)(2,1)S(1)} %bitcast.12), custom_call_target="tpu_custom_call" | custom-call | flops 67108864 | bytes 900000 | tf_op jit(solution)/shard_map/gradient/pallas_call | solution.py:376
  36.0 4.8 %all-to-all-done.1 = f32[32,1,128]{2,1,0:T(1,128)S(1)} async-done(((f32[32,1,128]{2,1,0:T(1,128)}), f32[32,1,128]{2,1,0:T(1,128)S(1)}, u32[]{:S(2)}, u32[]{:S(2)}) %all-to-all-start.1) | async-done | bytes 16416 | tf_op jit(solution)/shard_map/all_to_all | solution.py:373
  40.8 1.8 %all-gather.3 = f32[64,1,128]{2,1,0:T(1,128)S(1)} all-gather(f32[32,1,128]{2,1,0:T(1,128)S(1)} %all-to-all-done.1), channel_id=5, replica_groups={{0,64},{128,192},{256,320},{384,448},{1,65},{129,193},{257,321},{385,44..., dimensions={0}, use_global_device_ids=true | all-gather | bytes 49152 | tf_op jit(solution)/shard_map/all_gather | solution.py:334
  42.6 0.7 %final.1 = (f32[1,8]{1,0:T(1,128)}, f32[4,8]{1,0:T(4,128)}) custom-call(f32[2,32,128]{2,1,0:T(8,128)S(1)} %bitcast.14), custom_call_target="tpu_custom_call" | custom-call | tf_op jit(solution)/shard_map/final/pallas_call | solution.py:390
  (1 shorter events, 0.0 us)
Async XLA Ops:
  2.7 5.0 %copy-start.3 = (bf16[1,2,128,512]{3,2,1,0:T(8,128)(2,1)S(1)}, bf16[1,2,128,512]{3,2,1,0:T(8,128)(2,1)}, u32[]{:S(2)}) copy-start(bf16[1,2,128,512]{3,2,1,0:T(8,128)(2,1)} %param.9) | copy-start | bytes 786436
  2.8 5.0 %copy-start.4 = (bf16[1,2,128,128]{3,2,1,0:T(8,128)(2,1)S(1)}, bf16[1,2,128,128]{3,2,1,0:T(8,128)(2,1)}, u32[]{:S(2)}) copy-start(bf16[1,2,128,128]{3,2,1,0:T(8,128)(2,1)} %param.10) | copy-start | bytes 196612
  2.8 15.1 %all-to-all-start = ((f32[4,264,128]{2,1,0:T(8,128)}), f32[4,264,128]{2,1,0:T(8,128)S(1)}, u32[]{:S(2)}, u32[]{:S(2)}) async-start(f32[4,264,128]{2,1,0:T(8,128)} %teacher.1), calls=%async_computation | async-start | bytes 1081344 | tf_op jit(solution)/shard_map/all_to_all | solution.py:330
  15.2 0.7 %copy-start = (f32[8,4]{0,1:T(4,128)S(1)}, f32[8,4]{0,1:T(4,128)}, u32[]{:S(2)}) copy-start(f32[8,4]{0,1:T(4,128)} %param.11) | copy-start | bytes 388
  15.2 0.7 %copy-start.1 = (s32[8]{0:T(128)S(1)}, s32[8]{0:T(128)}, u32[]{:S(2)}) copy-start(s32[8]{0:T(128)} %pairing.3) | copy-start | bytes 100
  15.2 0.7 %copy-start.2 = (s32[8]{0:T(128)S(1)}, s32[8]{0:T(128)}, u32[]{:S(2)}) copy-start(s32[8]{0:T(128)} %placement.3) | copy-start | bytes 100
  24.0 16.8 %all-to-all-start.1 = ((f32[32,1,128]{2,1,0:T(1,128)}), f32[32,1,128]{2,1,0:T(1,128)S(1)}, u32[]{:S(2)}, u32[]{:S(2)}) async-start(f32[32,1,128]{2,1,0:T(1,128)} %bitcast.7), calls=%async_computation.1 | async-start | bytes 32768 | tf_op jit(solution)/shard_map/all_to_all | solution.py:373

commit v14 on v11

--- a/solution.py
+++ b/solution.py
@@ -306,9 +306,9 @@
 
 
 def final_kernel(rows_ref, kl_ref, scale_ref):
-    divergence = jnp.sum(rows_ref[0], axis=0, keepdims=True)
+    divergence = jnp.sum(rows_ref[1], axis=0, keepdims=True)
     kl_ref[...] = divergence[:, :LAYERS] / (STUDENT_HEADS * TOKENS)
-    terms = jnp.sum(rows_ref[1], axis=0, keepdims=True)
+    terms = jnp.sum(rows_ref[0], axis=0, keepdims=True)
     scale_ref[...] = jnp.concatenate(
         [terms[:, SCALE_LANE + LAYERS * h : SCALE_LANE + LAYERS * (h + 1)] for h in range(HEADS)], axis=0
     )
@@ -433,10 +433,10 @@
 
     chips = range(sections // 2)
     first = [
-        [flat(2 * x, h, d) for x in chips for h in range(heads)] for d in range(replicas)
+        [flat(2 * x + 1, h, d) for x in chips for h in range(heads)] for d in range(replicas)
     ]
     second = [
-        [flat(2 * x + 1, h, d) for x in chips for d in range(replicas)] for h in range(heads)
+        [flat(2 * x, h, d) for x in chips for d in range(replicas)] for h in range(heads)
     ]
     return first + second
 

time: 44.9 us -> 43.8 us (0.976)
  blocking collectives: 24.2 us -> 17 us
  waiting for transfers between devices: 1.04 us -> 4.67 us
  starting transfers between devices: 9.77 us -> 13 us
  Pallas kernels: 8.13 us -> 7.27 us
    all_gather x4, blocking collectives: 24.2 us -> 17 us  [of_both_cores(): return lax.all_gather(array, 'section', axis_index_groups=of_chip)]
    all_to_all x1, waiting for transfers between devices: 1.04 us -> 4.67 us  [local(): lax.all_to_all(sums.reshape(members, 1, TOKENS), AXES, 0, 0, tiled=True,...]
    all_to_all x1, starting transfers between devices: 4.78 us -> 7.99 us  [local(): lax.all_to_all(sums.reshape(members, 1, TOKENS), AXES, 0, 0, tiled=True,...]
  transfers between devices with their start and end apart: 2 -> 2, of which waited for: 1 -> 1; matrix products, arithmetic and copies ran while one was open for 0% -> 0% of each run, Pallas kernels for 9% -> 7%
where the time goes in v14:
time: 43.8 us; the launch traced here: 43.4 us
  blocking collectives  17 us (39%)
  starting transfers between devices  13 us (30%)
  Pallas kernels  7.27 us (17%)
  waiting for transfers between devices  4.67 us (11%)
  local copies, waits for them, and re-layouts  0.7 us (2%)
  between operations  0.7 us (2%)
    all_gather x4, blocking collectives, of_both_cores(): return lax.all_gather(array, 'section', axis_index_groups=of_chip)  17 us
    all_to_all x1, starting transfers between devices, local(): lax.all_to_all(sums.reshape(members, 1, TOKENS), AXES, 0, 0, tiled=True,...  7.99 us
    all_to_all x1, starting transfers between devices, local(): lax.all_to_all(packed, 'section', 0, 0, tiled=True, axis_index_groups=ove...  5 us
    all_to_all x1, waiting for transfers between devices, local(): lax.all_to_all(sums.reshape(members, 1, TOKENS), AXES, 0, 0, tiled=True,...  4.67 us
    pallas_call x1, Pallas kernels, local(): pl.pallas_call(teacher_kernel, out_shape=jax.ShapeDtypeStruct((chips, PAC...  2.09 us
    pallas_call x1, Pallas kernels, local(): pl.pallas_call(gradient_kernel, out_shape=(jax.ShapeDtypeStruct(student_q...  1.33 us
    pallas_call x1, Pallas kernels, local(): pl.pallas_call(scores_kernel, out_shape=(squares, squares, pltpu.VMEM((2,...  1.18 us
  transfers between devices with their start and end apart: 2, of which 1 were waited for; matrix products, arithmetic and copies ran while one was open for 0% of the time, Pallas kernels for 7%

profile of v14, /device:TPU:1, one launch (start us, length us, event | category | flops | bytes accessed | tf_op | source)
XLA Modules:
  0.0 43.4 jit_solution(4914534701288556950)
XLA Ops:
  0.6 2.1 %teacher.1 = f32[4,264,128]{2,1,0:T(8,128)} custom-call(s32[8]{0:T(128)} %pairing.3, s32[8]{0:T(128)} %placement.3, bf16[1,128,1024]{2,1,0:T(8,128)(2,1)} %q_ref.1, bf16[1,128,128]{2,1,0:T(8,128)(2,1)} %k_ref.1), custom_call_target="tpu_custom_call" | custom-call | flops 33554432 | bytes 400000 | tf_op jit(solution)/shard_map/teacher/pallas_call | solution.py:337
  2.7 0.0 copy-start.3
  2.7 0.0 copy-start.4
  2.8 5.0 %all-to-all-start = ((f32[4,264,128]{2,1,0:T(8,128)}), f32[4,264,128]{2,1,0:T(8,128)S(1)}, u32[]{:S(2)}, u32[]{:S(2)}) async-start(f32[4,264,128]{2,1,0:T(8,128)} %teacher.1), calls=%async_computation | async-start | bytes 1081344 | tf_op jit(solution)/shard_map/all_to_all | solution.py:349
  7.8 0.0 copy-done.3
  7.8 0.0 copy-done.4
  7.8 7.4 %all-gather = bf16[4,128,640]{2,1,0:T(8,128)(2,1)S(1)} all-gather(bf16[2,128,640]{2,1,0:T(8,128)(2,1)S(1)} %pad_maximum_fusion), channel_id=2, replica_groups={{0,64},{128,192},{256,320},{384,448},{1,65},{129,193},{257,321},{385,44..., dimensions={0}, use_global_device_ids=true | all-gather | bytes 983040 | tf_op jit(solution)/shard_map/all_gather | solution.py:353
  15.2 0.0 copy-start
  15.2 0.0 copy-start.1
  15.2 0.0 copy-start.2
  15.2 0.7 %copy-done = f32[8,4]{0,1:T(4,128)S(1)} copy-done((f32[8,4]{0,1:T(4,128)S(1)}, f32[8,4]{0,1:T(4,128)}, u32[]{:S(2)}) %copy-start) | copy-done | bytes 152
  15.9 0.0 copy-done.1
  15.9 0.0 copy-done.2
  15.9 1.2 %scores.1 = (f32[4,264,128]{2,1,0:T(8,128)S(1)}, f32[4,264,128]{2,1,0:T(8,128)S(1)}, s32[2,8]{1,0:T(2,128)S(1)}) custom-call(s32[8]{0:T(128)S(1)} %copy-done.1, s32[8]{0:T(128)S(1)} %copy-done.2, f32[4,8]{1,0:T(4,128)S(1)} %bitcast.15, bf16[2,2,128,640]{3,2,1,0:T(8,128)(2,1)S(1)} %bitcast.11), custom_call_target="tpu_custom_call" | custom-call | flops 33554432 | bytes 1400000 | tf_op jit(solution)/shard_map/scores/pallas_call | solution.py:358
  17.1 0.0 all-to-all-done.arrived_ref
  17.1 0.7 %student.1 = f32[1,128]{1,0:T(1,128)S(1)} custom-call(s32[2,8]{1,0:T(2,128)S(1)} %get-tuple-element.13.table, f32[4,264,128]{2,1,0:T(8,128)S(1)} %all-to-all-done.arrived_ref, f32[4,264,128]{2,1,0:T(8,128)S(1)} %get-tuple-element.14.raw_ref, f32[4,264,128]{2,1,0:T(8,128)S(1)} %get-tuple-element.15.logp_ref), custom_call_target="tpu_custom_call" | custom-call | flops 33554432 | bytes 1800000 | tf_op jit(solution)/shard_map/student/pallas_call | solution.py:370
  17.8 5.7 %all-gather.4.pair_ref = f32[2,1,128]{2,1,0:T(1,128)S(1)} all-gather(f32[1,1,128]{2,1,0:T(1,128)S(1)} %bitcast.16), channel_id=4, replica_groups={{0,64},{128,192},{256,320},{384,448},{1,65},{129,193},{257,321},{385,44..., dimensions={0}, use_global_device_ids=true | all-gather | bytes 1536 | tf_op jit(solution)/shard_map/all_gather | solution.py:353
  23.6 0.6 %spread.1 = f32[32,128]{1,0:T(8,128)} custom-call(f32[2,1,128]{2,1,0:T(1,128)S(1)} %all-gather.4.pair_ref), custom_call_target="tpu_custom_call" | custom-call | tf_op jit(solution)/shard_map/spread/pallas_call | solution.py:390
  24.2 8.0 %all-to-all-start.1 = ((f32[32,1,128]{2,1,0:T(1,128)}), f32[32,1,128]{2,1,0:T(1,128)S(1)}, u32[]{:S(2)}, u32[]{:S(2)}) async-start(f32[32,1,128]{2,1,0:T(1,128)} %bitcast.7), calls=%async_computation.1 | async-start | bytes 32768 | tf_op jit(solution)/shard_map/all_to_all | solution.py:399
  32.2 0.6 %slope.1 = (bf16[544,128]{1,0:T(8,128)(2,1)S(1)}, bf16[544,128]{1,0:T(8,128)(2,1)S(1)}) custom-call(s32[2,8]{1,0:T(2,128)S(1)} %get-tuple-element.13.table, f32[4,264,128]{2,1,0:T(8,128)S(1)} %all-to-all-done.arrived_ref, f32[4,264,128]{2,1,0:T(8,128)S(1)} %get-tuple-element.14.raw_ref, f32[4,264,128]{2,1,0:T(8,128)S(1)} %get-tuple-element.15.logp_ref), custom_call_target="tpu_custom_call" | custom-call | flops 33554432 | bytes 1800000 | tf_op jit(solution)/shard_map/slope/pallas_call | solution.py:380
  32.8 2.0 %all-gather.1 = bf16[1088,128]{1,0:T(8,128)(2,1)S(1)} all-gather(bf16[544,128]{1,0:T(8,128)(2,1)S(1)} %get-tuple-element.17), channel_id=3, replica_groups={{0,64},{128,192},{256,320},{384,448},{1,65},{129,193},{257,321},{385,44..., dimensions={0}, use_global_device_ids=true | all-gather | bytes 417792 | tf_op jit(solution)/shard_map/all_gather | solution.py:353
  34.8 1.3 %gradient.1 = (bf16[1,2,128,512]{3,2,1,0:T(8,128)(2,1)}, bf16[1,2,128,128]{3,2,1,0:T(8,128)(2,1)}) custom-call(s32[2,8]{1,0:T(2,128)S(1)} %get-tuple-element.13.table, bf16[544,128]{1,0:T(8,128)(2,1)S(1)} %get-tuple-element.16.grad_ref, bf16[2,544,128]{2,1,0:T(8,128)(2,1)S(1)} %bitcast.13, bf16[2,2,128,640]{3,2,1,0:T(8,128)(2,1)S(1)} %bitcast.12), custom_call_target="tpu_custom_call" | custom-call | flops 67108864 | bytes 900000 | tf_op jit(solution)/shard_map/gradient/pallas_call | solution.py:402
  36.1 4.7 %all-to-all-done.1 = f32[32,1,128]{2,1,0:T(1,128)S(1)} async-done(((f32[32,1,128]{2,1,0:T(1,128)}), f32[32,1,128]{2,1,0:T(1,128)S(1)}, u32[]{:S(2)}, u32[]{:S(2)}) %all-to-all-start.1) | async-done | bytes 16416 | tf_op jit(solution)/shard_map/all_to_all | solution.py:399
  40.8 1.8 %all-gather.3 = f32[64,1,128]{2,1,0:T(1,128)S(1)} all-gather(f32[32,1,128]{2,1,0:T(1,128)S(1)} %all-to-all-done.1), channel_id=5, replica_groups={{0,64},{128,192},{256,320},{384,448},{1,65},{129,193},{257,321},{385,44..., dimensions={0}, use_global_device_ids=true | all-gather | bytes 49152 | tf_op jit(solution)/shard_map/all_gather | solution.py:353
  42.6 0.7 %final.1 = (f32[1,8]{1,0:T(1,128)}, f32[4,8]{1,0:T(4,128)}) custom-call(f32[2,32,128]{2,1,0:T(8,128)S(1)} %bitcast.14), custom_call_target="tpu_custom_call" | custom-call | tf_op jit(solution)/shard_map/final/pallas_call | solution.py:416
  (1 shorter events, 0.0 us)
Async XLA Ops:
  2.7 5.0 %copy-start.3 = (bf16[1,2,128,512]{3,2,1,0:T(8,128)(2,1)S(1)}, bf16[1,2,128,512]{3,2,1,0:T(8,128)(2,1)}, u32[]{:S(2)}) copy-start(bf16[1,2,128,512]{3,2,1,0:T(8,128)(2,1)} %param.9) | copy-start | bytes 786436
  2.7 5.0 %copy-start.4 = (bf16[1,2,128,128]{3,2,1,0:T(8,128)(2,1)S(1)}, bf16[1,2,128,128]{3,2,1,0:T(8,128)(2,1)}, u32[]{:S(2)}) copy-start(bf16[1,2,128,128]{3,2,1,0:T(8,128)(2,1)} %param.10) | copy-start | bytes 196612
  2.8 14.4 %all-to-all-start = ((f32[4,264,128]{2,1,0:T(8,128)}), f32[4,264,128]{2,1,0:T(8,128)S(1)}, u32[]{:S(2)}, u32[]{:S(2)}) async-start(f32[4,264,128]{2,1,0:T(8,128)} %teacher.1), calls=%async_computation | async-start | bytes 1081344 | tf_op jit(solution)/shard_map/all_to_all | solution.py:349
  15.2 0.7 %copy-start = (f32[8,4]{0,1:T(4,128)S(1)}, f32[8,4]{0,1:T(4,128)}, u32[]{:S(2)}) copy-start(f32[8,4]{0,1:T(4,128)} %param.11) | copy-start | bytes 388
  15.2 0.7 %copy-start.1 = (s32[8]{0:T(128)S(1)}, s32[8]{0:T(128)}, u32[]{:S(2)}) copy-start(s32[8]{0:T(128)} %pairing.3) | copy-start | bytes 100
  15.2 0.7 %copy-start.2 = (s32[8]{0:T(128)S(1)}, s32[8]{0:T(128)}, u32[]{:S(2)}) copy-start(s32[8]{0:T(128)} %placement.3) | copy-start | bytes 100
  24.2 16.6 %all-to-all-start.1 = ((f32[32,1,128]{2,1,0:T(1,128)}), f32[32,1,128]{2,1,0:T(1,128)S(1)}, u32[]{:S(2)}, u32[]{:S(2)}) async-start(f32[32,1,128]{2,1,0:T(1,128)} %bitcast.7), calls=%async_computation.1 | async-start | bytes 32768 | tf_op jit(solution)/shard_map/all_to_all | solution.py:399
